TPU v7x, 32 devices: a whole 2x2x4 slice. The times are simulated.
32 devices in a mesh: groups: 2 (over y), dp: 4 (over x, core), tensor: 4 (over z).
Axes of the slice: x: 2, y: 2, z: 4, core: 2. Of those that a mesh axis runs over, the one named last changes fastest.
Arguments:
- hidden_first: bfloat16 [32, 16384], P('groups', 'dp'), parts along dimension 0, may hold values from -6 to 6
- hidden_second: bfloat16 [32, 16384], P('groups', 'dp'), parts along dimension 0, may hold values from -6 to 6
- norm_gain: bfloat16 [16384], P('dp'), may hold values from 0.25 to 1.75
- query_weight: bfloat16 [16384, 16384], P('dp', 'tensor'), may hold values from -0.0625 to 0.0625
- w_key: bfloat16 [16384, 1024], P('dp', 'tensor'), may hold values from -0.046875 to 0.046875
- w_value: bfloat16 [16384, 1024], P('dp', 'tensor'), may hold values from -0.046875 to 0.046875
- w_out: bfloat16 [16384, 16384], P('tensor', 'dp'), may hold values from -0.046875 to 0.046875
- a_query: bfloat16 [16384, 128], P(('dp', 'tensor')), may hold values from -0.046875 to 0.046875
- b_query: bfloat16 [128, 16384], P(None, ('tensor', 'dp')), may hold values from -0.1796875 to 0.1796875
- a_key: bfloat16 [16384, 128], P(('dp', 'tensor')), may hold values from -0.046875 to 0.046875
- b_key: bfloat16 [128, 1024], P(None, ('tensor', 'dp')), may hold values from -0.1796875 to 0.1796875
- a_value: bfloat16 [16384, 128], P(('dp', 'tensor')), may hold values from -0.046875 to 0.046875
- b_value: bfloat16 [128, 1024], P(None, ('tensor', 'dp')), may hold values from -0.1796875 to 0.1796875
- a_out: bfloat16 [16384, 128], P(('tensor', 'dp')), may hold values from -0.046875 to 0.046875
- b_out: bfloat16 [128, 16384], P(None, ('dp', 'tensor')), may hold values from -0.1796875 to 0.1796875
- cache_keys: bfloat16 [32, 8, 192, 128], P(('groups', 'dp'), None, 'tensor'), parts along dimension 0, may hold values from -6 to 6
- cache_values: bfloat16 [32, 8, 192, 128], P(('groups', 'dp'), None, 'tensor'), parts along dimension 0, may hold values from -6 to 6
- lengths: int32 [32], P(('groups', 'dp')), parts along dimension 0, may hold values from 1 to 192, as said below
Outputs:
- attn_first: bfloat16 [32, 16384], P('groups', 'dp'), parts along dimension 0
- attn_second: bfloat16 [32, 16384], P('groups', 'dp'), parts along dimension 0
There are 2 independent parts, one for each index of `groups`. A program takes and returns all parts, laid end to end along the dimension named above; an argument that names none is the same for every part. Nothing has to cross between parts.
Inputs may be any that keep to these rules, and one draw needn't show every extreme that they name: `lengths`: cache positions below a row's length hold its earlier tokens; some row of each part uses all 192 positions.
All inputs are finite; a program needn't handle non-finite values.
Results may differ from a plain program's by a relative error of at most 0.0087.
Values may be sent and summed in bfloat16 or wider, within the bound.
No kernel may reach another device: no remote copies, remote signals or barrier semaphores. Data moves between devices by JAX's collectives and lax.ppermute only.
A program may use at most 320 MiB of HBM per device.

v0:
```python
import math

import jax
import jax.numpy as jnp
from jax import lax
from jax.sharding import PartitionSpec as P

D = 16384


ADAPTER_SCALE = 2.0
ROPE_BASE = 500000.0
EPS = 1e-05
MASKED_FILLER = -1e30


def joined_2(part, axis, combine):
    gathered = jax.tree.map(lambda a: lax.all_gather(a, axis), part)

    def take(source):
        return jax.tree.map(lambda a: lax.dynamic_index_in_dim(a, source, 0, False), gathered)

    return lax.fori_loop(
        1, lax.axis_size(axis), lambda source, state: combine(state, take(source)), take(0)
    )


def merge_weight(frozen_weight, factor_in, factor_out):
    adapter_update = jnp.dot(factor_in, factor_out, preferred_element_type=jnp.float32)
    return (frozen_weight.astype(jnp.float32) + ADAPTER_SCALE * adapter_update).astype(jnp.bfloat16)


def rotary(vectors, positions_now):
    half_dim = vectors.shape[-1] // 2
    frequency = ROPE_BASE ** (-jnp.arange(half_dim, dtype=jnp.float32) / half_dim)
    angles = positions_now.astype(jnp.float32)[:, None] * frequency[None, :]
    cosine = jnp.cos(angles)[:, None, :]
    sine_part = jnp.sin(angles)[:, None, :]
    lower = vectors[..., :half_dim]
    upper = vectors[..., half_dim:]
    return jnp.concatenate(
        [lower * cosine - upper * sine_part, upper * cosine + lower * sine_part], axis=-1
    )


def combine_partial(earlier, later):
    highest = jnp.maximum(earlier[0], later[0])
    weight_a = jnp.exp(earlier[0] - highest)
    weight_b = jnp.exp(later[0] - highest)
    return (
        highest,
        earlier[1] * weight_a + later[1] * weight_b,
        earlier[2] * weight_a[..., None] + later[2] * weight_b[..., None],
    )


def on_device(
    hidden_first,
    hidden_second,
    norm_gain,
    query_weight,
    w_key,
    w_value,
    w_out,
    a_query,
    b_query,
    a_key,
    b_key,
    a_value,
    b_value,
    a_out,
    b_out,
    cache_keys,
    cache_values,
    lengths,
):
    tensor_parts = (
        lax.all_gather(a_query, "tensor", axis=0, tiled=True),
        lax.all_gather(a_key, "tensor", axis=0, tiled=True),
        lax.all_gather(a_value, "tensor", axis=0, tiled=True),
        lax.all_gather(b_out, "tensor", axis=1, tiled=True),
    )
    data_parts = (
        lax.all_gather(b_query, "dp", axis=1, tiled=True),
        lax.all_gather(b_key, "dp", axis=1, tiled=True),
        lax.all_gather(b_value, "dp", axis=1, tiled=True),
        lax.all_gather(a_out, "dp", axis=0, tiled=True),
    )
    merged_qkv = jnp.concatenate(
        [
            merge_weight(query_weight, tensor_parts[0], data_parts[0]),
            merge_weight(w_key, tensor_parts[1], data_parts[1]),
            merge_weight(w_value, tensor_parts[2], data_parts[2]),
        ],
        axis=1,
    )
    merged_output = merge_weight(w_out, data_parts[3], tensor_parts[3])
    n_tensor = lax.axis_size("tensor")
    tensor_index = lax.axis_index("tensor")
    rows_dev, key_value_heads, cache_span, head_dim = cache_keys.shape
    query_cols = query_weight.shape[1]
    key_cols = w_key.shape[1]
    joint_cols = query_cols + 2 * key_cols
    heads_here = query_cols // head_dim
    all_heads = heads_here * n_tensor
    group_size = all_heads // key_value_heads
    score_scale = 1.0 / math.sqrt(head_dim)
    cache_positions = tensor_index * cache_span + jnp.arange(cache_span, dtype=jnp.int32)
    cache_valid = cache_positions[None, :] < lengths[:, None]
    first_owner = tensor_index == 0
    fresh_keys = []
    fresh_values = []
    results = []
    for step_index, hidden in enumerate((hidden_first, hidden_second)):
        values_f = hidden.astype(jnp.float32)
        squares = lax.psum(jnp.sum(values_f * values_f, axis=1), "dp")
        normed = (
            values_f * lax.rsqrt(squares / D + EPS)[:, None] * norm_gain.astype(jnp.float32)
        ).astype(jnp.bfloat16)
        projected = lax.psum_scatter(
            jnp.dot(normed, merged_qkv, preferred_element_type=jnp.float32),
            "dp",
            scatter_dimension=0,
            tiled=True,
        ).astype(jnp.bfloat16)
        joined = lax.all_gather(projected, "tensor", axis=1, tiled=True).reshape(
            rows_dev, n_tensor, joint_cols
        )
        queries = joined[:, :, :query_cols].reshape(rows_dev, all_heads, head_dim)
        key_now = joined[:, :, query_cols : query_cols + key_cols].reshape(
            rows_dev, key_value_heads, head_dim
        )
        value_now = joined[:, :, query_cols + key_cols :].reshape(
            rows_dev, key_value_heads, head_dim
        )
        positions_now = lengths + step_index
        queries = rotary(queries.astype(jnp.float32), positions_now).astype(jnp.bfloat16)
        queries = queries.reshape(rows_dev, key_value_heads, group_size, head_dim)
        fresh_keys.append(rotary(key_now.astype(jnp.float32), positions_now).astype(jnp.bfloat16))
        fresh_values.append(value_now)
        cache_scores = (
            jnp.einsum("rkgd,rksd->rkgs", queries, cache_keys, preferred_element_type=jnp.float32)
            * score_scale
        )
        cache_scores = jnp.where(cache_valid[:, None, None, :], cache_scores, MASKED_FILLER)
        new_scores = (
            jnp.einsum(
                "rkgd,rknd->rkgn",
                queries,
                jnp.stack(fresh_keys, axis=2),
                preferred_element_type=jnp.float32,
            )
            * score_scale
        )
        new_scores = jnp.where(first_owner, new_scores, MASKED_FILLER)
        highest = jnp.maximum(jnp.max(cache_scores, axis=-1), jnp.max(new_scores, axis=-1))
        cache_weights = jnp.where(
            cache_valid[:, None, None, :], jnp.exp(cache_scores - highest[..., None]), 0.0
        )
        new_weights = jnp.where(first_owner, jnp.exp(new_scores - highest[..., None]), 0.0)
        totals = jnp.sum(cache_weights, axis=-1) + jnp.sum(new_weights, axis=-1)
        weighted = jnp.einsum(
            "rkgs,rksd->rkgd", cache_weights, cache_values, preferred_element_type=jnp.float32
        )
        weighted = weighted + jnp.einsum(
            "rkgn,rknd->rkgd",
            new_weights,
            jnp.stack(fresh_values, axis=2),
            preferred_element_type=jnp.float32,
        )
        highest = highest.reshape(rows_dev, all_heads)
        totals = totals.reshape(rows_dev, all_heads)
        weighted = weighted.reshape(rows_dev, all_heads, head_dim)
        high_all, total_all, weighted_all = joined_2(
            (highest, totals, weighted), "tensor", combine_partial
        )
        normalized = weighted_all / total_all[..., None]
        own_heads = lax.dynamic_slice_in_dim(normalized, tensor_index * heads_here, heads_here, 1)
        heads = own_heads.reshape(rows_dev, query_cols).astype(jnp.bfloat16)
        out_terms = jnp.dot(
            lax.all_gather(heads, "dp", axis=0, tiled=True),
            merged_output,
            preferred_element_type=jnp.float32,
        )
        attn_out = lax.psum(out_terms, "tensor").astype(jnp.bfloat16)
        results.append(attn_out)
    return (results[0], results[1])


def solution(mesh):
    in_specs = (
        P("groups", "dp"),
        P("groups", "dp"),
        P("dp"),
        P("dp", "tensor"),
        P("dp", "tensor"),
        P("dp", "tensor"),
        P("tensor", "dp"),
        P(("dp", "tensor"), None),
        P(None, ("tensor", "dp")),
        P(("dp", "tensor"), None),
        P(None, ("tensor", "dp")),
        P(("dp", "tensor"), None),
        P(None, ("tensor", "dp")),
        P(("tensor", "dp"), None),
        P(None, ("dp", "tensor")),
        P(("groups", "dp"), None, "tensor", None),
        P(("groups", "dp"), None, "tensor", None),
        P(("groups", "dp")),
    )
    out_specs = (P("groups", "dp"), P("groups", "dp"))
    return jax.shard_map(
        on_device, mesh=mesh, in_specs=in_specs, out_specs=out_specs, check_vma=False
    )
```

profile of v0, /device:TPU:0, one launch (start us, length us, event | category | flops | bytes accessed | tf_op | source)
XLA Modules:
  0.0 401.6 jit_solution(509747269795897121)
XLA Ops:
  7.2 0.7 all-gather.11.cloned.1.call-update
  8.0 0.7 all-gather.13.cloned.1.call-update
  8.7 0.7 all-gather.15.cloned.1.call-update
  9.4 0.5 all-gather.17.cloned.1.call-update
  10.0 0.5 all-gather.21.cloned.1.call-update
  10.6 0.5 all-gather.23.cloned.1.call-update
  11.2 1.1 fusion.15
  12.3 1.1 fusion.18
  13.4 40.6 %copy.47 = bf16[4096,4096]{0,1:T(8,128)(2,1)} copy(bf16[4096,4096]{1,0:T(8,128)(2,1)} %param.25) | data formatting | bytes 67108864 | tf_op args[3]
  54.0 3.0 copy.48
  57.0 9.5 %all_gather.57 = bf16[128,256]{0,1:T(8,128)(2,1)S(1)} all-gather(bf16[128,64]{0,1:T(8,128)(2,1)S(1)} %copy-done.6), channel_id=1, replica_groups=mesh['groups'=2,'dp'=4,'tensor'=4] {'dp'}, dimensions={1}, use_global_device_ids=true | all-gather | bytes 81920 | tf_op jit(solution)/shard_map/all_gather | solution.py:85
  66.5 2.9 copy.49
  69.4 5.2 %all_gather.59 = bf16[128,256]{0,1:T(8,128)(2,1)S(1)} all-gather(bf16[128,64]{0,1:T(8,128)(2,1)S(1)} %copy-done.7), channel_id=1, replica_groups=mesh['groups'=2,'dp'=4,'tensor'=4] {'dp'}, dimensions={1}, use_global_device_ids=true | all-gather | bytes 81920 | tf_op jit(solution)/shard_map/all_gather | solution.py:86
  74.8 43.3 %copy.50 = bf16[4096,4096]{0,1:T(8,128)(2,1)} copy(bf16[4096,4096]{1,0:T(8,128)(2,1)} %param.28) | data formatting | bytes 67108864 | tf_op args[6]
  118.1 6.5 %all-reduce.4 = (f32[16]{0:T(128)S(1)}, f32[16]{0:T(128)S(1)}) all-reduce(f32[16]{0:T(128)S(1)} %fusion.15, f32[16]{0:T(128)S(1)} %fusion.18), channel_id=1, replica_groups=mesh['groups'=2,'dp'=4,'tensor'=4] {'dp'}, use_global_device_ids=true, to_apply=%region_1.0 | all-reduce | flops 32 | bytes 256 | tf_op jit(solution)/shard_map/psum | solution.py:116
  124.6 0.6 dynamic-slice
  126.0 23.7 %add_convert_fusion.1 = bf16[4096,4096]{0,1:T(8,128)(2,1)} fusion(bf16[4096,4096]{0,1:T(8,128)(2,1)} %copy.47, bf16[4096,128]{1,0:T(8,128)(2,1)} %all-gather.11.cloned.1.call-done, bf16[128,4096]{1,0:T(8,128)(2,1)} %all-gather.13.cloned.1.call-done), kind=kOutput, calls=%fused_computation.17 | convolution fusion | flops 4362076160 | bytes 69206016 | tf_op jit(solution)/shard_map/dot_general | solution.py:29
  149.7 4.0 fusion.10
  153.7 1.9 fusion.11
  155.7 26.0 %fusion.6 = f32[16,4608]{1,0:T(8,128)S(1)} fusion(bf16[4096,256]{0,1:T(8,128)(2,1)S(1)} %fusion.11, bf16[4096,256]{0,1:T(8,128)(2,1)} %fusion.10, bf16[4096,4096]{0,1:T(8,128)(2,1)} %add_convert_fusion.1, bf16[16,4096]{1,0:T(8,128)(2,1)S(1)} %copy-done.4, f32[16]{0:T(128)S(1)} %get-tuple-element.433, f32[4096]{0:T(1024)S(1)} %convert_element_type.118), kind=kOutput, calls=%fused_computation.19 | convolution fusion | flops 717488128 | bytes 38191168 | tf_op jit(solution)/shard_map/dot_general | solution.py:121
  181.8 13.5 %fusion.7 = f32[16,4608]{1,0:T(8,128)S(1)} fusion(bf16[4096,256]{0,1:T(8,128)(2,1)S(1)} %fusion.11, bf16[4096,256]{0,1:T(8,128)(2,1)S(1)} %copy-done.2, bf16[4096,4096]{0,1:T(8,128)(2,1)} %add_convert_fusion.1, bf16[16,4096]{1,0:T(8,128)(2,1)S(1)} %copy-done.5, f32[4096]{0:T(1024)S(1)} %convert_element_type.118, f32[16]{0:T(128)S(1)} %get-tuple-element.434), kind=kOutput, calls=%fused_computation.20 | convolution fusion | flops 717488128 | bytes 38191168 | tf_op jit(solution)/shard_map/dot_general | solution.py:121
  195.2 16.3 %all-reduce.7 = (bf16[16,4608]{1,0:T(8,128)(2,1)S(1)}, bf16[16,4608]{1,0:T(8,128)(2,1)S(1)}) all-reduce(f32[16,4608]{1,0:T(8,128)S(1)} %fusion.7, f32[16,4608]{1,0:T(8,128)S(1)} %fusion.6), channel_id=2, replica_groups=mesh['groups'=2,'dp'=4,'tensor'=4] {'dp'}, use_global_device_ids=true, to_apply=%region_2.0.clone | all-reduce | flops 147456 | bytes 884736
  211.6 13.4 %all_gather.67 = bf16[4,18432]{1,0:T(4,128)(2,1)S(1)} all-gather(bf16[4,4608]{1,0:T(4,128)(2,1)S(1)} %dynamic-slice_convert_fusion), channel_id=1, replica_groups=mesh['groups'=2,'dp'=4,'tensor'=4] {'tensor'}, dimensions={1}, use_global_device_ids=true | all-gather | bytes 184320 | tf_op jit(solution)/shard_map/all_gather | solution.py:126
  225.2 13.6 %all_gather.60 = bf16[4,18432]{1,0:T(4,128)(2,1)S(1)} all-gather(bf16[4,4608]{1,0:T(4,128)(2,1)S(1)} %dynamic-slice_convert_fusion.1), channel_id=1, replica_groups=mesh['groups'=2,'dp'=4,'tensor'=4] {'tensor'}, dimensions={1}, use_global_device_ids=true | all-gather | bytes 184320 | tf_op jit(solution)/shard_map/all_gather | solution.py:126
  240.2 0.5 fusion.70
  241.4 0.5 fusion.69
  241.8 1.0 convolution_add_fusion
  243.8 12.0 %all_gather.69 = f32[4,4,128]{2,1,0:T(4,128)S(1)} all-gather(f32[1,4,128]{2,1,0:T(4,128)S(1)} %add.227), channel_id=1, replica_groups=mesh['groups'=2,'dp'=4,'tensor'=4] {'tensor'}, dimensions={0}, use_global_device_ids=true | all-gather | bytes 10240 | tf_op jit(solution)/shard_map/all_gather | solution.py:18
  255.8 11.9 %all_gather.68 = f32[4,4,128]{2,1,0:T(4,128)S(1)} all-gather(f32[1,4,128]{2,1,0:T(4,128)S(1)} %max.55), channel_id=1, replica_groups=mesh['groups'=2,'dp'=4,'tensor'=4] {'tensor'}, dimensions={0}, use_global_device_ids=true | all-gather | bytes 10240 | tf_op jit(solution)/shard_map/all_gather | solution.py:18
  267.7 11.9 %all_gather.62 = f32[4,4,128]{2,1,0:T(4,128)S(1)} all-gather(f32[1,4,128]{2,1,0:T(4,128)S(1)} %add.218), channel_id=1, replica_groups=mesh['groups'=2,'dp'=4,'tensor'=4] {'tensor'}, dimensions={0}, use_global_device_ids=true | all-gather | bytes 10240 | tf_op jit(solution)/shard_map/all_gather | solution.py:18
  279.5 11.9 %all_gather.61 = f32[4,4,128]{2,1,0:T(4,128)S(1)} all-gather(f32[1,4,128]{2,1,0:T(4,128)S(1)} %max.53), channel_id=1, replica_groups=mesh['groups'=2,'dp'=4,'tensor'=4] {'tensor'}, dimensions={0}, use_global_device_ids=true | all-gather | bytes 10240 | tf_op jit(solution)/shard_map/all_gather | solution.py:18
  291.4 1.0 convolution_add_fusion.1
  292.5 23.6 %add_convert_fusion = bf16[4096,4096]{0,1:T(8,128)(2,1)} fusion(bf16[4096,4096]{0,1:T(8,128)(2,1)} %copy.50, bf16[4096,128]{1,0:T(8,128)(2,1)} %all-gather.21.cloned.1.call-done, bf16[128,4096]{1,0:T(8,128)(2,1)} %all-gather.23.cloned.1.call-done), kind=kOutput, calls=%fused_computation.16 | convolution fusion | flops 4362076160 | bytes 69206016 | tf_op jit(solution)/shard_map/dot_general | solution.py:29
  316.1 1.0 slice_bitcast_fusion
  317.1 3.8 while.39
  317.1 1.2 fusion.97
  318.4 1.2 fusion.97
  319.7 1.2 fusion.97
  321.1 5.4 %all-gather.1 = bf16[4,4,4096]{2,1,0:T(4,128)(2,1)S(1)} all-gather(bf16[1,4,4096]{2,1,0:T(4,128)(2,1)S(1)} %reshape.344), channel_id=1, replica_groups=mesh['groups'=2,'dp'=4,'tensor'=4] {'dp'}, dimensions={0}, use_global_device_ids=true | all-gather | bytes 163840 | tf_op jit(solution)/shard_map/all_gather | solution.py:181
  326.5 14.5 %fusion.73 = f32[16,4096]{1,0:T(8,128)S(1)} fusion(bf16[16,4096]{1,0:T(8,128)(2,1)S(1)} %reshape.345, bf16[4096,4096]{0,1:T(8,128)(2,1)} %add_convert_fusion), kind=kOutput, calls=%fused_computation.136 | convolution fusion | flops 536870912 | bytes 33947648 | tf_op jit(solution)/shard_map/dot_general | solution.py:180
  341.0 1.0 slice_bitcast_fusion.1
  342.0 3.8 while.38
  342.1 1.2 fusion.95
  343.3 1.2 fusion.95
  344.6 1.2 fusion.95
  346.0 5.6 %all-gather = bf16[4,4,4096]{2,1,0:T(4,128)(2,1)S(1)} all-gather(bf16[1,4,4096]{2,1,0:T(4,128)(2,1)S(1)} %reshape.342), channel_id=1, replica_groups=mesh['groups'=2,'dp'=4,'tensor'=4] {'dp'}, dimensions={0}, use_global_device_ids=true | all-gather | bytes 163840 | tf_op jit(solution)/shard_map/all_gather | solution.py:181
  351.7 14.5 %fusion.72 = f32[16,4096]{1,0:T(8,128)S(1)} fusion(bf16[16,4096]{1,0:T(8,128)(2,1)S(1)} %reshape.343, bf16[4096,4096]{0,1:T(8,128)(2,1)} %add_convert_fusion), kind=kOutput, calls=%fused_computation.135 | convolution fusion | flops 536870912 | bytes 33947648 | tf_op jit(solution)/shard_map/dot_general | solution.py:180
  366.2 28.5 %all-reduce.8 = (bf16[16,4096]{1,0:T(8,128)(2,1)}, bf16[16,4096]{1,0:T(8,128)(2,1)}) all-reduce(f32[16,4096]{1,0:T(8,128)S(1)} %fusion.72, f32[16,4096]{1,0:T(8,128)S(1)} %fusion.73), channel_id=1, replica_groups=mesh['groups'=2,'dp'=4,'tensor'=4] {'tensor'}, use_global_device_ids=true, to_apply=%region_7.8 | all-reduce | flops 131072 | bytes 786432 | tf_op jit(solution)/shard_map/psum | solution.py:185
  (102 shorter events, 4.3 us)
Async XLA Ops:
  7.2 234.7 %copy-start = (bf16[4,8,48,128]{3,2,1,0:T(8,128)(2,1)S(1)}, bf16[4,8,48,128]{3,2,1,0:T(8,128)(2,1)}, u32[]{:S(2)}) copy-start(bf16[4,8,48,128]{3,2,1,0:T(8,128)(2,1)} %param.38) | copy-start | bytes 1179652
  7.2 118.8 %all-gather.11.cloned.1.call-start = ((), (), s32[]{:S(2)}) async-start(), calls=%async_computation | async-start | bytes 1310720 | tf_op jit(solution)/shard_map/all_gather | solution.py:78
  7.9 118.1 %all-gather.13.cloned.1.call-start = ((), (), s32[]{:S(2)}) async-start(), calls=%async_computation.1 | async-start | bytes 1310720 | tf_op jit(solution)/shard_map/all_gather | solution.py:84
  8.7 141.1 %all-gather.15.cloned.1.call-start = ((), (), s32[]{:S(2)}) async-start(), calls=%async_computation.2 | async-start | bytes 1310720 | tf_op jit(solution)/shard_map/all_gather | solution.py:79
  9.4 144.4 %all-gather.17.cloned.1.call-start = ((), (), s32[]{:S(2)}) async-start(), calls=%async_computation.3 | async-start | bytes 1310720 | tf_op jit(solution)/shard_map/all_gather | solution.py:80
  10.0 282.5 %all-gather.21.cloned.1.call-start = ((), (), s32[]{:S(2)}) async-start(), calls=%async_computation.5 | async-start | bytes 1310720 | tf_op jit(solution)/shard_map/all_gather | solution.py:87
  10.6 281.9 %all-gather.23.cloned.1.call-start = ((), (), s32[]{:S(2)}) async-start(), calls=%async_computation.6 | async-start | bytes 1310720 | tf_op jit(solution)/shard_map/all_gather | solution.py:81
  11.1 305.0 %all-gather.25.cloned.1.call-start = ((), (), s32[]{:S(2)}) async-start(), calls=%async_computation.7 | async-start | bytes 1310720 | tf_op jit(solution)/shard_map/all_gather | solution.py:18
  13.3 40.7 %copy-start.1 = (bf16[4096,256]{1,0:T(8,128)(2,1)S(1)}, bf16[4096,256]{1,0:T(8,128)(2,1)}, u32[]{:S(2)}) copy-start(bf16[4096,256]{1,0:T(8,128)(2,1)} %param.26) | copy-start | bytes 6291460
  13.3 43.7 %copy-start.6 = (bf16[128,64]{0,1:T(8,128)(2,1)S(1)}, bf16[128,64]{0,1:T(8,128)(2,1)}, u32[]{:S(2)}) copy-start(bf16[128,64]{0,1:T(8,128)(2,1)} %param.32) | copy-start | bytes 49156
  13.3 56.1 %copy-start.7 = (bf16[128,64]{0,1:T(8,128)(2,1)S(1)}, bf16[128,64]{0,1:T(8,128)(2,1)}, u32[]{:S(2)}) copy-start(bf16[128,64]{0,1:T(8,128)(2,1)} %param.34) | copy-start | bytes 49156
  13.3 61.3 %copy-start.8 = (bf16[4096]{0:T(1024)(128)(2,1)S(1)}, bf16[4096]{0:T(1024)(128)(2,1)}, u32[]{:S(2)}) copy-start(bf16[4096]{0:T(1024)(128)(2,1)} %param.24) | copy-start | bytes 24580
  13.4 61.3 %copy-start.9 = (s32[4]{0:T(128)S(1)}, s32[4]{0:T(128)}, u32[]{:S(2)}) copy-start(s32[4]{0:T(128)} %param.39) | copy-start | bytes 52
  74.8 49.8 %copy-start.10 = (u32[32]{0:T(128)S(1)}, u32[32]{0:T(128)}, u32[]{:S(2)}) copy-start(u32[32]{0:T(128)} %constant.139) | copy-start | bytes 388
  126.0 29.7 %copy-start.4 = (bf16[16,4096]{1,0:T(8,128)(2,1)S(1)}, bf16[16,4096]{1,0:T(8,128)(2,1)}, u32[]{:S(2)}) copy-start(bf16[16,4096]{1,0:T(8,128)(2,1)} %param.23) | copy-start | bytes 393220
  155.7 26.0 %copy-start.2 = (bf16[4096,256]{0,1:T(8,128)(2,1)S(1)}, bf16[4096,256]{0,1:T(8,128)(2,1)}, u32[]{:S(2)}) copy-start(bf16[4096,256]{0,1:T(8,128)(2,1)} %fusion.10) | copy-start | bytes 6291460
  155.7 26.0 %copy-start.5 = (bf16[16,4096]{1,0:T(8,128)(2,1)S(1)}, bf16[16,4096]{1,0:T(8,128)(2,1)}, u32[]{:S(2)}) copy-start(bf16[16,4096]{1,0:T(8,128)(2,1)} %param.22) | copy-start | bytes 393220
  181.8 58.4 %copy-start.3 = (bf16[4,8,48,128]{3,2,1,0:T(8,128)(2,1)S(1)}, bf16[4,8,48,128]{3,2,1,0:T(8,128)(2,1)}, u32[]{:S(2)}) copy-start(bf16[4,8,48,128]{3,2,1,0:T(8,128)(2,1)} %param.37) | copy-start | bytes 1179652
  242.9 98.2 %all-gather.19.cloned.1.call-start = ((), (), s32[]{:S(2)}) async-start(), calls=%async_computation.4 | async-start | bytes 1310720 | tf_op jit(solution)/shard_map/all_gather | solution.py:18
Sparse Core Ops, SparseCore 0:
  9.6 30.6 all-gather.10
  41.8 16.2 all-gather.12
  59.6 27.9 all-gather.14
  89.0 27.4 all-gather.16
  117.9 16.2 all-gather.20
  135.6 27.9 all-gather.22
  243.0 29.0 all-gather.24
  292.6 26.1 all-gather.18
where the time goes:
time: 404 us; the launch traced here: 402 us
  blocking collectives  152 us (38%)
  matrix products  125 us (31%)
  local copies, waits for them, and re-layouts  93.8 us (23%)
  between operations  15.3 us (4%)
  other arithmetic  11 us (3%)
    unnamed x31, local copies, waits for them, and re-layouts  90.6 us
    dot_general x4, matrix products, merge_weight(): jnp.dot(factor_in, factor_out, preferred_element_type=jnp.float32)  53.3 us
    all_gather x4, blocking collectives, joined_2(): gathered = jax.tree.map(lambda a: lax.all_gather(a, axis), part)  47.6 us
    dot_general x2, matrix products, on_device(): jnp.dot(normed, merged_qkv, preferred_element_type=jnp.float32)  39.5 us
    dot_general x2, matrix products, on_device(): jnp.dot(lax.all_gather(heads, 'dp', axis=0, tiled=True), merged_output, p...  29 us
    psum x1, blocking collectives, on_device(): attn_out = lax.psum(out_terms, 'tensor').astype(jnp.bfloat16)  28.5 us
    all_gather x2, blocking collectives, on_device(): lax.all_gather(projected, 'tensor', axis=1, tiled=True)  27 us
    unnamed x1, blocking collectives  16.3 us
  transfers between devices with their start and end apart: 8, of which 0 were waited for; matrix products, arithmetic and copies ran while one was open for 52% of the time, Pallas kernels for 0%

commit v1 on v0

--- a/solution.py
+++ b/solution.py
@@ -1,8 +1,12 @@
+import functools
 import math
 
 import jax
 import jax.numpy as jnp
+import numpy as np
 from jax import lax
+from jax.experimental import pallas as pl
+from jax.experimental.pallas import tpu as pltpu
 from jax.sharding import PartitionSpec as P
 
 D = 16384
@@ -12,6 +16,8 @@
 ROPE_BASE = 500000.0
 EPS = 1e-05
 MASKED_FILLER = -1e30
+BF16 = jnp.bfloat16
+F32 = jnp.float32
 
 
 def joined_2(part, axis, combine):
@@ -186,6 +192,693 @@
         results.append(attn_out)
     return (results[0], results[1])
 
+def swapped(array, axis, mask):
+    size = lax.axis_size(axis)
+    return lax.ppermute(array, axis, [(k, k ^ mask) for k in range(size)])
+
+
+def vmem_spec():
+    return pl.BlockSpec(memory_space=pltpu.VMEM)
+
+
+def hbm_spec():
+    return pl.BlockSpec(memory_space=pltpu.HBM)
+
+
+def in_hbm(*arrays):
+    return [pltpu.with_memory_space_constraint(array, pltpu.HBM) for array in arrays]
+
+
+def cost(moved):
+    return pl.CostEstimate(flops=0, bytes_accessed=int(moved), transcendentals=0)
+
+
+def kernel_call(body, outs, in_specs, scratch=(), mib=24, out_specs=None, moved=0):
+    return pl.pallas_call(
+        body,
+        out_shape=outs,
+        in_specs=in_specs,
+        out_specs=out_specs or tuple(vmem_spec() for _ in outs),
+        scratch_shapes=list(scratch),
+        cost_estimate=cost(moved),
+        compiler_params=pltpu.CompilerParams(vmem_limit_bytes=mib << 20),
+    )
+
+
+def aligned(start, size, unit):
+    return pl.ds(pl.multiple_of(start, unit), size)
+
+
+def split_sum(total, width):
+    high = total.astype(BF16).astype(F32)
+    rest = total - high
+    middle = rest.astype(BF16).astype(F32)
+    low = rest - middle
+    lane = lax.broadcasted_iota(jnp.int32, (total.shape[0], width), 1)
+    return jnp.where(
+        lane == 0, high, jnp.where(lane == 1, middle, jnp.where(lane == 2, low, 0.0))
+    )
+
+
+def prepare_body(
+    rows_dev,
+    first_ref,
+    second_ref,
+    gain_ref,
+    a_query_ref,
+    a_key_ref,
+    a_value_ref,
+    keys_ref,
+    values_ref,
+    b_query_ref,
+    b_key_ref,
+    b_value_ref,
+    a_out_ref,
+    scaled_ref,
+    squares_ref,
+    low_ref,
+    near,
+    far_1,
+    far_2,
+    far_3,
+    factors_ref,
+    hidden,
+    gain_held,
+    a_held,
+    sems,
+):
+    tensor_index = lax.axis_index("tensor")
+    heads_here = keys_ref.shape[1] // lax.axis_size("tensor")
+    rank = a_query_ref.shape[1]
+    wide = b_query_ref.shape[1]
+    narrow = b_key_ref.shape[0]
+
+    def begun(group, pairs):
+        copies = [pltpu.make_async_copy(*pair, sems.at[group]) for pair in pairs]
+        for copy in copies:
+            copy.start()
+        return copies
+
+    inputs = begun(
+        0, [(first_ref, hidden.at[0]), (second_ref, hidden.at[1]), (gain_ref, gain_held)]
+    )
+    inputs += begun(
+        1,
+        [(ref, a_held.at[place]) for place, ref in enumerate((a_query_ref, a_key_ref, a_value_ref))],
+    )
+    moves = []
+    for mask, far in enumerate((near, far_1, far_2, far_3)):
+        head = jnp.bitwise_xor(tensor_index, mask) * heads_here
+        for kind, cache in enumerate((keys_ref, values_ref)):
+            for row in range(rows_dev):
+                start = (kind * rows_dev + row) * heads_here
+                moves.append((cache.at[row, pl.ds(head, heads_here)], far.at[pl.ds(start, heads_here)]))
+    moves.append((b_query_ref, factors_ref.at[:, pl.ds(0, wide)]))
+    for place, ref in enumerate((b_key_ref, b_value_ref)):
+        moves.append((ref, factors_ref.at[pl.ds(place * narrow, narrow), pl.ds(wide, rank)]))
+    for piece in range(a_out_ref.shape[0] // rank):
+        moves.append(
+            (
+                a_out_ref.at[pl.ds(piece * rank, rank)],
+                factors_ref.at[:, pl.ds(wide + (piece + 1) * rank, rank)],
+            )
+        )
+    moves = begun(2, moves)
+    for copy in inputs[:3]:
+        copy.wait()
+    rows, width = first_ref.shape
+    pieces = []
+    sums = [jnp.zeros((rows, 128), F32), jnp.zeros((rows, 128), F32)]
+
+    def by_owner(pair):
+        ordered = []
+        for owner in range(rows // rows_dev):
+            for part in pair:
+                ordered.append(part[owner * rows_dev : (owner + 1) * rows_dev])
+        return jnp.concatenate(ordered, axis=0)
+
+    for piece in range(width // 128):
+        columns = slice(piece * 128, (piece + 1) * 128)
+        steps = [hidden[step, :, columns].astype(F32) for step in range(2)]
+        sums = [total + step * step for total, step in zip(sums, steps)]
+        gain = gain_held[piece : piece + 1, :].astype(F32)
+        scaled_ref[:, columns] = by_owner([step * gain for step in steps]).astype(BF16)
+    squares_ref[...] = by_owner(sums)
+    for copy in inputs[3:]:
+        copy.wait()
+    depth = a_query_ref.shape[0]
+    own = scaled_ref[:, aligned(tensor_index * depth, depth, 128)]
+    start = 2 * rows_dev * heads_here
+    low_rows = scaled_ref.shape[0]
+    for place in range(3):
+        low = jnp.dot(own, a_held[place], preferred_element_type=F32)
+        low_ref[:, place * rank : (place + 1) * rank] = low
+        for far in (far_1, far_2, far_3):
+            far[start + place, :low_rows, :] = low.astype(BF16)
+    for copy in moves:
+        copy.wait()
+
+
+def project_body(
+    rows_dev,
+    lengths_ref,
+    scaled_ref,
+    query_ref,
+    key_ref,
+    value_ref,
+    sums_ref,
+    trig_ref,
+    length_ref,
+    ring,
+    key_held,
+    value_held,
+    lengths_held,
+    ring_sem,
+    held_sem,
+):
+    slots, depth, columns = ring.shape
+    chunks = query_ref.shape[0] // depth
+
+    def fetch(chunk):
+        slot = chunk % slots
+        return pltpu.make_async_copy(
+            query_ref.at[pl.ds(chunk * depth, depth)], ring.at[slot], ring_sem.at[slot]
+        )
+
+    side = [
+        pltpu.make_async_copy(key_ref, key_held, held_sem.at[0]),
+        pltpu.make_async_copy(value_ref, value_held, held_sem.at[1]),
+    ]
+    for chunk in range(min(slots, chunks)):
+        fetch(chunk).start()
+    for copy in side:
+        copy.start()
+    lengths_copy = pltpu.make_async_copy(lengths_ref, lengths_held, held_sem.at[2])
+    lengths_copy.start()
+    lengths_copy.wait()
+    shape = length_ref.shape
+    half = shape[1] // 2
+    row = lax.broadcasted_iota(jnp.int32, shape, 0)
+    lane = lax.broadcasted_iota(jnp.int32, shape, 1)
+    length = jnp.zeros(shape, jnp.int32)
+    for place in range(rows_dev):
+        length = length + jnp.where(row % rows_dev == place, lengths_held[place], 0)
+    length_ref[...] = length
+    exponent = (lane % half).astype(F32) / half
+    frequency = jnp.exp(exponent * (-math.log(ROPE_BASE)))
+    angles = (length + row // rows_dev).astype(F32) * frequency
+    sine = jnp.sin(angles)
+    trig_ref[: shape[0], :] = jnp.cos(angles)
+    trig_ref[shape[0] :, :] = jnp.where(lane < half, -sine, sine)
+    for chunk in range(chunks):
+        fetch(chunk).wait()
+        term = jnp.dot(
+            scaled_ref[:, chunk * depth : (chunk + 1) * depth],
+            ring[chunk % slots],
+            preferred_element_type=F32,
+        )
+        if chunk == 0:
+            sums_ref[:, :columns] = term
+        else:
+            sums_ref[:, :columns] += term
+        if chunk + slots < chunks:
+            fetch(chunk + slots).start()
+    place = columns
+    for copy, held in zip(side, (key_held, value_held)):
+        copy.wait()
+        sums_ref[:, place : place + held.shape[1]] = jnp.dot(
+            scaled_ref[...], held[...], preferred_element_type=F32
+        )
+        place += held.shape[1]
+
+
+def first_send_body(sums_ref, low_ref, squares_ref, far_1, far_2, far_3, send_ref, keep_ref, full):
+    core = lax.rem(lax.axis_index("dp"), 2)
+    columns = sums_ref.shape[1]
+    rows, low_columns = low_ref.shape
+    rank = low_columns // 3
+    full[:, :columns] = sums_ref[...]
+    for place in range(3):
+        low = low_ref[:, place * rank : (place + 1) * rank]
+        for far in (far_1, far_2, far_3):
+            low = low + far[far.shape[0] - 3 + place, :rows, :].astype(F32)
+        full[:, columns + place * rank : columns + (place + 1) * rank] = low
+    full[:, columns + low_columns :] = split_sum(
+        jnp.sum(squares_ref[...], axis=1, keepdims=True), 128
+    )
+    share = rows // 4
+    other = 1 - core
+    send_ref[...] = jnp.concatenate(
+        [
+            full[aligned(other * share, share, 8), :],
+            full[aligned((other + 2) * share, share, 8), :],
+        ],
+        axis=0,
+    ).astype(BF16)
+    keep_ref[:share, :] = full[aligned(core * share, share, 8), :]
+    keep_ref[share:, :] = full[aligned((core + 2) * share, share, 8), :]
+
+
+def second_send_body(keep_ref, arrived_ref, send_ref, kept_ref, full):
+    chip = lax.axis_index("dp") // 2
+    full[...] = keep_ref[...] + arrived_ref[...].astype(F32)
+    full[:, -128:] = split_sum(jnp.sum(full[:, -128:], axis=1, keepdims=True), 128)
+    share = full.shape[0] // 2
+    send_ref[...] = full[aligned((1 - chip) * share, share, 8), :].astype(BF16)
+    kept_ref[...] = full[aligned(chip * share, share, 8), :]
+
+
+def attend_body(
+    rows_dev,
+    length_ref,
+    trig_ref,
+    kept_ref,
+    arrived_ref,
+    factors_0,
+    factors_1,
+    factors_2,
+    factors_3,
+    near,
+    far_1,
+    far_2,
+    far_3,
+    heads_ref,
+    low_query,
+    low_narrow,
+    turned,
+    mixed,
+    keys_all,
+    values_all,
+):
+    dp_index = lax.axis_index("dp")
+    tensor_index = lax.axis_index("tensor")
+    rows = 2 * rows_dev
+    span, head_dim = near.shape[1:]
+    key_heads = keys_all.shape[0] // rows_dev
+    query_columns = heads_ref.shape[1]
+    heads = query_columns // head_dim
+    group = heads // key_heads
+    sources = lax.axis_size("tensor")
+    rank = factors_0.shape[0]
+    owners = lax.axis_size("dp")
+    wide = query_columns // owners
+    narrow = key_heads * head_dim // owners
+
+    for place in range(rows_dev * key_heads):
+        for mask, block in enumerate((near, far_1, far_2, far_3)):
+            rows_here = slice(mask * span, (mask + 1) * span)
+            keys_all[place, rows_here, :] = block[place]
+            values_all[place, rows_here, :] = block[rows_dev * key_heads + place]
+
+    total = kept_ref[...] + arrived_ref[...].astype(F32)
+    joint = query_columns + 2 * key_heads * head_dim
+    squares = jnp.sum(total[:, -128:], axis=1, keepdims=True)
+    scale = lax.rsqrt(squares / D + EPS)
+    lows = [
+        total[:, joint + place * rank : joint + (place + 1) * rank].astype(BF16)
+        for place in range(3)
+    ]
+    for mask, factors in enumerate((factors_0, factors_1, factors_2, factors_3)):
+        owner = jnp.bitwise_xor(dp_index, mask)
+        low_query[owner] = jnp.dot(lows[0], factors[:, :wide], preferred_element_type=F32)
+        pair = factors[:, wide : wide + 2 * narrow]
+        for place in range(2):
+            low_narrow[place, owner] = lax.dot_general(
+                lows[place + 1], pair, (((1,), (1,)), ((), ())), preferred_element_type=F32
+            )
+    cosine = trig_ref[:rows, :]
+    sine = trig_ref[rows:, :]
+
+    def turn(vector):
+        return vector * cosine + pltpu.roll(vector, head_dim // 2, 1) * sine
+
+    def rounded(vector):
+        return vector.astype(BF16).astype(F32)
+
+    for head in range(heads):
+        column = head * head_dim
+        owner, inner = column // wide, column % wide
+        vector = (
+            total[:, column : column + head_dim]
+            + ADAPTER_SCALE * low_query[owner, :, inner : inner + head_dim]
+        )
+        start = (head % group) * rows
+        turned[head // group, start : start + rows, :] = turn(rounded(vector * scale))
+
+    lane = lax.broadcasted_iota(jnp.int32, (rows, head_dim), 1)
+    per_head = head_dim // narrow
+    fresh = [[], []]
+    for place in range(2):
+        for head in range(key_heads):
+            low = jnp.zeros((rows, head_dim), F32)
+            for part in range(per_head):
+                piece = low_narrow[place, head * per_head + part]
+                shift = (part * narrow - place * narrow) % (2 * narrow)
+                if shift:
+                    piece = pltpu.roll(piece, shift, 1)
+                low = jnp.where(lane // narrow == part, piece, low)
+            column = query_columns + place * key_heads * head_dim + head * head_dim
+            vector = rounded(
+                (total[:, column : column + head_dim] + ADAPTER_SCALE * low) * scale
+            )
+            fresh[place].append(turn(vector) if place == 0 else vector)
+
+    cached = sources * span
+    width = keys_all.shape[1]
+    column = lax.broadcasted_iota(jnp.int32, (1, width), 1)
+    position = jnp.where(column == cached, -1, 1 << 30)
+    for mask in range(sources):
+        base = jnp.bitwise_xor(tensor_index, mask) * span
+        inside = (column >= mask * span) & (column < (mask + 1) * span)
+        position = jnp.where(inside, column - mask * span + base, position)
+    step = lax.broadcasted_iota(jnp.int32, (2 * group, width), 0) % 2
+    second = (step == 1) & (
+        lax.broadcasted_iota(jnp.int32, (2 * group, width), 1) == cached + 1
+    )
+    score_scale = 1.0 / math.sqrt(head_dim)
+    for row in range(rows_dev):
+        valid = (position < length_ref[row : row + 1, :1]) | second
+        for head in range(key_heads):
+            place = row * key_heads + head
+            for joined, parts in ((keys_all, fresh[0]), (values_all, fresh[1])):
+                joined[place, cached:, :] = jnp.concatenate(
+                    [
+                        parts[head][row : row + 1],
+                        parts[head][rows_dev + row : rows_dev + row + 1],
+                        jnp.zeros((width - cached - 2, head_dim), F32),
+                    ],
+                    axis=0,
+                ).astype(BF16)
+            query = turned[head, pl.ds(row, 2 * group, stride=rows_dev), :].astype(BF16)
+            scores = (
+                lax.dot_general(
+                    query,
+                    keys_all[place],
+                    (((1,), (1,)), ((), ())),
+                    preferred_element_type=F32,
+                )
+                * score_scale
+            )
+            scores = jnp.where(valid, scores, MASKED_FILLER)
+            highest = jnp.max(scores, axis=1, keepdims=True)
+            weights = jnp.where(valid, jnp.exp(scores - highest), 0.0)
+            totals = jnp.sum(weights, axis=1, keepdims=True)
+            weighted = jnp.dot(
+                weights.astype(BF16), values_all[place], preferred_element_type=F32
+            )
+            mixed[head, pl.ds(row, 2 * group, stride=rows_dev), :] = weighted / totals
+    for head in range(heads):
+        start = (head % group) * rows
+        heads_ref[:, head * head_dim : (head + 1) * head_dim] = mixed[
+            head // group, start : start + rows, :
+        ].astype(BF16)
+
+
+def output_body(
+    heads_0,
+    heads_1,
+    heads_2,
+    heads_3,
+    factors_0,
+    factors_1,
+    factors_2,
+    factors_3,
+    weight_ref,
+    send_1,
+    send_2,
+    send_3,
+    keep_ref,
+    wide_rows,
+    all_rows,
+    sums,
+    ring,
+    ring_sem,
+):
+    dp_index = lax.axis_index("dp")
+    tensor_index = lax.axis_index("tensor")
+    slots, depth, columns = ring.shape
+    chunks = weight_ref.shape[0] // depth
+
+    def fetch(chunk):
+        slot = chunk % slots
+        return pltpu.make_async_copy(
+            weight_ref.at[pl.ds(chunk * depth, depth)], ring.at[slot], ring_sem.at[slot]
+        )
+
+    for chunk in range(min(slots, chunks)):
+        fetch(chunk).start()
+    share = heads_0.shape[0]
+    for mask, part in enumerate((heads_0, heads_1, heads_2, heads_3)):
+        owner = jnp.bitwise_xor(dp_index, mask)
+        wide_rows[aligned(owner * share, share, 8), :] = part[...].astype(F32)
+    all_rows[...] = wide_rows[...].astype(BF16)
+    rank = factors_0.shape[0]
+    block = all_rows.shape[1] // lax.axis_size("dp")
+    pieces = block // rank
+    base = factors_0.shape[1] - pieces * rank
+    low = jnp.zeros((all_rows.shape[0], rank), F32)
+    for mask, factors in enumerate((factors_0, factors_1, factors_2, factors_3)):
+        owner = jnp.bitwise_xor(dp_index, mask)
+        for piece in range(pieces):
+            low = low + jnp.dot(
+                all_rows[:, aligned(owner * block + piece * rank, rank, 128)],
+                factors[:, base + piece * rank : base + (piece + 1) * rank],
+                preferred_element_type=F32,
+            )
+    for chunk in range(chunks):
+        fetch(chunk).wait()
+        term = jnp.dot(
+            all_rows[:, chunk * depth : (chunk + 1) * depth],
+            ring[chunk % slots],
+            preferred_element_type=F32,
+        )
+        if chunk == 0:
+            sums[...] = term
+        else:
+            sums[...] += term
+        if chunk + slots < chunks:
+            fetch(chunk + slots).start()
+    part = columns // lax.axis_size("tensor")
+    for mask, send in ((1, send_1), (2, send_2), (3, send_3)):
+        target = jnp.bitwise_xor(tensor_index, mask)
+        send[:, :part] = sums[:, aligned(target * part, part, 128)].astype(BF16)
+        send[:, part:] = low.astype(BF16)
+    keep_ref[:, :part] = sums[:, aligned(tensor_index * part, part, 128)]
+    keep_ref[:, part:] = low
+
+
+def finish_body(rows_dev, keep_ref, far_1, far_2, far_3, b_out_ref, part_ref):
+    total = keep_ref[...]
+    for far in (far_1, far_2, far_3):
+        total = total + far[...].astype(F32)
+    part = b_out_ref.shape[1]
+    low = total[:, part:].astype(BF16)
+    result = total[:, :part] + ADAPTER_SCALE * jnp.dot(
+        low, b_out_ref[...], preferred_element_type=F32
+    )
+    pieces = []
+    for step in range(2):
+        for owner in range(result.shape[0] // (2 * rows_dev)):
+            start = (2 * owner + step) * rows_dev
+            pieces.append(result[start : start + rows_dev])
+    part_ref[...] = jnp.concatenate(pieces, axis=0).astype(BF16)
+
+
+def place_body(part_0, part_1, part_2, part_3, first_ref, second_ref, sems):
+    tensor_index = lax.axis_index("tensor")
+    rows = first_ref.shape[0]
+    copies = []
+    for mask, part in enumerate((part_0, part_1, part_2, part_3)):
+        width = part.shape[1]
+        columns = aligned(jnp.bitwise_xor(tensor_index, mask) * width, width, 128)
+        for step, target in enumerate((first_ref, second_ref)):
+            copies.append(
+                pltpu.make_async_copy(
+                    part.at[pl.ds(step * rows, rows)],
+                    target.at[:, columns],
+                    sems.at[mask, step],
+                )
+            )
+    for copy in copies:
+        copy.start()
+    for copy in copies:
+        copy.wait()
+
+
+def on_device_joined(
+    hidden_first,
+    hidden_second,
+    norm_gain,
+    query_weight,
+    w_key,
+    w_value,
+    w_out,
+    a_query,
+    b_query,
+    a_key,
+    b_key,
+    a_value,
+    b_value,
+    a_out,
+    b_out,
+    cache_keys,
+    cache_values,
+    lengths,
+):
+    shape = jax.ShapeDtypeStruct
+    rows, width = hidden_first.shape
+    rows_dev, all_key_heads, span, head_dim = cache_keys.shape
+    n_tensor = lax.axis_size("tensor")
+    key_heads = all_key_heads // n_tensor
+    rank = a_query.shape[1]
+    query_columns = query_weight.shape[1]
+    key_columns = w_key.shape[1]
+    joint = query_columns + 2 * key_columns
+    both = 2 * rows
+    share = 2 * rows_dev
+    low_columns = 3 * rank
+    blocks = 2 * rows_dev * key_heads
+    pack_columns = b_query.shape[1] + rank + a_out.shape[0]
+
+    scaled, squares, low, near, far_1, far_2, far_3, factors = kernel_call(
+        functools.partial(prepare_body, rows_dev),
+        (
+            shape((both, width), BF16),
+            shape((both, 128), F32),
+            shape((both, low_columns), F32),
+            shape((blocks, span, head_dim), BF16),
+            shape((blocks + 3, span, head_dim), BF16),
+            shape((blocks + 3, span, head_dim), BF16),
+            shape((blocks + 3, span, head_dim), BF16),
+            shape((rank, pack_columns), BF16),
+        ),
+        [hbm_spec()] * 12,
+        [
+            pltpu.VMEM((2, rows, width), BF16),
+            pltpu.VMEM((width // 128, 128), BF16),
+            pltpu.VMEM((3,) + a_query.shape, BF16),
+            pltpu.SemaphoreType.DMA((3,)),
+        ],
+        moved=6e6,
+    )(
+        *in_hbm(
+            hidden_first,
+            hidden_second,
+            norm_gain.reshape(width // 128, 128),
+            a_query,
+            a_key,
+            a_value,
+            cache_keys,
+            cache_values,
+            b_query,
+            b_key.T,
+            b_value.T,
+            a_out,
+        )
+    )
+    far = [swapped(part, "tensor", mask) for mask, part in ((1, far_1), (2, far_2), (3, far_3))]
+    factors_x = swapped(factors, "dp", 2)
+    factors_core = swapped(factors, "dp", 1)
+
+    depth = math.gcd(width, 256)
+    sums, trig, length = kernel_call(
+        functools.partial(project_body, rows_dev),
+        (
+            shape((both, joint), F32),
+            shape((2 * share, head_dim), F32),
+            shape((share, head_dim), jnp.int32),
+        ),
+        [hbm_spec(), vmem_spec(), hbm_spec(), hbm_spec(), hbm_spec()],
+        [
+            pltpu.VMEM((4, depth, query_columns), BF16),
+            pltpu.VMEM((width, key_columns), BF16),
+            pltpu.VMEM((width, key_columns), BF16),
+            pltpu.SMEM((rows_dev,), jnp.int32),
+            pltpu.SemaphoreType.DMA((4,)),
+            pltpu.SemaphoreType.DMA((3,)),
+        ],
+        moved=2 * width * joint,
+    )(*in_hbm(lengths), scaled, *in_hbm(query_weight, w_key, w_value))
+    extended = joint + low_columns + 128
+    send, keep = kernel_call(
+        first_send_body,
+        (shape((rows, extended), BF16), shape((rows, extended), F32)),
+        [vmem_spec()] * 6,
+        [pltpu.VMEM((both, extended), F32)],
+    )(sums, low, squares, *far)
+    factors_x, send = lax.optimization_barrier((factors_x, send))
+    arrived = swapped(send, "dp", 1)
+    factors_both = swapped(factors_x, "dp", 1)
+    all_factors = (factors, factors_core, factors_x, factors_both)
+    send, kept = kernel_call(
+        second_send_body,
+        (shape((share, extended), BF16), shape((share, extended), F32)),
+        [vmem_spec()] * 2,
+        [pltpu.VMEM((rows, extended), F32)],
+    )(keep, arrived)
+    arrived = swapped(send, "dp", 2)
+    heads_here = query_columns // head_dim
+    group = heads_here // key_heads
+    positions = n_tensor * span + 16
+    owners = lax.axis_size("dp")
+    (heads,) = kernel_call(
+        functools.partial(attend_body, rows_dev),
+        (shape((share, query_columns), BF16),),
+        [vmem_spec()] * 12,
+        [
+            pltpu.VMEM((owners, share, query_columns // owners), F32),
+            pltpu.VMEM((2, owners, share, 2 * key_columns // owners), F32),
+            pltpu.VMEM((key_heads, group * share, head_dim), F32),
+            pltpu.VMEM((key_heads, group * share, head_dim), F32),
+            pltpu.VMEM((rows_dev * key_heads, positions, head_dim), BF16),
+            pltpu.VMEM((rows_dev * key_heads, positions, head_dim), BF16),
+        ],
+        moved=10e6,
+    )(length, trig, kept, arrived, *all_factors, near, *far)
+
+    heads_x = swapped(heads, "dp", 2)
+    heads_core = swapped(heads, "dp", 1)
+    heads_both = swapped(heads_x, "dp", 1)
+    out_columns = w_out.shape[1]
+    part = out_columns // n_tensor
+    depth = math.gcd(w_out.shape[0], 256)
+    send_1, send_2, send_3, keep = kernel_call(
+        output_body,
+        (
+            shape((both, part + rank), BF16),
+            shape((both, part + rank), BF16),
+            shape((both, part + rank), BF16),
+            shape((both, part + rank), F32),
+        ),
+        [vmem_spec()] * 8 + [hbm_spec()],
+        [
+            pltpu.VMEM((both, w_out.shape[0]), F32),
+            pltpu.VMEM((both, w_out.shape[0]), BF16),
+            pltpu.VMEM((both, out_columns), F32),
+            pltpu.VMEM((4, depth, out_columns), BF16),
+            pltpu.SemaphoreType.DMA((4,)),
+        ],
+        moved=2 * w_out.size,
+    )(heads, heads_core, heads_x, heads_both, *all_factors, *in_hbm(w_out))
+    far = [swapped(block, "tensor", mask) for mask, block in ((1, send_1), (2, send_2), (3, send_3))]
+    (done,) = kernel_call(
+        functools.partial(finish_body, rows_dev),
+        (shape((both, part), BF16),),
+        [vmem_spec()] * 5,
+    )(keep, *far, b_out)
+    parts = [done] + [swapped(done, "tensor", mask) for mask in (1, 2, 3)]
+    return kernel_call(
+        place_body,
+        (shape((rows, out_columns), BF16), shape((rows, out_columns), BF16)),
+        [vmem_spec()] * 4,
+        [pltpu.SemaphoreType.DMA((4, 2))],
+        out_specs=(hbm_spec(), hbm_spec()),
+    )(*parts)
+
+
+def takes_joined(mesh):
+    return mesh.shape["dp"] == 4 and mesh.shape["tensor"] == 4
+
 
 def solution(mesh):
     in_specs = (
@@ -210,5 +903,9 @@
     )
     out_specs = (P("groups", "dp"), P("groups", "dp"))
     return jax.shard_map(
-        on_device, mesh=mesh, in_specs=in_specs, out_specs=out_specs, check_vma=False
-    )
+        on_device_joined if takes_joined(mesh) else on_device,
+        mesh=mesh,
+        in_specs=in_specs,
+        out_specs=out_specs,
+        check_vma=False,
+    )

time: 404 us -> 76.5 us (0.19)
  blocking collectives: 152 us -> 0 us
  matrix products: 125 us -> 0 us
  local copies, waits for them, and re-layouts: 93.8 us -> 0.01 us
  Pallas kernels: 0 us -> 31.5 us
  waiting for transfers between devices: 3.76 us -> 24 us
  starting transfers between devices: 0.31 us -> 20 us
  between operations: 15.3 us -> 0.72 us
  other arithmetic: 11 us -> 0 us
    dot_general x15 -> x0, matrix products: 125 us -> none  [the longest x4 53.3 us: merge_weight(): jnp.dot(factor_in, factor_out, preferred_element_type=jnp.float32)]
    all_gather x10 -> x0, blocking collectives: 100 us -> none  [the longest x4 47.6 us: joined_2(): gathered = jax.tree.map(lambda a: lax.all_gather(a, axis), part)]
    unnamed x31 -> x2, local copies, waits for them, and re-layouts: 90.6 us -> 0.01 us
    psum x2 -> x0, blocking collectives: 35 us -> none  [the longest x1 28.5 us: on_device(): attn_out = lax.psum(out_terms, 'tensor').astype(jnp.bfloat16)]
    pallas_call x0 -> x8, Pallas kernels: none -> 31.5 us  [the longest x1 14 us: on_device_joined(): kernel_call(functools.partial(project_body, rows_dev), (shape((both, join...]
    ppermute x0 -> x17, waiting for transfers between devices: none -> 24 us  [swapped(): return lax.ppermute(array, axis, [(k, k ^ mask) for k in range(size)])]
    ppermute x0 -> x17, starting transfers between devices: none -> 20 us  [swapped(): return lax.ppermute(array, axis, [(k, k ^ mask) for k in range(size)])]
    unnamed x1 -> x0, blocking collectives: 16.3 us -> none
  transfers between devices with their start and end apart: 8 -> 17, of which waited for: 0 -> 9; matrix products, arithmetic and copies ran while one was open for 52% -> 0% of each run, Pallas kernels for 0% -> 19%
where the time goes in v1:
time: 76.5 us; the launch traced here: 76.3 us
  Pallas kernels  31.5 us (41%)
  waiting for transfers between devices  24 us (31%)
  starting transfers between devices  20 us (26%)
    ppermute x17, waiting for transfers between devices, swapped(): return lax.ppermute(array, axis, [(k, k ^ mask) for k in range(size)])  24 us
    ppermute x17, starting transfers between devices, swapped(): return lax.ppermute(array, axis, [(k, k ^ mask) for k in range(size)])  20 us
    pallas_call x1, Pallas kernels, on_device_joined(): kernel_call(functools.partial(project_body, rows_dev), (shape((both, join...  14 us
    pallas_call x1, Pallas kernels, on_device_joined(): kernel_call(output_body, (shape((both, part + rank), BF16), shape((both,...  12 us
    pallas_call x1, Pallas kernels, on_device_joined(): kernel_call(functools.partial(attend_body, rows_dev), (shape((share, quer...  2.78 us
    pallas_call x1, Pallas kernels, on_device_joined(): kernel_call(functools.partial(prepare_body, rows_dev), (shape((both, widt...  1.63 us
  transfers between devices with their start and end apart: 17, of which 9 were waited for; matrix products, arithmetic and copies ran while one was open for 0% of the time, Pallas kernels for 19%

profile of v1, /device:TPU:0, one launch (start us, length us, event | category | flops | bytes accessed | tf_op | source)
XLA Modules:
  0.0 76.3 jit_solution(1336351692303535728)
XLA Ops:
  0.6 1.6 %shard_map.185 = (bf16[32,4096]{1,0:T(8,128)(2,1)S(1)}, f32[32,128]{1,0:T(8,128)S(1)}, f32[32,384]{1,0:T(8,128)S(1)}, bf16[16,48,128]{2,1,0:T(8,128)(2,1)S(1)}, ...) custom-call(bf16[16,4096]{1,0:T(8,128)(2,1)} %first_ref.1, ...), custom_call_target="tpu_custom_call" | custom-call | bytes 6000000 | tf_op jit(solution)/shard_map/pallas_call | solution.py:743
  2.3 3.0 %collective-permute-start.3 = (bf16[128,2176]{1,0:T(8,128)(2,1)S(1)}, bf16[128,2176]{1,0:T(8,128)(2,1)S(1)}, u32[]{:S(2)}, u32[]{:S(2)}) collective-permute-start(bf16[128,2176]{1,0:T(8,128)(2,1)S(1)} %get-tuple-element.33.factors_0), channel_id=1, source_target_pairs={{0,8},{4,12},{8,0},{12,4},{1,9},{5,13},{9,1},{13,5},{2,10},{6,14},... | collective-permute-start | bytes 1671176 | tf_op jit(solution)/shard_map/ppermute | solution.py:197
  5.3 1.6 %collective-permute-start = (bf16[19,48,128]{2,1,0:T(8,128)(2,1)S(1)}, bf16[19,48,128]{2,1,0:T(8,128)(2,1)S(1)}, u32[]{:S(2)}, u32[]{:S(2)}) collective-permute-start(bf16[19,48,128]{2,1,0:T(8,128)(2,1)S(1)} %get-tuple-element.29), channel_id=1, source_target_pairs={{0,1},{1,0},{2,3},{3,2},{4,5},{5,4},{6,7},{7,6},{8,9},{9,8},{10,11... | collective-permute-start | bytes 700424 | tf_op jit(solution)/shard_map/ppermute | solution.py:197
  6.9 2.6 %collective-permute-start.1 = (bf16[19,48,128]{2,1,0:T(8,128)(2,1)S(1)}, bf16[19,48,128]{2,1,0:T(8,128)(2,1)S(1)}, u32[]{:S(2)}, u32[]{:S(2)}) collective-permute-start(bf16[19,48,128]{2,1,0:T(8,128)(2,1)S(1)} %get-tuple-element.30), channel_id=1, source_target_pairs={{0,2},{1,3},{2,0},{3,1},{4,6},{5,7},{6,4},{7,5},{8,10},{9,11},{10,... | collective-permute-start | bytes 700424 | tf_op jit(solution)/shard_map/ppermute | solution.py:197
  9.4 0.2 collective-permute-start.2
  9.7 0.0 collective-permute-start.6
  9.7 0.0 copy-start
  9.7 14.0 %shard_map.186 = (f32[32,4608]{1,0:T(8,128)S(1)}, f32[16,128]{1,0:T(8,128)S(1)}, s32[8,128]{1,0:T(8,128)S(1)}) custom-call(s32[4]{0:T(128)} %lengths_ref.1, bf16[32,4096]{1,0:T(8,128)(2,1)S(1)} %get-tuple-element.23.scaled_ref, bf16[4096,4096]{1,0:T(8,128)(2,1)} %query_ref.1, bf16[4096,256]{1,0:T(8,128)(2,1)} %key_ref.1, bf16[4096,256]{1,0:T(8,128)(2,1)} %value_ref.1), custom_call_target="tpu_custom_call" | custom-call | bytes 37748736 | tf_op jit(solution)/shard_map/pallas_call | solution.py:784
  23.6 0.0 collective-permute-done.far_1
  23.6 2.7 %collective-permute-done.1.far_2 = bf16[19,48,128]{2,1,0:T(8,128)(2,1)S(1)} collective-permute-done((bf16[19,48,128]{2,1,0:T(8,128)(2,1)S(1)}, bf16[19,48,128]{2,1,0:T(8,128)(2,1)S(1)}, u32[]{:S(2)}, u32[]{:S(2)}) %collective-permute-start.1) | collective-permute-done | bytes 233504 | tf_op jit(solution)/shard_map/ppermute | solution.py:197
  26.4 0.0 collective-permute-done.2.far_3
  26.4 0.1 shard_map.187
  26.5 0.0 collective-permute-done.3.factors_2
  26.5 0.1 collective-permute-start.7
  26.6 0.5 collective-permute-start.4
  27.1 1.7 %collective-permute-done.4.arrived_ref = bf16[16,5120]{1,0:T(8,128)(2,1)S(1)} collective-permute-done((bf16[16,5120]{1,0:T(8,128)(2,1)S(1)}, bf16[16,5120]{1,0:T(8,128)(2,1)S(1)}, u32[]{:S(2)}, u32[]{:S(2)}) %collective-permute-start.4) | collective-permute-done | bytes 163872 | tf_op jit(solution)/shard_map/ppermute | solution.py:197
  28.8 0.1 shard_map.188
  28.9 0.6 collective-permute-start.5
  29.5 0.0 collective-permute-done.6.factors_1
  29.5 3.9 %collective-permute-done.5.arrived_ref = bf16[8,5120]{1,0:T(8,128)(2,1)S(1)} collective-permute-done((bf16[8,5120]{1,0:T(8,128)(2,1)S(1)}, bf16[8,5120]{1,0:T(8,128)(2,1)S(1)}, u32[]{:S(2)}, u32[]{:S(2)}) %collective-permute-start.5) | collective-permute-done | bytes 81952 | tf_op jit(solution)/shard_map/ppermute | solution.py:197
  33.4 0.0 collective-permute-done.7.factors_3
  33.4 2.8 %shard_map.189.heads_0 = bf16[8,4096]{1,0:T(8,128)(2,1)S(1)} custom-call(s32[8,128]{1,0:T(8,128)S(1)} %get-tuple-element.24.length_ref, f32[16,128]{1,0:T(8,128)S(1)} %get-tuple-element.25.trig_ref, f32[8,5120]{1,0:T(8,128)S(1)} %get-tuple-element.36.kept_ref, bf16[8,5120]{1,0:T(8,128)(2,1)S(1)} %collective-permute-done.5.arrived_ref, ...), custom_call_target="tpu_custom_call" | custom-call | bytes 10000000 | tf_op jit(solution)/shard_map/pallas_call | solution.py:824
  36.2 0.6 collective-permute-start.9
  36.8 0.0 collective-permute-start.8
  36.8 3.7 %collective-permute-done.9.heads_2 = bf16[8,4096]{1,0:T(8,128)(2,1)S(1)} collective-permute-done((bf16[8,4096]{1,0:T(8,128)(2,1)S(1)}, bf16[8,4096]{1,0:T(8,128)(2,1)S(1)}, u32[]{:S(2)}, u32[]{:S(2)}) %collective-permute-start.9) | collective-permute-done | bytes 65568 | tf_op jit(solution)/shard_map/ppermute | solution.py:197
  40.5 0.0 collective-permute-start.10
  40.6 0.0 collective-permute-done.8.heads_1
  40.6 1.2 %collective-permute-done.10.heads_3 = bf16[8,4096]{1,0:T(8,128)(2,1)S(1)} collective-permute-done((bf16[8,4096]{1,0:T(8,128)(2,1)S(1)}, bf16[8,4096]{1,0:T(8,128)(2,1)S(1)}, u32[]{:S(2)}, u32[]{:S(2)}) %collective-permute-start.10) | collective-permute-done | bytes 65568 | tf_op jit(solution)/shard_map/ppermute | solution.py:197
  41.8 12.0 %shard_map.190 = (bf16[32,1152]{1,0:T(8,128)(2,1)S(1)}, bf16[32,1152]{1,0:T(8,128)(2,1)S(1)}, bf16[32,1152]{1,0:T(8,128)(2,1)S(1)}, f32[32,1152]{1,0:T(8,128)S(1)}) custom-call(bf16[8,4096]{1,0:T(8,128)(2,1)S(1)} %shard_map.189.heads_0, bf16[8,4096]{1,0:T(8,128)(2,1)S(1)} %collective-permute-done.8.heads_1, ...), custom_call_target="tpu_custom_call" | custom-call | bytes 33554432 | tf_op jit(solution)/shard_map/pallas_call | solution.py:845
  53.9 3.9 %collective-permute-start.11 = (bf16[32,1152]{1,0:T(8,128)(2,1)S(1)}, bf16[32,1152]{1,0:T(8,128)(2,1)S(1)}, u32[]{:S(2)}, u32[]{:S(2)}) collective-permute-start(bf16[32,1152]{1,0:T(8,128)(2,1)S(1)} %get-tuple-element.41), channel_id=1, source_target_pairs={{0,1},{1,0},{2,3},{3,2},{4,5},{5,4},{6,7},{7,6},{8,9},{9,8},{10,11... | collective-permute-start | bytes 221192 | tf_op jit(solution)/shard_map/ppermute | solution.py:197
  57.8 1.1 %collective-permute-start.12 = (bf16[32,1152]{1,0:T(8,128)(2,1)S(1)}, bf16[32,1152]{1,0:T(8,128)(2,1)S(1)}, u32[]{:S(2)}, u32[]{:S(2)}) collective-permute-start(bf16[32,1152]{1,0:T(8,128)(2,1)S(1)} %get-tuple-element.42), channel_id=1, source_target_pairs={{0,2},{1,3},{2,0},{3,1},{4,6},{5,7},{6,4},{7,5},{8,10},{9,11},{10,... | collective-permute-start | bytes 221192 | tf_op jit(solution)/shard_map/ppermute | solution.py:197
  58.9 1.4 %collective-permute-start.13 = (bf16[32,1152]{1,0:T(8,128)(2,1)S(1)}, bf16[32,1152]{1,0:T(8,128)(2,1)S(1)}, u32[]{:S(2)}, u32[]{:S(2)}) collective-permute-start(bf16[32,1152]{1,0:T(8,128)(2,1)S(1)} %get-tuple-element.43), channel_id=1, source_target_pairs={{0,3},{1,2},{2,1},{3,0},{4,7},{5,6},{6,5},{7,4},{8,11},{9,10},{10,... | collective-permute-start | bytes 221192 | tf_op jit(solution)/shard_map/ppermute | solution.py:197
  60.2 0.1 collective-permute-done.11.far_1
  60.4 6.3 %collective-permute-done.12.far_2 = bf16[32,1152]{1,0:T(8,128)(2,1)S(1)} collective-permute-done((bf16[32,1152]{1,0:T(8,128)(2,1)S(1)}, bf16[32,1152]{1,0:T(8,128)(2,1)S(1)}, u32[]{:S(2)}, u32[]{:S(2)}) %collective-permute-start.12) | collective-permute-done | bytes 73760 | tf_op jit(solution)/shard_map/ppermute | solution.py:197
  66.6 0.0 collective-permute-done.13.far_3
  66.6 0.0 copy-done
  66.6 0.2 shard_map.191.part_0
  66.8 2.2 %collective-permute-start.16 = (bf16[32,1024]{1,0:T(8,128)(2,1)S(1)}, bf16[32,1024]{1,0:T(8,128)(2,1)S(1)}, u32[]{:S(2)}, u32[]{:S(2)}) collective-permute-start(bf16[32,1024]{1,0:T(8,128)(2,1)S(1)} %shard_map.191.part_0), channel_id=1, source_target_pairs={{0,3},{1,2},{2,1},{3,0},{4,7},{5,6},{6,5},{7,4},{8,11},{9,10},{10,... | collective-permute-start | bytes 196616 | tf_op jit(solution)/shard_map/ppermute | solution.py:197
  69.0 0.8 %collective-permute-start.15 = (bf16[32,1024]{1,0:T(8,128)(2,1)S(1)}, bf16[32,1024]{1,0:T(8,128)(2,1)S(1)}, u32[]{:S(2)}, u32[]{:S(2)}) collective-permute-start(bf16[32,1024]{1,0:T(8,128)(2,1)S(1)} %shard_map.191.part_0), channel_id=1, source_target_pairs={{0,2},{1,3},{2,0},{3,1},{4,6},{5,7},{6,4},{7,5},{8,10},{9,11},{10,... | collective-permute-start | bytes 196616 | tf_op jit(solution)/shard_map/ppermute | solution.py:197
  69.8 1.5 %collective-permute-start.14 = (bf16[32,1024]{1,0:T(8,128)(2,1)S(1)}, bf16[32,1024]{1,0:T(8,128)(2,1)S(1)}, u32[]{:S(2)}, u32[]{:S(2)}) collective-permute-start(bf16[32,1024]{1,0:T(8,128)(2,1)S(1)} %shard_map.191.part_0), channel_id=1, source_target_pairs={{0,1},{1,0},{2,3},{3,2},{4,5},{5,4},{6,7},{7,6},{8,9},{9,8},{10,11... | collective-permute-start | bytes 196616 | tf_op jit(solution)/shard_map/ppermute | solution.py:197
  71.3 2.4 %collective-permute-done.16.part_3 = bf16[32,1024]{1,0:T(8,128)(2,1)S(1)} collective-permute-done((bf16[32,1024]{1,0:T(8,128)(2,1)S(1)}, bf16[32,1024]{1,0:T(8,128)(2,1)S(1)}, u32[]{:S(2)}, u32[]{:S(2)}) %collective-permute-start.16) | collective-permute-done | bytes 65568 | tf_op jit(solution)/shard_map/ppermute | solution.py:197
  73.7 1.8 %collective-permute-done.15.part_2 = bf16[32,1024]{1,0:T(8,128)(2,1)S(1)} collective-permute-done((bf16[32,1024]{1,0:T(8,128)(2,1)S(1)}, bf16[32,1024]{1,0:T(8,128)(2,1)S(1)}, u32[]{:S(2)}, u32[]{:S(2)}) %collective-permute-start.15) | collective-permute-done | bytes 65568 | tf_op jit(solution)/shard_map/ppermute | solution.py:197
  75.5 0.0 collective-permute-done.14.part_1
  75.5 0.8 shard_map.192
Async XLA Ops:
  2.3 24.2 %collective-permute-start.3 = (bf16[128,2176]{1,0:T(8,128)(2,1)S(1)}, bf16[128,2176]{1,0:T(8,128)(2,1)S(1)}, u32[]{:S(2)}, u32[]{:S(2)}) collective-permute-start(bf16[128,2176]{1,0:T(8,128)(2,1)S(1)} %get-tuple-element.33.factors_0), channel_id=1, source_target_pairs={{0,8},{4,12},{8,0},{12,4},{1,9},{5,13},{9,1},{13,5},{2,10},{6,14},... | collective-permute-start | bytes 1671176 | tf_op jit(solution)/shard_map/ppermute | solution.py:197
  5.3 18.4 %collective-permute-start = (bf16[19,48,128]{2,1,0:T(8,128)(2,1)S(1)}, bf16[19,48,128]{2,1,0:T(8,128)(2,1)S(1)}, u32[]{:S(2)}, u32[]{:S(2)}) collective-permute-start(bf16[19,48,128]{2,1,0:T(8,128)(2,1)S(1)} %get-tuple-element.29), channel_id=1, source_target_pairs={{0,1},{1,0},{2,3},{3,2},{4,5},{5,4},{6,7},{7,6},{8,9},{9,8},{10,11... | collective-permute-start | bytes 700424 | tf_op jit(solution)/shard_map/ppermute | solution.py:197
  6.9 19.5 %collective-permute-start.1 = (bf16[19,48,128]{2,1,0:T(8,128)(2,1)S(1)}, bf16[19,48,128]{2,1,0:T(8,128)(2,1)S(1)}, u32[]{:S(2)}, u32[]{:S(2)}) collective-permute-start(bf16[19,48,128]{2,1,0:T(8,128)(2,1)S(1)} %get-tuple-element.30), channel_id=1, source_target_pairs={{0,2},{1,3},{2,0},{3,1},{4,6},{5,7},{6,4},{7,5},{8,10},{9,11},{10,... | collective-permute-start | bytes 700424 | tf_op jit(solution)/shard_map/ppermute | solution.py:197
  9.4 16.9 %collective-permute-start.2 = (bf16[19,48,128]{2,1,0:T(8,128)(2,1)S(1)}, bf16[19,48,128]{2,1,0:T(8,128)(2,1)S(1)}, u32[]{:S(2)}, u32[]{:S(2)}) collective-permute-start(bf16[19,48,128]{2,1,0:T(8,128)(2,1)S(1)} %get-tuple-element.31), channel_id=1, source_target_pairs={{0,3},{1,2},{2,1},{3,0},{4,7},{5,6},{6,5},{7,4},{8,11},{9,10},{10,... | collective-permute-start | bytes 700424 | tf_op jit(solution)/shard_map/ppermute | solution.py:197
  9.7 19.8 %collective-permute-start.6 = (bf16[128,2176]{1,0:T(8,128)(2,1)S(1)}, bf16[128,2176]{1,0:T(8,128)(2,1)S(1)}, u32[]{:S(2)}, u32[]{:S(2)}) collective-permute-start(bf16[128,2176]{1,0:T(8,128)(2,1)S(1)} %get-tuple-element.33.factors_0), channel_id=1, source_target_pairs={{0,4},{4,0},{8,12},{12,8},{1,5},{5,1},{9,13},{13,9},{2,6},{6,2},{1... | collective-permute-start | bytes 1671176 | tf_op jit(solution)/shard_map/ppermute | solution.py:197
  9.7 57.0 %copy-start = (bf16[128,1024]{1,0:T(8,128)(2,1)S(1)}, bf16[128,1024]{1,0:T(8,128)(2,1)}, u32[]{:S(2)}) copy-start(bf16[128,1024]{1,0:T(8,128)(2,1)} %b_out_ref.1) | copy-start | bytes 786436
  26.5 6.9 %collective-permute-start.7 = (bf16[128,2176]{1,0:T(8,128)(2,1)S(1)}, bf16[128,2176]{1,0:T(8,128)(2,1)S(1)}, u32[]{:S(2)}, u32[]{:S(2)}) collective-permute-start(bf16[128,2176]{1,0:T(8,128)(2,1)S(1)} %collective-permute-done.3.factors_2), channel_id=1, source_target_pairs={{0,4},{4,0},{8,12},{12,8},{1,5},{5,1},{9,13},{13,9},{2,6},{6,2},{1... | collective-permute-start | bytes 1671176 | tf_op jit(solution)/shard_map/ppermute | solution.py:197
  26.6 2.2 %collective-permute-start.4 = (bf16[16,5120]{1,0:T(8,128)(2,1)S(1)}, bf16[16,5120]{1,0:T(8,128)(2,1)S(1)}, u32[]{:S(2)}, u32[]{:S(2)}) collective-permute-start(bf16[16,5120]{1,0:T(8,128)(2,1)S(1)} %get-tuple-element.35), channel_id=1, source_target_pairs={{0,4},{4,0},{8,12},{12,8},{1,5},{5,1},{9,13},{13,9},{2,6},{6,2},{1... | collective-permute-start | bytes 491528 | tf_op jit(solution)/shard_map/ppermute | solution.py:197
  28.9 4.6 %collective-permute-start.5 = (bf16[8,5120]{1,0:T(8,128)(2,1)S(1)}, bf16[8,5120]{1,0:T(8,128)(2,1)S(1)}, u32[]{:S(2)}, u32[]{:S(2)}) collective-permute-start(bf16[8,5120]{1,0:T(8,128)(2,1)S(1)} %get-tuple-element.37), channel_id=1, source_target_pairs={{0,8},{4,12},{8,0},{12,4},{1,9},{5,13},{9,1},{13,5},{2,10},{6,14},... | collective-permute-start | bytes 245768 | tf_op jit(solution)/shard_map/ppermute | solution.py:197
  36.2 4.3 %collective-permute-start.9 = (bf16[8,4096]{1,0:T(8,128)(2,1)S(1)}, bf16[8,4096]{1,0:T(8,128)(2,1)S(1)}, u32[]{:S(2)}, u32[]{:S(2)}) collective-permute-start(bf16[8,4096]{1,0:T(8,128)(2,1)S(1)} %shard_map.189.heads_0), channel_id=1, source_target_pairs={{0,8},{4,12},{8,0},{12,4},{1,9},{5,13},{9,1},{13,5},{2,10},{6,14},... | collective-permute-start | bytes 196616 | tf_op jit(solution)/shard_map/ppermute | solution.py:197
  36.8 3.7 %collective-permute-start.8 = (bf16[8,4096]{1,0:T(8,128)(2,1)S(1)}, bf16[8,4096]{1,0:T(8,128)(2,1)S(1)}, u32[]{:S(2)}, u32[]{:S(2)}) collective-permute-start(bf16[8,4096]{1,0:T(8,128)(2,1)S(1)} %shard_map.189.heads_0), channel_id=1, source_target_pairs={{0,4},{4,0},{8,12},{12,8},{1,5},{5,1},{9,13},{13,9},{2,6},{6,2},{1... | collective-permute-start | bytes 196616 | tf_op jit(solution)/shard_map/ppermute | solution.py:197
  40.5 1.3 %collective-permute-start.10 = (bf16[8,4096]{1,0:T(8,128)(2,1)S(1)}, bf16[8,4096]{1,0:T(8,128)(2,1)S(1)}, u32[]{:S(2)}, u32[]{:S(2)}) collective-permute-start(bf16[8,4096]{1,0:T(8,128)(2,1)S(1)} %collective-permute-done.9.heads_2), channel_id=1, source_target_pairs={{0,4},{4,0},{8,12},{12,8},{1,5},{5,1},{9,13},{13,9},{2,6},{6,2},{1... | collective-permute-start | bytes 196616 | tf_op jit(solution)/shard_map/ppermute | solution.py:197
  53.9 6.5 %collective-permute-start.11 = (bf16[32,1152]{1,0:T(8,128)(2,1)S(1)}, bf16[32,1152]{1,0:T(8,128)(2,1)S(1)}, u32[]{:S(2)}, u32[]{:S(2)}) collective-permute-start(bf16[32,1152]{1,0:T(8,128)(2,1)S(1)} %get-tuple-element.41), channel_id=1, source_target_pairs={{0,1},{1,0},{2,3},{3,2},{4,5},{5,4},{6,7},{7,6},{8,9},{9,8},{10,11... | collective-permute-start | bytes 221192 | tf_op jit(solution)/shard_map/ppermute | solution.py:197
  57.8 8.9 %collective-permute-start.12 = (bf16[32,1152]{1,0:T(8,128)(2,1)S(1)}, bf16[32,1152]{1,0:T(8,128)(2,1)S(1)}, u32[]{:S(2)}, u32[]{:S(2)}) collective-permute-start(bf16[32,1152]{1,0:T(8,128)(2,1)S(1)} %get-tuple-element.42), channel_id=1, source_target_pairs={{0,2},{1,3},{2,0},{3,1},{4,6},{5,7},{6,4},{7,5},{8,10},{9,11},{10,... | collective-permute-start | bytes 221192 | tf_op jit(solution)/shard_map/ppermute | solution.py:197
  58.9 7.8 %collective-permute-start.13 = (bf16[32,1152]{1,0:T(8,128)(2,1)S(1)}, bf16[32,1152]{1,0:T(8,128)(2,1)S(1)}, u32[]{:S(2)}, u32[]{:S(2)}) collective-permute-start(bf16[32,1152]{1,0:T(8,128)(2,1)S(1)} %get-tuple-element.43), channel_id=1, source_target_pairs={{0,3},{1,2},{2,1},{3,0},{4,7},{5,6},{6,5},{7,4},{8,11},{9,10},{10,... | collective-permute-start | bytes 221192 | tf_op jit(solution)/shard_map/ppermute | solution.py:197
  66.8 6.9 %collective-permute-start.16 = (bf16[32,1024]{1,0:T(8,128)(2,1)S(1)}, bf16[32,1024]{1,0:T(8,128)(2,1)S(1)}, u32[]{:S(2)}, u32[]{:S(2)}) collective-permute-start(bf16[32,1024]{1,0:T(8,128)(2,1)S(1)} %shard_map.191.part_0), channel_id=1, source_target_pairs={{0,3},{1,2},{2,1},{3,0},{4,7},{5,6},{6,5},{7,4},{8,11},{9,10},{10,... | collective-permute-start | bytes 196616 | tf_op jit(solution)/shard_map/ppermute | solution.py:197
  69.0 6.5 %collective-permute-start.15 = (bf16[32,1024]{1,0:T(8,128)(2,1)S(1)}, bf16[32,1024]{1,0:T(8,128)(2,1)S(1)}, u32[]{:S(2)}, u32[]{:S(2)}) collective-permute-start(bf16[32,1024]{1,0:T(8,128)(2,1)S(1)} %shard_map.191.part_0), channel_id=1, source_target_pairs={{0,2},{1,3},{2,0},{3,1},{4,6},{5,7},{6,4},{7,5},{8,10},{9,11},{10,... | collective-permute-start | bytes 196616 | tf_op jit(solution)/shard_map/ppermute | solution.py:197
  69.8 5.7 %collective-permute-start.14 = (bf16[32,1024]{1,0:T(8,128)(2,1)S(1)}, bf16[32,1024]{1,0:T(8,128)(2,1)S(1)}, u32[]{:S(2)}, u32[]{:S(2)}) collective-permute-start(bf16[32,1024]{1,0:T(8,128)(2,1)S(1)} %shard_map.191.part_0), channel_id=1, source_target_pairs={{0,1},{1,0},{2,3},{3,2},{4,5},{5,4},{6,7},{7,6},{8,9},{9,8},{10,11... | collective-permute-start | bytes 196616 | tf_op jit(solution)/shard_map/ppermute | solution.py:197

commit v2 on v1

--- a/solution.py
+++ b/solution.py
@@ -201,6 +201,10 @@
     return pl.BlockSpec(memory_space=pltpu.VMEM)
 
 
+def any_spec():
+    return pl.BlockSpec(memory_space=pl.ANY)
+
+
 def hbm_spec():
     return pl.BlockSpec(memory_space=pltpu.HBM)
 
@@ -213,7 +217,7 @@
     return pl.CostEstimate(flops=0, bytes_accessed=int(moved), transcendentals=0)
 
 
-def kernel_call(body, outs, in_specs, scratch=(), mib=24, out_specs=None, moved=0):
+def kernel_call(body, outs, in_specs, scratch=(), mib=12, out_specs=None, moved=0):
     return pl.pallas_call(
         body,
         out_shape=outs,
@@ -238,6 +242,14 @@
     return jnp.where(
         lane == 0, high, jnp.where(lane == 1, middle, jnp.where(lane == 2, low, 0.0))
     )
+
+
+def low_places(shape, rows, place):
+    blocks, span, _ = shape
+    first = blocks - -(-3 * rows // span)
+    for part in range(0, rows, 16):
+        flat = place * rows + part
+        yield first + flat // span, flat % span, part
 
 
 def prepare_body(
@@ -261,6 +273,7 @@
     far_1,
     far_2,
     far_3,
+    far_values,
     factors_ref,
     hidden,
     gain_held,
@@ -290,9 +303,13 @@
     for mask, far in enumerate((near, far_1, far_2, far_3)):
         head = jnp.bitwise_xor(tensor_index, mask) * heads_here
         for kind, cache in enumerate((keys_ref, values_ref)):
+            late = mask == 3 and kind == 1
             for row in range(rows_dev):
-                start = (kind * rows_dev + row) * heads_here
-                moves.append((cache.at[row, pl.ds(head, heads_here)], far.at[pl.ds(start, heads_here)]))
+                start = (row if late else kind * rows_dev + row) * heads_here
+                target = far_values if late else far
+                moves.append(
+                    (cache.at[row, pl.ds(head, heads_here)], target.at[pl.ds(start, heads_here)])
+                )
     moves.append((b_query_ref, factors_ref.at[:, pl.ds(0, wide)]))
     for place, ref in enumerate((b_key_ref, b_value_ref)):
         moves.append((ref, factors_ref.at[pl.ds(place * narrow, narrow), pl.ds(wide, rank)]))
@@ -304,37 +321,40 @@
             )
         )
     moves = begun(2, moves)
-    for copy in inputs[:3]:
-        copy.wait()
-    rows, width = first_ref.shape
-    pieces = []
-    sums = [jnp.zeros((rows, 128), F32), jnp.zeros((rows, 128), F32)]
-
-    def by_owner(pair):
-        ordered = []
-        for owner in range(rows // rows_dev):
-            for part in pair:
-                ordered.append(part[owner * rows_dev : (owner + 1) * rows_dev])
-        return jnp.concatenate(ordered, axis=0)
-
-    for piece in range(width // 128):
-        columns = slice(piece * 128, (piece + 1) * 128)
-        steps = [hidden[step, :, columns].astype(F32) for step in range(2)]
-        sums = [total + step * step for total, step in zip(sums, steps)]
-        gain = gain_held[piece : piece + 1, :].astype(F32)
-        scaled_ref[:, columns] = by_owner([step * gain for step in steps]).astype(BF16)
-    squares_ref[...] = by_owner(sums)
-    for copy in inputs[3:]:
-        copy.wait()
-    depth = a_query_ref.shape[0]
-    own = scaled_ref[:, aligned(tensor_index * depth, depth, 128)]
-    start = 2 * rows_dev * heads_here
-    low_rows = scaled_ref.shape[0]
-    for place in range(3):
-        low = jnp.dot(own, a_held[place], preferred_element_type=F32)
-        low_ref[:, place * rank : (place + 1) * rank] = low
-        for far in (far_1, far_2, far_3):
-            far[start + place, :low_rows, :] = low.astype(BF16)
+    @pl.when(tensor_index >= 0)
+    def scaled():
+        for copy in inputs[:3]:
+            copy.wait()
+        rows, width = first_ref.shape
+        pieces = []
+        sums = [jnp.zeros((rows, 128), F32), jnp.zeros((rows, 128), F32)]
+
+        def by_owner(pair):
+            ordered = []
+            for owner in range(rows // rows_dev):
+                for part in pair:
+                    ordered.append(part[owner * rows_dev : (owner + 1) * rows_dev])
+            return jnp.concatenate(ordered, axis=0)
+
+        for piece in range(width // 128):
+            columns = slice(piece * 128, (piece + 1) * 128)
+            steps = [hidden[step, :, columns].astype(F32) for step in range(2)]
+            sums = [total + step * step for total, step in zip(sums, steps)]
+            gain = gain_held[piece : piece + 1, :].astype(F32)
+            scaled_ref[:, columns] = by_owner([step * gain for step in steps]).astype(BF16)
+        squares_ref[...] = by_owner(sums)
+        for copy in inputs[3:]:
+            copy.wait()
+        depth = a_query_ref.shape[0]
+        own = scaled_ref[:, aligned(tensor_index * depth, depth, 128)]
+        low_rows = scaled_ref.shape[0]
+        for place in range(3):
+            low = jnp.dot(own, a_held[place], preferred_element_type=F32)
+            low_ref[:, place * rank : (place + 1) * rank] = low
+            for far in (far_1, far_2, far_3):
+                for at, row, part in low_places(far.shape, low_rows, place):
+                    far[at, row : row + 16, :] = low[part : part + 16].astype(BF16)
+
     for copy in moves:
         copy.wait()
 
@@ -369,10 +389,10 @@
         pltpu.make_async_copy(key_ref, key_held, held_sem.at[0]),
         pltpu.make_async_copy(value_ref, value_held, held_sem.at[1]),
     ]
+    for copy in side:
+        copy.start()
     for chunk in range(min(slots, chunks)):
         fetch(chunk).start()
-    for copy in side:
-        copy.start()
     lengths_copy = pltpu.make_async_copy(lengths_ref, lengths_held, held_sem.at[2])
     lengths_copy.start()
     lengths_copy.wait()
@@ -390,6 +410,13 @@
     sine = jnp.sin(angles)
     trig_ref[: shape[0], :] = jnp.cos(angles)
     trig_ref[shape[0] :, :] = jnp.where(lane < half, -sine, sine)
+    place = columns
+    for copy, held in zip(side, (key_held, value_held)):
+        copy.wait()
+        sums_ref[:, place : place + held.shape[1]] = jnp.dot(
+            scaled_ref[...], held[...], preferred_element_type=F32
+        )
+        place += held.shape[1]
     for chunk in range(chunks):
         fetch(chunk).wait()
         term = jnp.dot(
@@ -403,13 +430,6 @@
             sums_ref[:, :columns] += term
         if chunk + slots < chunks:
             fetch(chunk + slots).start()
-    place = columns
-    for copy, held in zip(side, (key_held, value_held)):
-        copy.wait()
-        sums_ref[:, place : place + held.shape[1]] = jnp.dot(
-            scaled_ref[...], held[...], preferred_element_type=F32
-        )
-        place += held.shape[1]
 
 
 def first_send_body(sums_ref, low_ref, squares_ref, far_1, far_2, far_3, send_ref, keep_ref, full):
@@ -421,7 +441,13 @@
     for place in range(3):
         low = low_ref[:, place * rank : (place + 1) * rank]
         for far in (far_1, far_2, far_3):
-            low = low + far[far.shape[0] - 3 + place, :rows, :].astype(F32)
+            low = low + jnp.concatenate(
+                [
+                    far[at, row : row + 16, :].astype(F32)
+                    for at, row, _ in low_places(far.shape, rows, place)
+                ],
+                axis=0,
+            )
         full[:, columns + place * rank : columns + (place + 1) * rank] = low
     full[:, columns + low_columns :] = split_sum(
         jnp.sum(squares_ref[...], axis=1, keepdims=True), 128
@@ -462,139 +488,203 @@
     far_1,
     far_2,
     far_3,
+    far_values,
+    _,
+    weight_ref,
     heads_ref,
+    block_ref,
     low_query,
     low_narrow,
     turned,
     mixed,
     keys_all,
     values_all,
+    sems,
 ):
     dp_index = lax.axis_index("dp")
     tensor_index = lax.axis_index("tensor")
-    rows = 2 * rows_dev
-    span, head_dim = near.shape[1:]
-    key_heads = keys_all.shape[0] // rows_dev
-    query_columns = heads_ref.shape[1]
-    heads = query_columns // head_dim
-    group = heads // key_heads
-    sources = lax.axis_size("tensor")
-    rank = factors_0.shape[0]
-    owners = lax.axis_size("dp")
-    wide = query_columns // owners
-    narrow = key_heads * head_dim // owners
-
-    for place in range(rows_dev * key_heads):
-        for mask, block in enumerate((near, far_1, far_2, far_3)):
-            rows_here = slice(mask * span, (mask + 1) * span)
-            keys_all[place, rows_here, :] = block[place]
-            values_all[place, rows_here, :] = block[rows_dev * key_heads + place]
-
-    total = kept_ref[...] + arrived_ref[...].astype(F32)
-    joint = query_columns + 2 * key_heads * head_dim
-    squares = jnp.sum(total[:, -128:], axis=1, keepdims=True)
-    scale = lax.rsqrt(squares / D + EPS)
-    lows = [
-        total[:, joint + place * rank : joint + (place + 1) * rank].astype(BF16)
-        for place in range(3)
+    copies = fetch_copies(weight_ref, jnp.bitwise_xor(tensor_index, 2), 0, block_ref, sems)
+    for copy in copies:
+        copy.start()
+    @pl.when(dp_index >= 0)
+    def attended():
+        rows = 2 * rows_dev
+        span, head_dim = near.shape[1:]
+        key_heads = keys_all.shape[0] // rows_dev
+        query_columns = heads_ref.shape[1]
+        heads = query_columns // head_dim
+        group = heads // key_heads
+        sources = lax.axis_size("tensor")
+        rank = factors_0.shape[0]
+        owners = lax.axis_size("dp")
+        wide = query_columns // owners
+        narrow = key_heads * head_dim // owners
+
+        for place in range(rows_dev * key_heads):
+            for mask, block in enumerate((near, far_1, far_2, far_3)):
+                rows_here = slice(mask * span, (mask + 1) * span)
+                keys_all[place, rows_here, :] = block[place]
+                if mask == 3:
+                    values_all[place, rows_here, :] = far_values[place]
+                else:
+                    values_all[place, rows_here, :] = block[rows_dev * key_heads + place]
+
+        total = kept_ref[...] + arrived_ref[...].astype(F32)
+        joint = query_columns + 2 * key_heads * head_dim
+        squares = jnp.sum(total[:, -128:], axis=1, keepdims=True)
+        scale = lax.rsqrt(squares / D + EPS)
+        lows = [
+            total[:, joint + place * rank : joint + (place + 1) * rank].astype(BF16)
+            for place in range(3)
+        ]
+        for mask, factors in enumerate((factors_0, factors_1, factors_2, factors_3)):
+            owner = jnp.bitwise_xor(dp_index, mask)
+            low_query[owner] = jnp.dot(lows[0], factors[:, :wide], preferred_element_type=F32)
+            pair = factors[:, wide : wide + 2 * narrow]
+            for place in range(2):
+                low_narrow[place, owner] = lax.dot_general(
+                    lows[place + 1], pair, (((1,), (1,)), ((), ())), preferred_element_type=F32
+                )
+        cosine = trig_ref[:rows, :]
+        sine = trig_ref[rows:, :]
+
+        def turn(vector):
+            return vector * cosine + pltpu.roll(vector, head_dim // 2, 1) * sine
+
+        def rounded(vector):
+            return vector.astype(BF16).astype(F32)
+
+        for head in range(heads):
+            column = head * head_dim
+            owner, inner = column // wide, column % wide
+            vector = (
+                total[:, column : column + head_dim]
+                + ADAPTER_SCALE * low_query[owner, :, inner : inner + head_dim]
+            )
+            start = (head % group) * rows
+            turned[head // group, start : start + rows, :] = turn(rounded(vector * scale))
+
+        lane = lax.broadcasted_iota(jnp.int32, (rows, head_dim), 1)
+        per_head = head_dim // narrow
+        fresh = [[], []]
+        for place in range(2):
+            for head in range(key_heads):
+                low = jnp.zeros((rows, head_dim), F32)
+                for part in range(per_head):
+                    piece = low_narrow[place, head * per_head + part]
+                    shift = (part * narrow - place * narrow) % (2 * narrow)
+                    if shift:
+                        piece = pltpu.roll(piece, shift, 1)
+                    low = jnp.where(lane // narrow == part, piece, low)
+                column = query_columns + place * key_heads * head_dim + head * head_dim
+                vector = rounded(
+                    (total[:, column : column + head_dim] + ADAPTER_SCALE * low) * scale
+                )
+                fresh[place].append(turn(vector) if place == 0 else vector)
+
+        cached = sources * span
+        width = keys_all.shape[1]
+        column = lax.broadcasted_iota(jnp.int32, (1, width), 1)
+        position = jnp.where(column == cached, -1, 1 << 30)
+        for mask in range(sources):
+            base = jnp.bitwise_xor(tensor_index, mask) * span
+            inside = (column >= mask * span) & (column < (mask + 1) * span)
+            position = jnp.where(inside, column - mask * span + base, position)
+        step = lax.broadcasted_iota(jnp.int32, (2 * group, width), 0) % 2
+        second = (step == 1) & (
+            lax.broadcasted_iota(jnp.int32, (2 * group, width), 1) == cached + 1
+        )
+        score_scale = 1.0 / math.sqrt(head_dim)
+        for row in range(rows_dev):
+            valid = (position < length_ref[row : row + 1, :1]) | second
+            for head in range(key_heads):
+                place = row * key_heads + head
+                for joined, parts in ((keys_all, fresh[0]), (values_all, fresh[1])):
+                    joined[place, cached:, :] = jnp.concatenate(
+                        [
+                            parts[head][row : row + 1],
+                            parts[head][rows_dev + row : rows_dev + row + 1],
+                            jnp.zeros((width - cached - 2, head_dim), F32),
+                        ],
+                        axis=0,
+                    ).astype(BF16)
+                query = turned[head, pl.ds(row, 2 * group, stride=rows_dev), :].astype(BF16)
+                scores = (
+                    lax.dot_general(
+                        query,
+                        keys_all[place],
+                        (((1,), (1,)), ((), ())),
+                        preferred_element_type=F32,
+                    )
+                    * score_scale
+                )
+                scores = jnp.where(valid, scores, MASKED_FILLER)
+                highest = jnp.max(scores, axis=1, keepdims=True)
+                weights = jnp.where(valid, jnp.exp(scores - highest), 0.0)
+                totals = jnp.sum(weights, axis=1, keepdims=True)
+                weighted = jnp.dot(
+                    weights.astype(BF16), values_all[place], preferred_element_type=F32
+                )
+                mixed[head, pl.ds(row, 2 * group, stride=rows_dev), :] = weighted / totals
+        for head in range(heads):
+            start = (head % group) * rows
+            heads_ref[:, head * head_dim : (head + 1) * head_dim] = mixed[
+                head // group, start : start + rows, :
+            ].astype(BF16)
+
+    for copy in copies:
+        copy.wait()
+
+
+def fetch_copies(weight_ref, target, first, block_ref, sems):
+    depth, part = block_ref.shape
+    pieces = sems.shape[0]
+    rows = depth // pieces
+    return [
+        pltpu.make_async_copy(
+            weight_ref.at[
+                pl.ds(first + piece * rows, rows), aligned(target * part, part, 128)
+            ],
+            block_ref.at[pl.ds(piece * rows, rows)],
+            sems.at[piece],
+        )
+        for piece in range(pieces)
     ]
-    for mask, factors in enumerate((factors_0, factors_1, factors_2, factors_3)):
-        owner = jnp.bitwise_xor(dp_index, mask)
-        low_query[owner] = jnp.dot(lows[0], factors[:, :wide], preferred_element_type=F32)
-        pair = factors[:, wide : wide + 2 * narrow]
-        for place in range(2):
-            low_narrow[place, owner] = lax.dot_general(
-                lows[place + 1], pair, (((1,), (1,)), ((), ())), preferred_element_type=F32
+
+
+def fetch_body(pieces, weight_ref, _, *blocks_and_sems):
+    *blocks, sems = blocks_and_sems
+    copies = []
+    for place, ((mask, first), block_ref) in enumerate(zip(pieces, blocks)):
+        target = jnp.bitwise_xor(lax.axis_index("tensor"), mask)
+        copies += fetch_copies(weight_ref, target, first, block_ref, sems.at[place])
+    for copy in copies:
+        copy.start()
+    for copy in copies:
+        copy.wait()
+
+
+def product(rows_ref, *blocks):
+    width = math.gcd(blocks[0].shape[1], 512)
+    results = []
+    for start in range(0, blocks[0].shape[1], width):
+        first, result = 0, None
+        for block in blocks:
+            depth = block.shape[0]
+            term = jnp.dot(
+                rows_ref[:, first : first + depth],
+                block[:, start : start + width],
+                preferred_element_type=F32,
             )
-    cosine = trig_ref[:rows, :]
-    sine = trig_ref[rows:, :]
-
-    def turn(vector):
-        return vector * cosine + pltpu.roll(vector, head_dim // 2, 1) * sine
-
-    def rounded(vector):
-        return vector.astype(BF16).astype(F32)
-
-    for head in range(heads):
-        column = head * head_dim
-        owner, inner = column // wide, column % wide
-        vector = (
-            total[:, column : column + head_dim]
-            + ADAPTER_SCALE * low_query[owner, :, inner : inner + head_dim]
-        )
-        start = (head % group) * rows
-        turned[head // group, start : start + rows, :] = turn(rounded(vector * scale))
-
-    lane = lax.broadcasted_iota(jnp.int32, (rows, head_dim), 1)
-    per_head = head_dim // narrow
-    fresh = [[], []]
-    for place in range(2):
-        for head in range(key_heads):
-            low = jnp.zeros((rows, head_dim), F32)
-            for part in range(per_head):
-                piece = low_narrow[place, head * per_head + part]
-                shift = (part * narrow - place * narrow) % (2 * narrow)
-                if shift:
-                    piece = pltpu.roll(piece, shift, 1)
-                low = jnp.where(lane // narrow == part, piece, low)
-            column = query_columns + place * key_heads * head_dim + head * head_dim
-            vector = rounded(
-                (total[:, column : column + head_dim] + ADAPTER_SCALE * low) * scale
-            )
-            fresh[place].append(turn(vector) if place == 0 else vector)
-
-    cached = sources * span
-    width = keys_all.shape[1]
-    column = lax.broadcasted_iota(jnp.int32, (1, width), 1)
-    position = jnp.where(column == cached, -1, 1 << 30)
-    for mask in range(sources):
-        base = jnp.bitwise_xor(tensor_index, mask) * span
-        inside = (column >= mask * span) & (column < (mask + 1) * span)
-        position = jnp.where(inside, column - mask * span + base, position)
-    step = lax.broadcasted_iota(jnp.int32, (2 * group, width), 0) % 2
-    second = (step == 1) & (
-        lax.broadcasted_iota(jnp.int32, (2 * group, width), 1) == cached + 1
-    )
-    score_scale = 1.0 / math.sqrt(head_dim)
-    for row in range(rows_dev):
-        valid = (position < length_ref[row : row + 1, :1]) | second
-        for head in range(key_heads):
-            place = row * key_heads + head
-            for joined, parts in ((keys_all, fresh[0]), (values_all, fresh[1])):
-                joined[place, cached:, :] = jnp.concatenate(
-                    [
-                        parts[head][row : row + 1],
-                        parts[head][rows_dev + row : rows_dev + row + 1],
-                        jnp.zeros((width - cached - 2, head_dim), F32),
-                    ],
-                    axis=0,
-                ).astype(BF16)
-            query = turned[head, pl.ds(row, 2 * group, stride=rows_dev), :].astype(BF16)
-            scores = (
-                lax.dot_general(
-                    query,
-                    keys_all[place],
-                    (((1,), (1,)), ((), ())),
-                    preferred_element_type=F32,
-                )
-                * score_scale
-            )
-            scores = jnp.where(valid, scores, MASKED_FILLER)
-            highest = jnp.max(scores, axis=1, keepdims=True)
-            weights = jnp.where(valid, jnp.exp(scores - highest), 0.0)
-            totals = jnp.sum(weights, axis=1, keepdims=True)
-            weighted = jnp.dot(
-                weights.astype(BF16), values_all[place], preferred_element_type=F32
-            )
-            mixed[head, pl.ds(row, 2 * group, stride=rows_dev), :] = weighted / totals
-    for head in range(heads):
-        start = (head % group) * rows
-        heads_ref[:, head * head_dim : (head + 1) * head_dim] = mixed[
-            head // group, start : start + rows, :
-        ].astype(BF16)
-
-
-def output_body(
+            result = term if result is None else result + term
+            first += depth
+        results.append(result)
+    return jnp.concatenate(results, axis=1)
+
+
+def far_output_body(
+    mask,
+    first,
     heads_0,
     heads_1,
     heads_2,
@@ -603,74 +693,80 @@
     factors_1,
     factors_2,
     factors_3,
+    block_ref,
+    _,
     weight_ref,
-    send_1,
-    send_2,
-    send_3,
-    keep_ref,
+    send_ref,
+    low_ref,
+    all_rows,
+    fetched_ref,
     wide_rows,
-    all_rows,
-    sums,
-    ring,
-    ring_sem,
+    sems,
 ):
     dp_index = lax.axis_index("dp")
-    tensor_index = lax.axis_index("tensor")
-    slots, depth, columns = ring.shape
-    chunks = weight_ref.shape[0] // depth
-
-    def fetch(chunk):
-        slot = chunk % slots
-        return pltpu.make_async_copy(
-            weight_ref.at[pl.ds(chunk * depth, depth)], ring.at[slot], ring_sem.at[slot]
-        )
-
-    for chunk in range(min(slots, chunks)):
-        fetch(chunk).start()
-    share = heads_0.shape[0]
-    for mask, part in enumerate((heads_0, heads_1, heads_2, heads_3)):
-        owner = jnp.bitwise_xor(dp_index, mask)
-        wide_rows[aligned(owner * share, share, 8), :] = part[...].astype(F32)
-    all_rows[...] = wide_rows[...].astype(BF16)
-    rank = factors_0.shape[0]
-    block = all_rows.shape[1] // lax.axis_size("dp")
-    pieces = block // rank
-    base = factors_0.shape[1] - pieces * rank
-    low = jnp.zeros((all_rows.shape[0], rank), F32)
-    for mask, factors in enumerate((factors_0, factors_1, factors_2, factors_3)):
-        owner = jnp.bitwise_xor(dp_index, mask)
-        for piece in range(pieces):
-            low = low + jnp.dot(
-                all_rows[:, aligned(owner * block + piece * rank, rank, 128)],
-                factors[:, base + piece * rank : base + (piece + 1) * rank],
-                preferred_element_type=F32,
-            )
-    for chunk in range(chunks):
-        fetch(chunk).wait()
-        term = jnp.dot(
-            all_rows[:, chunk * depth : (chunk + 1) * depth],
-            ring[chunk % slots],
-            preferred_element_type=F32,
-        )
-        if chunk == 0:
-            sums[...] = term
+    target = jnp.bitwise_xor(lax.axis_index("tensor"), mask)
+    copies = fetch_copies(weight_ref, target, first, fetched_ref, sems)
+    for copy in copies:
+        copy.start()
+    @pl.when(dp_index >= 0)
+    def multiplied():
+        share = heads_0.shape[0]
+        for distance, part in enumerate((heads_0, heads_1, heads_2, heads_3)):
+            owner = jnp.bitwise_xor(dp_index, distance)
+            wide_rows[aligned(owner * share, share, 8), :] = part[...].astype(F32)
+        all_rows[...] = wide_rows[...].astype(BF16)
+        rank = factors_0.shape[0]
+        block = all_rows.shape[1] // lax.axis_size("dp")
+        pieces = block // rank
+        base = factors_0.shape[1] - pieces * rank
+        low = jnp.zeros((all_rows.shape[0], rank), F32)
+        for distance, factors in enumerate((factors_0, factors_1, factors_2, factors_3)):
+            owner = jnp.bitwise_xor(dp_index, distance)
+            for piece in range(pieces):
+                low = low + jnp.dot(
+                    all_rows[:, aligned(owner * block + piece * rank, rank, 128)],
+                    factors[:, base + piece * rank : base + (piece + 1) * rank],
+                    preferred_element_type=F32,
+                )
+        low_ref[...] = low
+        part = block_ref.shape[1]
+        send_ref[:, :part] = product(all_rows, block_ref).astype(BF16)
+        send_ref[:, part:] = low.astype(BF16)
+
+    for copy in copies:
+        copy.wait()
+
+
+def next_output_body(all_rows, low_ref, *blocks_and_result):
+    *blocks, result_ref = blocks_and_result
+    part = blocks[0].shape[1]
+    result_ref[:, :part] = product(all_rows, *blocks).astype(result_ref.dtype)
+    result_ref[:, part:] = low_ref[...].astype(result_ref.dtype)
+
+
+def own_output_body(all_rows, low_ref, weight_ref, result_ref, held, sems):
+    copies = fetch_copies(weight_ref, lax.axis_index("tensor"), 0, held, sems)
+    for copy in copies:
+        copy.start()
+    part = held.shape[1]
+    rows = held.shape[0] // len(copies)
+    result_ref[:, part:] = low_ref[...]
+    for piece, copy in enumerate(copies):
+        copy.wait()
+        here = slice(piece * rows, (piece + 1) * rows)
+        term = jnp.dot(all_rows[:, here], held[here, :], preferred_element_type=F32)
+        if piece == 0:
+            result_ref[:, :part] = term
         else:
-            sums[...] += term
-        if chunk + slots < chunks:
-            fetch(chunk + slots).start()
-    part = columns // lax.axis_size("tensor")
-    for mask, send in ((1, send_1), (2, send_2), (3, send_3)):
-        target = jnp.bitwise_xor(tensor_index, mask)
-        send[:, :part] = sums[:, aligned(target * part, part, 128)].astype(BF16)
-        send[:, part:] = low.astype(BF16)
-    keep_ref[:, :part] = sums[:, aligned(tensor_index * part, part, 128)]
-    keep_ref[:, part:] = low
-
-
-def finish_body(rows_dev, keep_ref, far_1, far_2, far_3, b_out_ref, part_ref):
-    total = keep_ref[...]
-    for far in (far_1, far_2, far_3):
-        total = total + far[...].astype(F32)
+            result_ref[:, :part] += term
+
+
+def add_far_body(keep_ref, far, sum_ref):
+    sum_ref[...] = keep_ref[...] + far[...].astype(F32)
+
+
+def finish_body(rows_dev, sum_ref, far_1, b_out_ref, part_ref):
+    total = sum_ref[...] + far_1[...].astype(F32)
     part = b_out_ref.shape[1]
     low = total[:, part:].astype(BF16)
     result = total[:, :part] + ADAPTER_SCALE * jnp.dot(
@@ -738,18 +834,20 @@
     share = 2 * rows_dev
     low_columns = 3 * rank
     blocks = 2 * rows_dev * key_heads
+    low_blocks = -(-3 * both // span)
     pack_columns = b_query.shape[1] + rank + a_out.shape[0]
 
-    scaled, squares, low, near, far_1, far_2, far_3, factors = kernel_call(
+    scaled, squares, low, near, far_1, far_2, far_3, far_values, factors = kernel_call(
         functools.partial(prepare_body, rows_dev),
         (
             shape((both, width), BF16),
             shape((both, 128), F32),
             shape((both, low_columns), F32),
             shape((blocks, span, head_dim), BF16),
-            shape((blocks + 3, span, head_dim), BF16),
-            shape((blocks + 3, span, head_dim), BF16),
-            shape((blocks + 3, span, head_dim), BF16),
+            shape((blocks + low_blocks, span, head_dim), BF16),
+            shape((blocks + low_blocks, span, head_dim), BF16),
+            shape((blocks // 2 + low_blocks, span, head_dim), BF16),
+            shape((blocks // 2, span, head_dim), BF16),
             shape((rank, pack_columns), BF16),
         ),
         [hbm_spec()] * 12,
@@ -759,7 +857,7 @@
             pltpu.VMEM((3,) + a_query.shape, BF16),
             pltpu.SemaphoreType.DMA((3,)),
         ],
-        moved=6e6,
+        moved=12e6,
     )(
         *in_hbm(
             hidden_first,
@@ -798,7 +896,31 @@
             pltpu.SemaphoreType.DMA((3,)),
         ],
         moved=2 * width * joint,
+        mib=16,
     )(*in_hbm(lengths), scaled, *in_hbm(query_weight, w_key, w_value))
+    heads_here = query_columns // head_dim
+    out_columns = w_out.shape[1]
+    part = out_columns // n_tensor
+    eighth = w_out.shape[0] // 8
+
+    def weight_block(eighths):
+        return pltpu.VMEM((eighths * eighth, part), BF16)
+
+    (w_out,) = in_hbm(w_out)
+    fetch_sems = pltpu.SemaphoreType.DMA((4,))
+
+    def fetched(after, *pieces):
+        return kernel_call(
+            functools.partial(
+                fetch_body, [(mask, first * eighth) for mask, first, _ in pieces]
+            ),
+            tuple(weight_block(eighths) for _, _, eighths in pieces),
+            [hbm_spec(), any_spec()],
+            [pltpu.SemaphoreType.DMA((len(pieces), 4))],
+            mib=4,
+            moved=2 * sum(eighths for _, _, eighths in pieces) * eighth * part,
+        )(w_out, after)
+
     extended = joint + low_columns + 128
     send, keep = kernel_call(
         first_send_body,
@@ -806,10 +928,11 @@
         [vmem_spec()] * 6,
         [pltpu.VMEM((both, extended), F32)],
     )(sums, low, squares, *far)
-    factors_x, send = lax.optimization_barrier((factors_x, send))
-    arrived = swapped(send, "dp", 1)
+    factors_x, far_values, send = lax.optimization_barrier((factors_x, far_values, send))
+    far_values = swapped(far_values, "tensor", 3)
     factors_both = swapped(factors_x, "dp", 1)
     all_factors = (factors, factors_core, factors_x, factors_both)
+    arrived = swapped(send, "dp", 1)
     send, kept = kernel_call(
         second_send_body,
         (shape((share, extended), BF16), shape((share, extended), F32)),
@@ -817,14 +940,14 @@
         [pltpu.VMEM((rows, extended), F32)],
     )(keep, arrived)
     arrived = swapped(send, "dp", 2)
-    heads_here = query_columns // head_dim
+    (block_3,) = fetched(send, (3, 0, 8))
     group = heads_here // key_heads
     positions = n_tensor * span + 16
     owners = lax.axis_size("dp")
-    (heads,) = kernel_call(
+    heads, block_2 = kernel_call(
         functools.partial(attend_body, rows_dev),
-        (shape((share, query_columns), BF16),),
-        [vmem_spec()] * 12,
+        (shape((share, query_columns), BF16), weight_block(6)),
+        [vmem_spec()] * 13 + [any_spec(), hbm_spec()],
         [
             pltpu.VMEM((owners, share, query_columns // owners), F32),
             pltpu.VMEM((2, owners, share, 2 * key_columns // owners), F32),
@@ -832,40 +955,64 @@
             pltpu.VMEM((key_heads, group * share, head_dim), F32),
             pltpu.VMEM((rows_dev * key_heads, positions, head_dim), BF16),
             pltpu.VMEM((rows_dev * key_heads, positions, head_dim), BF16),
+            fetch_sems,
         ],
         moved=10e6,
-    )(length, trig, kept, arrived, *all_factors, near, *far)
+    )(length, trig, kept, arrived, *all_factors, near, *far, far_values, block_3, w_out)
 
     heads_x = swapped(heads, "dp", 2)
     heads_core = swapped(heads, "dp", 1)
+    last_2, block_1 = fetched(heads, (2, 6, 2), (1, 0, 4))
+    heads_x, _ = lax.optimization_barrier((heads_x, block_1))
     heads_both = swapped(heads_x, "dp", 1)
-    out_columns = w_out.shape[1]
-    part = out_columns // n_tensor
-    depth = math.gcd(w_out.shape[0], 256)
-    send_1, send_2, send_3, keep = kernel_call(
-        output_body,
+    message = shape((both, part + rank), BF16)
+    summed = shape((both, part + rank), F32)
+    send_3, low, all_rows, last_1 = kernel_call(
+        functools.partial(far_output_body, 1, 4 * eighth),
         (
-            shape((both, part + rank), BF16),
-            shape((both, part + rank), BF16),
-            shape((both, part + rank), BF16),
-            shape((both, part + rank), F32),
+            message,
+            shape((both, rank), F32),
+            shape((both, w_out.shape[0]), BF16),
+            weight_block(4),
         ),
-        [vmem_spec()] * 8 + [hbm_spec()],
-        [
-            pltpu.VMEM((both, w_out.shape[0]), F32),
-            pltpu.VMEM((both, w_out.shape[0]), BF16),
-            pltpu.VMEM((both, out_columns), F32),
-            pltpu.VMEM((4, depth, out_columns), BF16),
-            pltpu.SemaphoreType.DMA((4,)),
-        ],
-        moved=2 * w_out.size,
-    )(heads, heads_core, heads_x, heads_both, *all_factors, *in_hbm(w_out))
-    far = [swapped(block, "tensor", mask) for mask, block in ((1, send_1), (2, send_2), (3, send_3))]
+        [vmem_spec()] * 9 + [any_spec(), hbm_spec()],
+        [pltpu.VMEM((both, w_out.shape[0]), F32), fetch_sems],
+        mib=8,
+        moved=10e6,
+    )(heads, heads_core, heads_x, heads_both, *all_factors, block_3, block_1, w_out)
+    far_3 = swapped(send_3, "tensor", 3)
+
+    def next_output(*weights):
+        return kernel_call(
+            next_output_body,
+            (message,),
+            [vmem_spec()] * (2 + len(weights)),
+            mib=8,
+            moved=40e6,
+        )(all_rows, low, *weights)[0]
+
+    def added(total, far_part, moved):
+        return kernel_call(add_far_body, (summed,), [vmem_spec()] * 2, mib=8, moved=moved)(
+            total, far_part
+        )[0]
+
+    far_2 = swapped(next_output(block_2, last_2), "tensor", 2)
+    far_1 = swapped(next_output(block_1, last_1), "tensor", 1)
+    (total,) = kernel_call(
+        own_output_body,
+        (summed,),
+        [vmem_spec(), vmem_spec(), hbm_spec()],
+        [weight_block(8), pltpu.SemaphoreType.DMA((8,))],
+        mib=12,
+        moved=40e6,
+    )(all_rows, low, w_out)
+    total = added(added(total, far_3, 40e6), far_2, 40e6)
     (done,) = kernel_call(
         functools.partial(finish_body, rows_dev),
         (shape((both, part), BF16),),
-        [vmem_spec()] * 5,
-    )(keep, *far, b_out)
+        [vmem_spec()] * 3,
+        mib=8,
+    )(total, far_1, b_out)
     parts = [done] + [swapped(done, "tensor", mask) for mask in (1, 2, 3)]
     return kernel_call(
         place_body,

time: 76.5 us -> 64.1 us (0.84)
  waiting for transfers between devices: 24 us -> 5.65 us
  Pallas kernels: 31.5 us -> 34.6 us
  starting transfers between devices: 20 us -> 22.7 us
    ppermute x17 -> x18, waiting for transfers between devices: 24 us -> 5.65 us  [swapped(): return lax.ppermute(array, axis, [(k, k ^ mask) for k in range(size)])]
    pallas_call x1 -> x8, Pallas kernels: 12 us -> 15.6 us  [the longest x2 6.42 us: fetched(): kernel_call(functools.partial(fetch_body, [(mask, first * eighth) for mas...]
    ppermute x17 -> x18, starting transfers between devices: 20 us -> 22.7 us  [swapped(): return lax.ppermute(array, axis, [(k, k ^ mask) for k in range(size)])]
  transfers between devices with their start and end apart: 17 -> 18, of which waited for: 9 -> 5; matrix products, arithmetic and copies ran while one was open for 0% -> 0% of each run, Pallas kernels for 19% -> 42%
where the time goes in v2:
time: 64.1 us; the launch traced here: 63.9 us
  Pallas kernels  34.6 us (54%)
  starting transfers between devices  22.7 us (35%)
  waiting for transfers between devices  5.65 us (9%)
  between operations  0.98 us (2%)
    ppermute x18, starting transfers between devices, swapped(): return lax.ppermute(array, axis, [(k, k ^ mask) for k in range(size)])  22.7 us
    pallas_call x1, Pallas kernels, on_device_joined(): kernel_call(functools.partial(project_body, rows_dev), (shape((both, join...  13.4 us
    pallas_call x2, Pallas kernels, fetched(): kernel_call(functools.partial(fetch_body, [(mask, first * eighth) for mas...  6.42 us
    ppermute x18, waiting for transfers between devices, swapped(): return lax.ppermute(array, axis, [(k, k ^ mask) for k in range(size)])  5.65 us
    pallas_call x1, Pallas kernels, on_device_joined(): kernel_call(own_output_body, (summed,), [vmem_spec(), vmem_spec(), hbm_sp...  3.79 us
    pallas_call x2, Pallas kernels, next_output(): kernel_call(next_output_body, (message,), [vmem_spec()] * (2 + len(weight...  3.09 us
    pallas_call x1, Pallas kernels, on_device_joined(): kernel_call(functools.partial(attend_body, rows_dev), (shape((share, quer...  2.88 us
    pallas_call x1, Pallas kernels, on_device_joined(): kernel_call(functools.partial(far_output_body, 1, 4 * eighth), (message,...  2.22 us
  transfers between devices with their start and end apart: 18, of which 5 were waited for; matrix products, arithmetic and copies ran while one was open for 0% of the time, Pallas kernels for 42%

profile of v2, /device:TPU:0, one launch (start us, length us, event | category | flops | bytes accessed | tf_op | source)
XLA Modules:
  0.0 63.9 jit_solution(11805978165432505692)
XLA Ops:
  0.6 1.6 %shard_map.185 = (bf16[32,4096]{1,0:T(8,128)(2,1)S(1)}, f32[32,128]{1,0:T(8,128)S(1)}, f32[32,384]{1,0:T(8,128)S(1)}, bf16[16,48,128]{2,1,0:T(8,128)(2,1)S(1)}, ...) custom-call(bf16[16,4096]{1,0:T(8,128)(2,1)} %first_ref.1, ...), custom_call_target="tpu_custom_call" | custom-call | bytes 12000000 | tf_op jit(solution)/shard_map/pallas_call | solution.py:840
  2.3 3.0 %collective-permute-start.3 = (bf16[128,2176]{1,0:T(8,128)(2,1)S(1)}, bf16[128,2176]{1,0:T(8,128)(2,1)S(1)}, u32[]{:S(2)}, u32[]{:S(2)}) collective-permute-start(bf16[128,2176]{1,0:T(8,128)(2,1)S(1)} %get-tuple-element.40.factors_0), channel_id=1, source_target_pairs={{0,8},{4,12},{8,0},{12,4},{1,9},{5,13},{9,1},{13,5},{2,10},{6,14},... | collective-permute-start | bytes 1671176 | tf_op jit(solution)/shard_map/ppermute | solution.py:197
  5.3 1.6 %collective-permute-start = (bf16[18,48,128]{2,1,0:T(8,128)(2,1)S(1)}, bf16[18,48,128]{2,1,0:T(8,128)(2,1)S(1)}, u32[]{:S(2)}, u32[]{:S(2)}) collective-permute-start(bf16[18,48,128]{2,1,0:T(8,128)(2,1)S(1)} %get-tuple-element.36), channel_id=1, source_target_pairs={{0,1},{1,0},{2,3},{3,2},{4,5},{5,4},{6,7},{7,6},{8,9},{9,8},{10,11... | collective-permute-start | bytes 663560 | tf_op jit(solution)/shard_map/ppermute | solution.py:197
  6.9 2.6 %collective-permute-start.1 = (bf16[18,48,128]{2,1,0:T(8,128)(2,1)S(1)}, bf16[18,48,128]{2,1,0:T(8,128)(2,1)S(1)}, u32[]{:S(2)}, u32[]{:S(2)}) collective-permute-start(bf16[18,48,128]{2,1,0:T(8,128)(2,1)S(1)} %get-tuple-element.37), channel_id=1, source_target_pairs={{0,2},{1,3},{2,0},{3,1},{4,6},{5,7},{6,4},{7,5},{8,10},{9,11},{10,... | collective-permute-start | bytes 663560 | tf_op jit(solution)/shard_map/ppermute | solution.py:197
  9.4 0.2 collective-permute-start.2
  9.7 0.0 collective-permute-start.6
  9.7 13.4 %shard_map.186 = (f32[32,4608]{1,0:T(8,128)S(1)}, f32[16,128]{1,0:T(8,128)S(1)}, s32[8,128]{1,0:T(8,128)S(1)}) custom-call(s32[4]{0:T(128)} %lengths_ref.1, bf16[32,4096]{1,0:T(8,128)(2,1)S(1)} %get-tuple-element.30.scaled_ref, bf16[4096,4096]{1,0:T(8,128)(2,1)} %query_ref.1, bf16[4096,256]{1,0:T(8,128)(2,1)} %key_ref.1, bf16[4096,256]{1,0:T(8,128)(2,1)} %value_ref.1), custom_call_target="tpu_custom_call" | custom-call | bytes 37748736 | tf_op jit(solution)/shard_map/pallas_call | solution.py:882
  23.1 0.0 collective-permute-done.2.far_3
  23.1 0.0 collective-permute-done.far_1
  23.1 0.0 collective-permute-done.1.far_2
  23.1 0.1 shard_map.187
  23.2 0.0 collective-permute-done.3.factors_2
  23.2 0.6 collective-permute-start.7
  23.8 0.1 collective-permute-start.4
  23.9 3.6 %collective-permute-start.8 = (bf16[8,48,128]{2,1,0:T(8,128)(2,1)S(1)}, bf16[8,48,128]{2,1,0:T(8,128)(2,1)S(1)}, u32[]{:S(2)}, u32[]{:S(2)}) collective-permute-start(bf16[8,48,128]{2,1,0:T(8,128)(2,1)S(1)} %get-tuple-element.48), channel_id=1, source_target_pairs={{0,3},{1,2},{2,1},{3,0},{4,7},{5,6},{6,5},{7,4},{8,11},{9,10},{10,... | collective-permute-start | bytes 294920 | tf_op jit(solution)/shard_map/ppermute | solution.py:197
  27.5 0.0 collective-permute-done.4.arrived_ref
  27.5 0.1 shard_map.188
  27.6 0.6 collective-permute-start.5
  28.2 3.5 %shard_map.189._.block_ref = bf16[4096,1024]{1,0:T(8,128)(2,1)S(1)} custom-call(bf16[4096,4096]{1,0:T(8,128)(2,1)} %weight_ref.9, bf16[8,5120]{1,0:T(8,128)(2,1)S(1)} %get-tuple-element.45._), custom_call_target="tpu_custom_call" | custom-call | bytes 8388608 | tf_op jit(solution)/shard_map/pallas_call | solution.py:913
  31.7 0.0 collective-permute-done.6.factors_1
  31.7 0.0 collective-permute-done.8.far_values
  31.7 0.4 collective-permute-done.5.arrived_ref
  32.2 0.0 collective-permute-done.7.factors_3
  32.2 2.9 %shard_map.190 = (bf16[8,4096]{1,0:T(8,128)(2,1)S(1)}, bf16[3072,1024]{1,0:T(8,128)(2,1)S(1)}) custom-call(s32[8,128]{1,0:T(8,128)S(1)} %get-tuple-element.31.length_ref, f32[16,128]{1,0:T(8,128)S(1)} %get-tuple-element.32.trig_ref, f32[8,5120]{1,0:T(8,128)S(1)} %get-tuple-element.44.kept_ref, bf16[8,5120]{1,0:T(8,128)(2,1)S(1)} %collective-permute-done.5.arrived_ref, ...), custom_call_target="tpu_custom_call" | custom-call | bytes 10000000 | tf_op jit(solution)/shard_map/pallas_call | solution.py:947
  35.1 1.2 %collective-permute-start.10 = (bf16[8,4096]{1,0:T(8,128)(2,1)S(1)}, bf16[8,4096]{1,0:T(8,128)(2,1)S(1)}, u32[]{:S(2)}, u32[]{:S(2)}) collective-permute-start(bf16[8,4096]{1,0:T(8,128)(2,1)S(1)} %get-tuple-element.49._.heads_0), channel_id=1, source_target_pairs={{0,8},{4,12},{8,0},{12,4},{1,9},{5,13},{9,1},{13,5},{2,10},{6,14},... | collective-permute-start | bytes 196616 | tf_op jit(solution)/shard_map/ppermute | solution.py:197
  36.2 0.0 collective-permute-start.9
  36.2 2.9 %shard_map.191 = (bf16[1024,1024]{1,0:T(8,128)(2,1)S(1)}, bf16[2048,1024]{1,0:T(8,128)(2,1)S(1)}) custom-call(bf16[4096,4096]{1,0:T(8,128)(2,1)} %weight_ref.9, bf16[8,4096]{1,0:T(8,128)(2,1)S(1)} %get-tuple-element.49._.heads_0), custom_call_target="tpu_custom_call" | custom-call | bytes 6291456 | tf_op jit(solution)/shard_map/pallas_call | solution.py:913
  39.1 0.3 collective-permute-done.10.heads_2
  39.4 0.3 collective-permute-start.11
  39.7 0.0 collective-permute-done.9.heads_1
  39.7 0.9 %collective-permute-done.11.heads_3 = bf16[8,4096]{1,0:T(8,128)(2,1)S(1)} collective-permute-done((bf16[8,4096]{1,0:T(8,128)(2,1)S(1)}, bf16[8,4096]{1,0:T(8,128)(2,1)S(1)}, u32[]{:S(2)}, u32[]{:S(2)}) %collective-permute-start.11) | collective-permute-done | bytes 65568 | tf_op jit(solution)/shard_map/ppermute | solution.py:197
  40.7 2.2 %shard_map.192 = (bf16[32,1152]{1,0:T(8,128)(2,1)S(1)}, f32[32,128]{1,0:T(8,128)S(1)}, bf16[32,4096]{1,0:T(8,128)(2,1)S(1)}, bf16[2048,1024]{1,0:T(8,128)(2,1)S(1)}) custom-call(bf16[8,4096]{1,0:T(8,128)(2,1)S(1)} %get-tuple-element.49._.heads_0, bf16[8,4096]{1,0:T(8,128)(2,1)S(1)} %collective-permute-done.9.heads_1, ...), custom_call_target="tpu_custom_call" | custom-call | bytes 10000000 | tf_op jit(solution)/shard_map/pallas_call | solution.py:970
  42.9 2.4 %collective-permute-start.12 = (bf16[32,1152]{1,0:T(8,128)(2,1)S(1)}, bf16[32,1152]{1,0:T(8,128)(2,1)S(1)}, u32[]{:S(2)}, u32[]{:S(2)}) collective-permute-start(bf16[32,1152]{1,0:T(8,128)(2,1)S(1)} %get-tuple-element.54), channel_id=1, source_target_pairs={{0,3},{1,2},{2,1},{3,0},{4,7},{5,6},{6,5},{7,4},{8,11},{9,10},{10,... | collective-permute-start | bytes 221192 | tf_op jit(solution)/shard_map/ppermute | solution.py:197
  45.2 1.5 %shard_map.195 = bf16[32,1152]{1,0:T(8,128)(2,1)S(1)} custom-call(bf16[32,4096]{1,0:T(8,128)(2,1)S(1)} %get-tuple-element.52.all_rows, f32[32,128]{1,0:T(8,128)S(1)} %get-tuple-element.53.low_ref, bf16[3072,1024]{1,0:T(8,128)(2,1)S(1)} %get-tuple-element.55.blocks_and_result_0_, bf16[1024,1024]{1,0:T(8,128)(2,1)S(1)} %get-tuple-element.56.blocks_and_result_1_), custom_call_target="tpu_custom_call" | custom-call | bytes 40000000 | tf_op jit(solution)/shard_map/pallas_call | solution.py:986
  46.8 0.0 collective-permute-start.13
  46.8 1.5 %shard_map.197 = bf16[32,1152]{1,0:T(8,128)(2,1)S(1)} custom-call(bf16[32,4096]{1,0:T(8,128)(2,1)S(1)} %get-tuple-element.52.all_rows, f32[32,128]{1,0:T(8,128)S(1)} %get-tuple-element.53.low_ref, bf16[2048,1024]{1,0:T(8,128)(2,1)S(1)} %get-tuple-element.50._.blocks_and_result_0_, bf16[2048,1024]{1,0:T(8,128)(2,1)S(1)} %get-tuple-element.57.blocks_and_result_1_), custom_call_target="tpu_custom_call" | custom-call | bytes 40000000 | tf_op jit(solution)/shard_map/pallas_call | solution.py:986
  48.4 2.1 %collective-permute-start.14 = (bf16[32,1152]{1,0:T(8,128)(2,1)S(1)}, bf16[32,1152]{1,0:T(8,128)(2,1)S(1)}, u32[]{:S(2)}, u32[]{:S(2)}) collective-permute-start(bf16[32,1152]{1,0:T(8,128)(2,1)S(1)} %shard_map.197), channel_id=1, source_target_pairs={{0,1},{1,0},{2,3},{3,2},{4,5},{5,4},{6,7},{7,6},{8,9},{9,8},{10,11... | collective-permute-start | bytes 221192 | tf_op jit(solution)/shard_map/ppermute | solution.py:197
  50.5 3.8 %shard_map.193.keep_ref = f32[32,1152]{1,0:T(8,128)S(1)} custom-call(bf16[32,4096]{1,0:T(8,128)(2,1)S(1)} %get-tuple-element.52.all_rows, f32[32,128]{1,0:T(8,128)S(1)} %get-tuple-element.53.low_ref, bf16[4096,4096]{1,0:T(8,128)(2,1)} %weight_ref.9), custom_call_target="tpu_custom_call" | custom-call | bytes 40000000 | tf_op jit(solution)/shard_map/pallas_call | solution.py:1001
  54.3 0.0 collective-permute-done.12.far
  54.3 0.0 collective-permute-done.13.far
  54.3 0.0 collective-permute-done.14.far_1
  54.4 0.2 shard_map.198.part_0
  54.5 2.4 %collective-permute-start.17 = (bf16[32,1024]{1,0:T(8,128)(2,1)S(1)}, bf16[32,1024]{1,0:T(8,128)(2,1)S(1)}, u32[]{:S(2)}, u32[]{:S(2)}) collective-permute-start(bf16[32,1024]{1,0:T(8,128)(2,1)S(1)} %shard_map.198.part_0), channel_id=1, source_target_pairs={{0,3},{1,2},{2,1},{3,0},{4,7},{5,6},{6,5},{7,4},{8,11},{9,10},{10,... | collective-permute-start | bytes 196616 | tf_op jit(solution)/shard_map/ppermute | solution.py:197
  56.9 2.1 %collective-permute-start.15 = (bf16[32,1024]{1,0:T(8,128)(2,1)S(1)}, bf16[32,1024]{1,0:T(8,128)(2,1)S(1)}, u32[]{:S(2)}, u32[]{:S(2)}) collective-permute-start(bf16[32,1024]{1,0:T(8,128)(2,1)S(1)} %shard_map.198.part_0), channel_id=1, source_target_pairs={{0,1},{1,0},{2,3},{3,2},{4,5},{5,4},{6,7},{7,6},{8,9},{9,8},{10,11... | collective-permute-start | bytes 196616 | tf_op jit(solution)/shard_map/ppermute | solution.py:197
  59.0 1.9 %collective-permute-done.17.part_3 = bf16[32,1024]{1,0:T(8,128)(2,1)S(1)} collective-permute-done((bf16[32,1024]{1,0:T(8,128)(2,1)S(1)}, bf16[32,1024]{1,0:T(8,128)(2,1)S(1)}, u32[]{:S(2)}, u32[]{:S(2)}) %collective-permute-start.17) | collective-permute-done | bytes 65568 | tf_op jit(solution)/shard_map/ppermute | solution.py:197
  60.9 2.1 %collective-permute-done.16.part_2 = bf16[32,1024]{1,0:T(8,128)(2,1)S(1)} collective-permute-done((bf16[32,1024]{1,0:T(8,128)(2,1)S(1)}, bf16[32,1024]{1,0:T(8,128)(2,1)S(1)}, u32[]{:S(2)}, u32[]{:S(2)}) %collective-permute-start.16) | collective-permute-done | bytes 65568 | tf_op jit(solution)/shard_map/ppermute | solution.py:197
  63.0 0.0 collective-permute-done.15.part_1
  63.0 0.8 %shard_map.199 = (bf16[16,4096]{1,0:T(8,128)(2,1)}, bf16[16,4096]{1,0:T(8,128)(2,1)}) custom-call(bf16[32,1024]{1,0:T(8,128)(2,1)S(1)} %shard_map.198.part_0, bf16[32,1024]{1,0:T(8,128)(2,1)S(1)} %collective-permute-done.15.part_1, bf16[32,1024]{1,0:T(8,128)(2,1)S(1)} %collective-permute-done.16.part_2, bf16[32,1024]{1,0:T(8,128)(2,1)S(1)} %collective-permute-done.17.part_3), custom_call_target="tpu_custom_call" | custom-call | tf_op jit(solution)/shard_map/pallas_call | solution.py:1017
  (5 shorter events, 0.0 us)
Async XLA Ops:
  2.3 20.9 %collective-permute-start.3 = (bf16[128,2176]{1,0:T(8,128)(2,1)S(1)}, bf16[128,2176]{1,0:T(8,128)(2,1)S(1)}, u32[]{:S(2)}, u32[]{:S(2)}) collective-permute-start(bf16[128,2176]{1,0:T(8,128)(2,1)S(1)} %get-tuple-element.40.factors_0), channel_id=1, source_target_pairs={{0,8},{4,12},{8,0},{12,4},{1,9},{5,13},{9,1},{13,5},{2,10},{6,14},... | collective-permute-start | bytes 1671176 | tf_op jit(solution)/shard_map/ppermute | solution.py:197
  5.3 17.8 %collective-permute-start = (bf16[18,48,128]{2,1,0:T(8,128)(2,1)S(1)}, bf16[18,48,128]{2,1,0:T(8,128)(2,1)S(1)}, u32[]{:S(2)}, u32[]{:S(2)}) collective-permute-start(bf16[18,48,128]{2,1,0:T(8,128)(2,1)S(1)} %get-tuple-element.36), channel_id=1, source_target_pairs={{0,1},{1,0},{2,3},{3,2},{4,5},{5,4},{6,7},{7,6},{8,9},{9,8},{10,11... | collective-permute-start | bytes 663560 | tf_op jit(solution)/shard_map/ppermute | solution.py:197
  6.9 16.2 %collective-permute-start.1 = (bf16[18,48,128]{2,1,0:T(8,128)(2,1)S(1)}, bf16[18,48,128]{2,1,0:T(8,128)(2,1)S(1)}, u32[]{:S(2)}, u32[]{:S(2)}) collective-permute-start(bf16[18,48,128]{2,1,0:T(8,128)(2,1)S(1)} %get-tuple-element.37), channel_id=1, source_target_pairs={{0,2},{1,3},{2,0},{3,1},{4,6},{5,7},{6,4},{7,5},{8,10},{9,11},{10,... | collective-permute-start | bytes 663560 | tf_op jit(solution)/shard_map/ppermute | solution.py:197
  9.4 13.6 %collective-permute-start.2 = (bf16[10,48,128]{2,1,0:T(8,128)(2,1)S(1)}, bf16[10,48,128]{2,1,0:T(8,128)(2,1)S(1)}, u32[]{:S(2)}, u32[]{:S(2)}) collective-permute-start(bf16[10,48,128]{2,1,0:T(8,128)(2,1)S(1)} %get-tuple-element.38), channel_id=1, source_target_pairs={{0,3},{1,2},{2,1},{3,0},{4,7},{5,6},{6,5},{7,4},{8,11},{9,10},{10,... | collective-permute-start | bytes 368648 | tf_op jit(solution)/shard_map/ppermute | solution.py:197
  9.7 22.1 %collective-permute-start.6 = (bf16[128,2176]{1,0:T(8,128)(2,1)S(1)}, bf16[128,2176]{1,0:T(8,128)(2,1)S(1)}, u32[]{:S(2)}, u32[]{:S(2)}) collective-permute-start(bf16[128,2176]{1,0:T(8,128)(2,1)S(1)} %get-tuple-element.40.factors_0), channel_id=1, source_target_pairs={{0,4},{4,0},{8,12},{12,8},{1,5},{5,1},{9,13},{13,9},{2,6},{6,2},{1... | collective-permute-start | bytes 1671176 | tf_op jit(solution)/shard_map/ppermute | solution.py:197
  23.2 9.0 %collective-permute-start.7 = (bf16[128,2176]{1,0:T(8,128)(2,1)S(1)}, bf16[128,2176]{1,0:T(8,128)(2,1)S(1)}, u32[]{:S(2)}, u32[]{:S(2)}) collective-permute-start(bf16[128,2176]{1,0:T(8,128)(2,1)S(1)} %collective-permute-done.3.factors_2), channel_id=1, source_target_pairs={{0,4},{4,0},{8,12},{12,8},{1,5},{5,1},{9,13},{13,9},{2,6},{6,2},{1... | collective-permute-start | bytes 1671176 | tf_op jit(solution)/shard_map/ppermute | solution.py:197
  23.8 3.7 %collective-permute-start.4 = (bf16[16,5120]{1,0:T(8,128)(2,1)S(1)}, bf16[16,5120]{1,0:T(8,128)(2,1)S(1)}, u32[]{:S(2)}, u32[]{:S(2)}) collective-permute-start(bf16[16,5120]{1,0:T(8,128)(2,1)S(1)} %get-tuple-element.43), channel_id=1, source_target_pairs={{0,4},{4,0},{8,12},{12,8},{1,5},{5,1},{9,13},{13,9},{2,6},{6,2},{1... | collective-permute-start | bytes 491528 | tf_op jit(solution)/shard_map/ppermute | solution.py:197
  23.9 7.9 %collective-permute-start.8 = (bf16[8,48,128]{2,1,0:T(8,128)(2,1)S(1)}, bf16[8,48,128]{2,1,0:T(8,128)(2,1)S(1)}, u32[]{:S(2)}, u32[]{:S(2)}) collective-permute-start(bf16[8,48,128]{2,1,0:T(8,128)(2,1)S(1)} %get-tuple-element.48), channel_id=1, source_target_pairs={{0,3},{1,2},{2,1},{3,0},{4,7},{5,6},{6,5},{7,4},{8,11},{9,10},{10,... | collective-permute-start | bytes 294920 | tf_op jit(solution)/shard_map/ppermute | solution.py:197
  27.6 4.6 %collective-permute-start.5 = (bf16[8,5120]{1,0:T(8,128)(2,1)S(1)}, bf16[8,5120]{1,0:T(8,128)(2,1)S(1)}, u32[]{:S(2)}, u32[]{:S(2)}) collective-permute-start(bf16[8,5120]{1,0:T(8,128)(2,1)S(1)} %get-tuple-element.45._), channel_id=1, source_target_pairs={{0,8},{4,12},{8,0},{12,4},{1,9},{5,13},{9,1},{13,5},{2,10},{6,14},... | collective-permute-start | bytes 245768 | tf_op jit(solution)/shard_map/ppermute | solution.py:197
  35.1 4.3 %collective-permute-start.10 = (bf16[8,4096]{1,0:T(8,128)(2,1)S(1)}, bf16[8,4096]{1,0:T(8,128)(2,1)S(1)}, u32[]{:S(2)}, u32[]{:S(2)}) collective-permute-start(bf16[8,4096]{1,0:T(8,128)(2,1)S(1)} %get-tuple-element.49._.heads_0), channel_id=1, source_target_pairs={{0,8},{4,12},{8,0},{12,4},{1,9},{5,13},{9,1},{13,5},{2,10},{6,14},... | collective-permute-start | bytes 196616 | tf_op jit(solution)/shard_map/ppermute | solution.py:197
  36.2 3.5 %collective-permute-start.9 = (bf16[8,4096]{1,0:T(8,128)(2,1)S(1)}, bf16[8,4096]{1,0:T(8,128)(2,1)S(1)}, u32[]{:S(2)}, u32[]{:S(2)}) collective-permute-start(bf16[8,4096]{1,0:T(8,128)(2,1)S(1)} %get-tuple-element.49._.heads_0), channel_id=1, source_target_pairs={{0,4},{4,0},{8,12},{12,8},{1,5},{5,1},{9,13},{13,9},{2,6},{6,2},{1... | collective-permute-start | bytes 196616 | tf_op jit(solution)/shard_map/ppermute | solution.py:197
  39.4 1.3 %collective-permute-start.11 = (bf16[8,4096]{1,0:T(8,128)(2,1)S(1)}, bf16[8,4096]{1,0:T(8,128)(2,1)S(1)}, u32[]{:S(2)}, u32[]{:S(2)}) collective-permute-start(bf16[8,4096]{1,0:T(8,128)(2,1)S(1)} %collective-permute-done.10.heads_2), channel_id=1, source_target_pairs={{0,4},{4,0},{8,12},{12,8},{1,5},{5,1},{9,13},{13,9},{2,6},{6,2},{1... | collective-permute-start | bytes 196616 | tf_op jit(solution)/shard_map/ppermute | solution.py:197
  42.9 11.4 %collective-permute-start.12 = (bf16[32,1152]{1,0:T(8,128)(2,1)S(1)}, bf16[32,1152]{1,0:T(8,128)(2,1)S(1)}, u32[]{:S(2)}, u32[]{:S(2)}) collective-permute-start(bf16[32,1152]{1,0:T(8,128)(2,1)S(1)} %get-tuple-element.54), channel_id=1, source_target_pairs={{0,3},{1,2},{2,1},{3,0},{4,7},{5,6},{6,5},{7,4},{8,11},{9,10},{10,... | collective-permute-start | bytes 221192 | tf_op jit(solution)/shard_map/ppermute | solution.py:197
  46.8 7.5 %collective-permute-start.13 = (bf16[32,1152]{1,0:T(8,128)(2,1)S(1)}, bf16[32,1152]{1,0:T(8,128)(2,1)S(1)}, u32[]{:S(2)}, u32[]{:S(2)}) collective-permute-start(bf16[32,1152]{1,0:T(8,128)(2,1)S(1)} %shard_map.195), channel_id=1, source_target_pairs={{0,2},{1,3},{2,0},{3,1},{4,6},{5,7},{6,4},{7,5},{8,10},{9,11},{10,... | collective-permute-start | bytes 221192 | tf_op jit(solution)/shard_map/ppermute | solution.py:197
  48.4 6.0 %copy-start = (bf16[128,1024]{1,0:T(8,128)(2,1)S(1)}, bf16[128,1024]{1,0:T(8,128)(2,1)}, u32[]{:S(2)}) copy-start(bf16[128,1024]{1,0:T(8,128)(2,1)} %b_out_ref.1) | copy-start | bytes 786436
  48.4 6.0 %collective-permute-start.14 = (bf16[32,1152]{1,0:T(8,128)(2,1)S(1)}, bf16[32,1152]{1,0:T(8,128)(2,1)S(1)}, u32[]{:S(2)}, u32[]{:S(2)}) collective-permute-start(bf16[32,1152]{1,0:T(8,128)(2,1)S(1)} %shard_map.197), channel_id=1, source_target_pairs={{0,1},{1,0},{2,3},{3,2},{4,5},{5,4},{6,7},{7,6},{8,9},{9,8},{10,11... | collective-permute-start | bytes 221192 | tf_op jit(solution)/shard_map/ppermute | solution.py:197
  54.5 6.3 %collective-permute-start.17 = (bf16[32,1024]{1,0:T(8,128)(2,1)S(1)}, bf16[32,1024]{1,0:T(8,128)(2,1)S(1)}, u32[]{:S(2)}, u32[]{:S(2)}) collective-permute-start(bf16[32,1024]{1,0:T(8,128)(2,1)S(1)} %shard_map.198.part_0), channel_id=1, source_target_pairs={{0,3},{1,2},{2,1},{3,0},{4,7},{5,6},{6,5},{7,4},{8,11},{9,10},{10,... | collective-permute-start | bytes 196616 | tf_op jit(solution)/shard_map/ppermute | solution.py:197
  56.9 6.1 %collective-permute-start.16 = (bf16[32,1024]{1,0:T(8,128)(2,1)S(1)}, bf16[32,1024]{1,0:T(8,128)(2,1)S(1)}, u32[]{:S(2)}, u32[]{:S(2)}) collective-permute-start(bf16[32,1024]{1,0:T(8,128)(2,1)S(1)} %shard_map.198.part_0), channel_id=1, source_target_pairs={{0,2},{1,3},{2,0},{3,1},{4,6},{5,7},{6,4},{7,5},{8,10},{9,11},{10,... | collective-permute-start | bytes 196616 | tf_op jit(solution)/shard_map/ppermute | solution.py:197
  56.9 6.1 %collective-permute-start.15 = (bf16[32,1024]{1,0:T(8,128)(2,1)S(1)}, bf16[32,1024]{1,0:T(8,128)(2,1)S(1)}, u32[]{:S(2)}, u32[]{:S(2)}) collective-permute-start(bf16[32,1024]{1,0:T(8,128)(2,1)S(1)} %shard_map.198.part_0), channel_id=1, source_target_pairs={{0,1},{1,0},{2,3},{3,2},{4,5},{5,4},{6,7},{7,6},{8,9},{9,8},{10,11... | collective-permute-start | bytes 196616 | tf_op jit(solution)/shard_map/ppermute | solution.py:197

commit v3 on v2

--- a/solution.py
+++ b/solution.py
@@ -266,6 +266,7 @@
     b_key_ref,
     b_value_ref,
     a_out_ref,
+    _,
     scaled_ref,
     squares_ref,
     low_ref,
@@ -273,7 +274,7 @@
     far_1,
     far_2,
     far_3,
-    far_values,
+    far_late,
     factors_ref,
     hidden,
     gain_held,
@@ -303,10 +304,13 @@
     for mask, far in enumerate((near, far_1, far_2, far_3)):
         head = jnp.bitwise_xor(tensor_index, mask) * heads_here
         for kind, cache in enumerate((keys_ref, values_ref)):
-            late = mask == 3 and kind == 1
             for row in range(rows_dev):
-                start = (row if late else kind * rows_dev + row) * heads_here
-                target = far_values if late else far
+                late = mask == 3 and (kind == 1 or row == rows_dev - 1)
+                if late:
+                    start = (row if kind == 1 else rows_dev) * heads_here
+                else:
+                    start = (kind * rows_dev + row) * heads_here
+                target = far_late if late else far
                 moves.append(
                     (cache.at[row, pl.ds(head, heads_here)], target.at[pl.ds(start, heads_here)])
                 )
@@ -370,8 +374,6 @@
     trig_ref,
     length_ref,
     ring,
-    key_held,
-    value_held,
     lengths_held,
     ring_sem,
     held_sem,
@@ -385,15 +387,9 @@
             query_ref.at[pl.ds(chunk * depth, depth)], ring.at[slot], ring_sem.at[slot]
         )
 
-    side = [
-        pltpu.make_async_copy(key_ref, key_held, held_sem.at[0]),
-        pltpu.make_async_copy(value_ref, value_held, held_sem.at[1]),
-    ]
-    for copy in side:
-        copy.start()
     for chunk in range(min(slots, chunks)):
         fetch(chunk).start()
-    lengths_copy = pltpu.make_async_copy(lengths_ref, lengths_held, held_sem.at[2])
+    lengths_copy = pltpu.make_async_copy(lengths_ref, lengths_held, held_sem.at[0])
     lengths_copy.start()
     lengths_copy.wait()
     shape = length_ref.shape
@@ -411,8 +407,7 @@
     trig_ref[: shape[0], :] = jnp.cos(angles)
     trig_ref[shape[0] :, :] = jnp.where(lane < half, -sine, sine)
     place = columns
-    for copy, held in zip(side, (key_held, value_held)):
-        copy.wait()
+    for held in (key_ref, value_ref):
         sums_ref[:, place : place + held.shape[1]] = jnp.dot(
             scaled_ref[...], held[...], preferred_element_type=F32
         )
@@ -488,7 +483,7 @@
     far_1,
     far_2,
     far_3,
-    far_values,
+    far_late,
     _,
     weight_ref,
     heads_ref,
@@ -521,13 +516,17 @@
         narrow = key_heads * head_dim // owners
 
         for place in range(rows_dev * key_heads):
+            last = place - (rows_dev - 1) * key_heads
             for mask, block in enumerate((near, far_1, far_2, far_3)):
                 rows_here = slice(mask * span, (mask + 1) * span)
-                keys_all[place, rows_here, :] = block[place]
+                key_block, value_block = block, block
+                key_place, value_place = place, rows_dev * key_heads + place
                 if mask == 3:
-                    values_all[place, rows_here, :] = far_values[place]
-                else:
-                    values_all[place, rows_here, :] = block[rows_dev * key_heads + place]
+                    value_block, value_place = far_late, place
+                    if last >= 0:
+                        key_block, key_place = far_late, rows_dev * key_heads + last
+                keys_all[place, rows_here, :] = key_block[key_place]
+                values_all[place, rows_here, :] = value_block[value_place]
 
         total = kept_ref[...] + arrived_ref[...].astype(F32)
         joint = query_columns + 2 * key_heads * head_dim
@@ -837,7 +836,7 @@
     low_blocks = -(-3 * both // span)
     pack_columns = b_query.shape[1] + rank + a_out.shape[0]
 
-    scaled, squares, low, near, far_1, far_2, far_3, far_values, factors = kernel_call(
+    scaled, squares, low, near, far_1, far_2, far_3, far_late, factors = kernel_call(
         functools.partial(prepare_body, rows_dev),
         (
             shape((both, width), BF16),
@@ -846,18 +845,18 @@
             shape((blocks, span, head_dim), BF16),
             shape((blocks + low_blocks, span, head_dim), BF16),
             shape((blocks + low_blocks, span, head_dim), BF16),
-            shape((blocks // 2 + low_blocks, span, head_dim), BF16),
-            shape((blocks // 2, span, head_dim), BF16),
+            shape((blocks // 2 - key_heads + low_blocks, span, head_dim), BF16),
+            shape((blocks // 2 + key_heads, span, head_dim), BF16),
             shape((rank, pack_columns), BF16),
         ),
-        [hbm_spec()] * 12,
+        [hbm_spec()] * 13,
         [
             pltpu.VMEM((2, rows, width), BF16),
             pltpu.VMEM((width // 128, 128), BF16),
             pltpu.VMEM((3,) + a_query.shape, BF16),
             pltpu.SemaphoreType.DMA((3,)),
         ],
-        moved=12e6,
+        moved=60e6,
     )(
         *in_hbm(
             hidden_first,
@@ -872,6 +871,7 @@
             b_key.T,
             b_value.T,
             a_out,
+            w_out,
         )
     )
     far = [swapped(part, "tensor", mask) for mask, part in ((1, far_1), (2, far_2), (3, far_3))]
@@ -886,18 +886,16 @@
             shape((2 * share, head_dim), F32),
             shape((share, head_dim), jnp.int32),
         ),
-        [hbm_spec(), vmem_spec(), hbm_spec(), hbm_spec(), hbm_spec()],
+        [hbm_spec(), vmem_spec(), hbm_spec(), vmem_spec(), vmem_spec()],
         [
             pltpu.VMEM((4, depth, query_columns), BF16),
-            pltpu.VMEM((width, key_columns), BF16),
-            pltpu.VMEM((width, key_columns), BF16),
             pltpu.SMEM((rows_dev,), jnp.int32),
             pltpu.SemaphoreType.DMA((4,)),
-            pltpu.SemaphoreType.DMA((3,)),
+            pltpu.SemaphoreType.DMA((1,)),
         ],
         moved=2 * width * joint,
         mib=16,
-    )(*in_hbm(lengths), scaled, *in_hbm(query_weight, w_key, w_value))
+    )(*in_hbm(lengths), scaled, *in_hbm(query_weight), w_key, w_value)
     heads_here = query_columns // head_dim
     out_columns = w_out.shape[1]
     part = out_columns // n_tensor
@@ -928,8 +926,8 @@
         [vmem_spec()] * 6,
         [pltpu.VMEM((both, extended), F32)],
     )(sums, low, squares, *far)
-    factors_x, far_values, send = lax.optimization_barrier((factors_x, far_values, send))
-    far_values = swapped(far_values, "tensor", 3)
+    factors_x, far_late, send = lax.optimization_barrier((factors_x, far_late, send))
+    far_late = swapped(far_late, "tensor", 3)
     factors_both = swapped(factors_x, "dp", 1)
     all_factors = (factors, factors_core, factors_x, factors_both)
     arrived = swapped(send, "dp", 1)
@@ -958,7 +956,7 @@
             fetch_sems,
         ],
         moved=10e6,
-    )(length, trig, kept, arrived, *all_factors, near, *far, far_values, block_3, w_out)
+    )(length, trig, kept, arrived, *all_factors, near, *far, far_late, block_3, w_out)
 
     heads_x = swapped(heads, "dp", 2)
     heads_core = swapped(heads, "dp", 1)

time: 64.1 us -> 62.6 us (0.977)
  Pallas kernels: 34.6 us -> 32.7 us
  waiting for transfers between devices: 5.65 us -> 7.4 us
  starting transfers between devices: 22.7 us -> 21.4 us
    pallas_call x1, Pallas kernels: 13.4 us -> 11.4 us  [on_device_joined(): kernel_call(functools.partial(project_body, rows_dev), (shape((both, join...]
    ppermute x18, waiting for transfers between devices: 5.65 us -> 7.4 us  [swapped(): return lax.ppermute(array, axis, [(k, k ^ mask) for k in range(size)])]
    ppermute x18, starting transfers between devices: 22.7 us -> 21.4 us  [swapped(): return lax.ppermute(array, axis, [(k, k ^ mask) for k in range(size)])]
  transfers between devices with their start and end apart: 18 -> 18, of which waited for: 5 -> 8; matrix products, arithmetic and copies ran while one was open for 0% -> 0% of each run, Pallas kernels for 42% -> 40%
where the time goes in v3:
time: 62.6 us; the launch traced here: 62.4 us
  Pallas kernels  32.7 us (52%)
  starting transfers between devices  21.4 us (34%)
  waiting for transfers between devices  7.4 us (12%)
  between operations  0.95 us (2%)
    ppermute x18, starting transfers between devices, swapped(): return lax.ppermute(array, axis, [(k, k ^ mask) for k in range(size)])  21.4 us
    pallas_call x1, Pallas kernels, on_device_joined(): kernel_call(functools.partial(project_body, rows_dev), (shape((both, join...  11.4 us
    ppermute x18, waiting for transfers between devices, swapped(): return lax.ppermute(array, axis, [(k, k ^ mask) for k in range(size)])  7.4 us
    pallas_call x2, Pallas kernels, fetched(): kernel_call(functools.partial(fetch_body, [(mask, first * eighth) for mas...  6.42 us
    pallas_call x1, Pallas kernels, on_device_joined(): kernel_call(own_output_body, (summed,), [vmem_spec(), vmem_spec(), hbm_sp...  3.79 us
    pallas_call x2, Pallas kernels, next_output(): kernel_call(next_output_body, (message,), [vmem_spec()] * (2 + len(weight...  3.08 us
    pallas_call x1, Pallas kernels, on_device_joined(): kernel_call(functools.partial(attend_body, rows_dev), (shape((share, quer...  2.89 us
    pallas_call x1, Pallas kernels, on_device_joined(): kernel_call(functools.partial(far_output_body, 1, 4 * eighth), (message,...  2.22 us
  transfers between devices with their start and end apart: 18, of which 8 were waited for; matrix products, arithmetic and copies ran while one was open for 0% of the time, Pallas kernels for 40%

profile of v3, /device:TPU:0, one launch (start us, length us, event | category | flops | bytes accessed | tf_op | source)
XLA Modules:
  0.0 62.4 jit_solution(15860069397025047544)
XLA Ops:
  0.7 1.7 %shard_map.185 = (bf16[32,4096]{1,0:T(8,128)(2,1)S(1)}, f32[32,128]{1,0:T(8,128)S(1)}, f32[32,384]{1,0:T(8,128)S(1)}, bf16[16,48,128]{2,1,0:T(8,128)(2,1)S(1)}, ...) custom-call(bf16[16,4096]{1,0:T(8,128)(2,1)} %first_ref.1, ...), custom_call_target="tpu_custom_call" | custom-call | bytes 60000000 | tf_op jit(solution)/shard_map/pallas_call | solution.py:839
  2.4 3.0 %collective-permute-start.3 = (bf16[128,2176]{1,0:T(8,128)(2,1)S(1)}, bf16[128,2176]{1,0:T(8,128)(2,1)S(1)}, u32[]{:S(2)}, u32[]{:S(2)}) collective-permute-start(bf16[128,2176]{1,0:T(8,128)(2,1)S(1)} %get-tuple-element.40.factors_0), channel_id=1, source_target_pairs={{0,8},{4,12},{8,0},{12,4},{1,9},{5,13},{9,1},{13,5},{2,10},{6,14},... | collective-permute-start | bytes 1671176 | tf_op jit(solution)/shard_map/ppermute | solution.py:197
  5.4 1.6 %collective-permute-start = (bf16[18,48,128]{2,1,0:T(8,128)(2,1)S(1)}, bf16[18,48,128]{2,1,0:T(8,128)(2,1)S(1)}, u32[]{:S(2)}, u32[]{:S(2)}) collective-permute-start(bf16[18,48,128]{2,1,0:T(8,128)(2,1)S(1)} %get-tuple-element.36), channel_id=1, source_target_pairs={{0,1},{1,0},{2,3},{3,2},{4,5},{5,4},{6,7},{7,6},{8,9},{9,8},{10,11... | collective-permute-start | bytes 663560 | tf_op jit(solution)/shard_map/ppermute | solution.py:197
  7.0 2.6 %collective-permute-start.1 = (bf16[18,48,128]{2,1,0:T(8,128)(2,1)S(1)}, bf16[18,48,128]{2,1,0:T(8,128)(2,1)S(1)}, u32[]{:S(2)}, u32[]{:S(2)}) collective-permute-start(bf16[18,48,128]{2,1,0:T(8,128)(2,1)S(1)} %get-tuple-element.37), channel_id=1, source_target_pairs={{0,2},{1,3},{2,0},{3,1},{4,6},{5,7},{6,4},{7,5},{8,10},{9,11},{10,... | collective-permute-start | bytes 663560 | tf_op jit(solution)/shard_map/ppermute | solution.py:197
  9.6 0.2 collective-permute-start.2
  9.8 0.0 collective-permute-start.6
  9.8 11.4 %shard_map.186 = (f32[32,4608]{1,0:T(8,128)S(1)}, f32[16,128]{1,0:T(8,128)S(1)}, s32[8,128]{1,0:T(8,128)S(1)}) custom-call(s32[4]{0:T(128)} %lengths_ref.1, bf16[32,4096]{1,0:T(8,128)(2,1)S(1)} %get-tuple-element.30.scaled_ref, bf16[4096,4096]{1,0:T(8,128)(2,1)} %query_ref.1, bf16[4096,256]{1,0:T(8,128)(2,1)S(1)} %copy-done, bf16[4096,256]{1,0:T(8,128)(2,1)S(1)} %copy-done.1), custom_call_target="tpu_custom_call" | custom-call | bytes 37748736 | tf_op jit(solution)/shard_map/pallas_call | solution.py:882
  21.2 0.1 collective-permute-done.2.far_3
  21.3 0.0 collective-permute-done.far_1
  21.3 1.2 %collective-permute-done.1.far_2 = bf16[18,48,128]{2,1,0:T(8,128)(2,1)S(1)} collective-permute-done((bf16[18,48,128]{2,1,0:T(8,128)(2,1)S(1)}, bf16[18,48,128]{2,1,0:T(8,128)(2,1)S(1)}, u32[]{:S(2)}, u32[]{:S(2)}) %collective-permute-start.1) | collective-permute-done | bytes 221216 | tf_op jit(solution)/shard_map/ppermute | solution.py:197
  22.4 0.1 shard_map.187
  22.5 0.0 collective-permute-done.3.factors_2
  22.6 0.1 collective-permute-start.7
  22.6 0.5 collective-permute-start.4
  23.1 2.5 %collective-permute-start.8 = (bf16[10,48,128]{2,1,0:T(8,128)(2,1)S(1)}, bf16[10,48,128]{2,1,0:T(8,128)(2,1)S(1)}, u32[]{:S(2)}, u32[]{:S(2)}) collective-permute-start(bf16[10,48,128]{2,1,0:T(8,128)(2,1)S(1)} %get-tuple-element.48), channel_id=1, source_target_pairs={{0,3},{1,2},{2,1},{3,0},{4,7},{5,6},{6,5},{7,4},{8,11},{9,10},{10,... | collective-permute-start | bytes 368648 | tf_op jit(solution)/shard_map/ppermute | solution.py:197
  25.6 0.0 collective-permute-done.4.arrived_ref
  25.6 0.1 shard_map.188
  25.7 0.6 collective-permute-start.5
  26.3 3.5 %shard_map.189._.block_ref = bf16[4096,1024]{1,0:T(8,128)(2,1)S(1)} custom-call(bf16[4096,4096]{1,0:T(8,128)(2,1)} %weight_ref.9, bf16[8,5120]{1,0:T(8,128)(2,1)S(1)} %get-tuple-element.45._), custom_call_target="tpu_custom_call" | custom-call | bytes 8388608 | tf_op jit(solution)/shard_map/pallas_call | solution.py:911
  29.9 0.0 collective-permute-done.6.factors_1
  29.9 0.5 collective-permute-done.8.far_late
  30.3 0.0 collective-permute-done.5.arrived_ref
  30.3 0.0 collective-permute-done.7.factors_3
  30.4 2.9 %shard_map.190 = (bf16[8,4096]{1,0:T(8,128)(2,1)S(1)}, bf16[3072,1024]{1,0:T(8,128)(2,1)S(1)}) custom-call(s32[8,128]{1,0:T(8,128)S(1)} %get-tuple-element.31.length_ref, f32[16,128]{1,0:T(8,128)S(1)} %get-tuple-element.32.trig_ref, f32[8,5120]{1,0:T(8,128)S(1)} %get-tuple-element.44.kept_ref, bf16[8,5120]{1,0:T(8,128)(2,1)S(1)} %collective-permute-done.5.arrived_ref, ...), custom_call_target="tpu_custom_call" | custom-call | bytes 10000000 | tf_op jit(solution)/shard_map/pallas_call | solution.py:945
  33.2 1.1 %collective-permute-start.10 = (bf16[8,4096]{1,0:T(8,128)(2,1)S(1)}, bf16[8,4096]{1,0:T(8,128)(2,1)S(1)}, u32[]{:S(2)}, u32[]{:S(2)}) collective-permute-start(bf16[8,4096]{1,0:T(8,128)(2,1)S(1)} %get-tuple-element.49._.heads_0), channel_id=1, source_target_pairs={{0,8},{4,12},{8,0},{12,4},{1,9},{5,13},{9,1},{13,5},{2,10},{6,14},... | collective-permute-start | bytes 196616 | tf_op jit(solution)/shard_map/ppermute | solution.py:197
  34.4 0.0 collective-permute-start.9
  34.4 2.9 %shard_map.191 = (bf16[1024,1024]{1,0:T(8,128)(2,1)S(1)}, bf16[2048,1024]{1,0:T(8,128)(2,1)S(1)}) custom-call(bf16[4096,4096]{1,0:T(8,128)(2,1)} %weight_ref.9, bf16[8,4096]{1,0:T(8,128)(2,1)S(1)} %get-tuple-element.49._.heads_0), custom_call_target="tpu_custom_call" | custom-call | bytes 6291456 | tf_op jit(solution)/shard_map/pallas_call | solution.py:911
  37.3 0.3 collective-permute-done.10.heads_2
  37.6 0.3 collective-permute-start.11
  37.8 0.0 collective-permute-done.9.heads_1
  37.9 1.0 %collective-permute-done.11.heads_3 = bf16[8,4096]{1,0:T(8,128)(2,1)S(1)} collective-permute-done((bf16[8,4096]{1,0:T(8,128)(2,1)S(1)}, bf16[8,4096]{1,0:T(8,128)(2,1)S(1)}, u32[]{:S(2)}, u32[]{:S(2)}) %collective-permute-start.11) | collective-permute-done | bytes 65568 | tf_op jit(solution)/shard_map/ppermute | solution.py:197
  38.8 2.2 %shard_map.192 = (bf16[32,1152]{1,0:T(8,128)(2,1)S(1)}, f32[32,128]{1,0:T(8,128)S(1)}, bf16[32,4096]{1,0:T(8,128)(2,1)S(1)}, bf16[2048,1024]{1,0:T(8,128)(2,1)S(1)}) custom-call(bf16[8,4096]{1,0:T(8,128)(2,1)S(1)} %get-tuple-element.49._.heads_0, bf16[8,4096]{1,0:T(8,128)(2,1)S(1)} %collective-permute-done.9.heads_1, ...), custom_call_target="tpu_custom_call" | custom-call | bytes 10000000 | tf_op jit(solution)/shard_map/pallas_call | solution.py:968
  41.1 2.9 %collective-permute-start.12 = (bf16[32,1152]{1,0:T(8,128)(2,1)S(1)}, bf16[32,1152]{1,0:T(8,128)(2,1)S(1)}, u32[]{:S(2)}, u32[]{:S(2)}) collective-permute-start(bf16[32,1152]{1,0:T(8,128)(2,1)S(1)} %get-tuple-element.54), channel_id=1, source_target_pairs={{0,3},{1,2},{2,1},{3,0},{4,7},{5,6},{6,5},{7,4},{8,11},{9,10},{10,... | collective-permute-start | bytes 221192 | tf_op jit(solution)/shard_map/ppermute | solution.py:197
  43.9 1.5 %shard_map.195 = bf16[32,1152]{1,0:T(8,128)(2,1)S(1)} custom-call(bf16[32,4096]{1,0:T(8,128)(2,1)S(1)} %get-tuple-element.52.all_rows, f32[32,128]{1,0:T(8,128)S(1)} %get-tuple-element.53.low_ref, bf16[3072,1024]{1,0:T(8,128)(2,1)S(1)} %get-tuple-element.55.blocks_and_result_0_, bf16[1024,1024]{1,0:T(8,128)(2,1)S(1)} %get-tuple-element.56.blocks_and_result_1_), custom_call_target="tpu_custom_call" | custom-call | bytes 40000000 | tf_op jit(solution)/shard_map/pallas_call | solution.py:984
  45.5 1.0 %collective-permute-start.13 = (bf16[32,1152]{1,0:T(8,128)(2,1)S(1)}, bf16[32,1152]{1,0:T(8,128)(2,1)S(1)}, u32[]{:S(2)}, u32[]{:S(2)}) collective-permute-start(bf16[32,1152]{1,0:T(8,128)(2,1)S(1)} %shard_map.195), channel_id=1, source_target_pairs={{0,2},{1,3},{2,0},{3,1},{4,6},{5,7},{6,4},{7,5},{8,10},{9,11},{10,... | collective-permute-start | bytes 221192 | tf_op jit(solution)/shard_map/ppermute | solution.py:197
  46.5 1.5 %shard_map.197 = bf16[32,1152]{1,0:T(8,128)(2,1)S(1)} custom-call(bf16[32,4096]{1,0:T(8,128)(2,1)S(1)} %get-tuple-element.52.all_rows, f32[32,128]{1,0:T(8,128)S(1)} %get-tuple-element.53.low_ref, bf16[2048,1024]{1,0:T(8,128)(2,1)S(1)} %get-tuple-element.50._.blocks_and_result_0_, bf16[2048,1024]{1,0:T(8,128)(2,1)S(1)} %get-tuple-element.57.blocks_and_result_1_), custom_call_target="tpu_custom_call" | custom-call | bytes 40000000 | tf_op jit(solution)/shard_map/pallas_call | solution.py:984
  48.0 0.6 collective-permute-start.14
  48.6 3.8 %shard_map.193.keep_ref = f32[32,1152]{1,0:T(8,128)S(1)} custom-call(bf16[32,4096]{1,0:T(8,128)(2,1)S(1)} %get-tuple-element.52.all_rows, f32[32,128]{1,0:T(8,128)S(1)} %get-tuple-element.53.low_ref, bf16[4096,4096]{1,0:T(8,128)(2,1)} %weight_ref.9), custom_call_target="tpu_custom_call" | custom-call | bytes 40000000 | tf_op jit(solution)/shard_map/pallas_call | solution.py:999
  52.4 0.0 collective-permute-done.12.far
  52.5 0.0 collective-permute-done.13.far
  52.5 0.3 collective-permute-done.14.far_1
  52.8 0.2 shard_map.198.part_0
  53.0 3.0 %collective-permute-start.17 = (bf16[32,1024]{1,0:T(8,128)(2,1)S(1)}, bf16[32,1024]{1,0:T(8,128)(2,1)S(1)}, u32[]{:S(2)}, u32[]{:S(2)}) collective-permute-start(bf16[32,1024]{1,0:T(8,128)(2,1)S(1)} %shard_map.198.part_0), channel_id=1, source_target_pairs={{0,3},{1,2},{2,1},{3,0},{4,7},{5,6},{6,5},{7,4},{8,11},{9,10},{10,... | collective-permute-start | bytes 196616 | tf_op jit(solution)/shard_map/ppermute | solution.py:197
  56.0 0.0 collective-permute-start.16
  56.0 1.5 %collective-permute-start.15 = (bf16[32,1024]{1,0:T(8,128)(2,1)S(1)}, bf16[32,1024]{1,0:T(8,128)(2,1)S(1)}, u32[]{:S(2)}, u32[]{:S(2)}) collective-permute-start(bf16[32,1024]{1,0:T(8,128)(2,1)S(1)} %shard_map.198.part_0), channel_id=1, source_target_pairs={{0,1},{1,0},{2,3},{3,2},{4,5},{5,4},{6,7},{7,6},{8,9},{9,8},{10,11... | collective-permute-start | bytes 196616 | tf_op jit(solution)/shard_map/ppermute | solution.py:197
  57.5 1.9 %collective-permute-done.17.part_3 = bf16[32,1024]{1,0:T(8,128)(2,1)S(1)} collective-permute-done((bf16[32,1024]{1,0:T(8,128)(2,1)S(1)}, bf16[32,1024]{1,0:T(8,128)(2,1)S(1)}, u32[]{:S(2)}, u32[]{:S(2)}) %collective-permute-start.17) | collective-permute-done | bytes 65568 | tf_op jit(solution)/shard_map/ppermute | solution.py:197
  59.4 2.2 %collective-permute-done.16.part_2 = bf16[32,1024]{1,0:T(8,128)(2,1)S(1)} collective-permute-done((bf16[32,1024]{1,0:T(8,128)(2,1)S(1)}, bf16[32,1024]{1,0:T(8,128)(2,1)S(1)}, u32[]{:S(2)}, u32[]{:S(2)}) %collective-permute-start.16) | collective-permute-done | bytes 65568 | tf_op jit(solution)/shard_map/ppermute | solution.py:197
  61.5 0.8 %shard_map.199 = (bf16[16,4096]{1,0:T(8,128)(2,1)}, bf16[16,4096]{1,0:T(8,128)(2,1)}) custom-call(bf16[32,1024]{1,0:T(8,128)(2,1)S(1)} %shard_map.198.part_0, bf16[32,1024]{1,0:T(8,128)(2,1)S(1)} %collective-permute-done.15.part_1, bf16[32,1024]{1,0:T(8,128)(2,1)S(1)} %collective-permute-done.16.part_2, bf16[32,1024]{1,0:T(8,128)(2,1)S(1)} %collective-permute-done.17.part_3), custom_call_target="tpu_custom_call" | custom-call | tf_op jit(solution)/shard_map/pallas_call | solution.py:1015
  (9 shorter events, 0.1 us)
Async XLA Ops:
  0.6 9.2 %copy-start = (bf16[4096,256]{1,0:T(8,128)(2,1)S(1)}, bf16[4096,256]{1,0:T(8,128)(2,1)}, u32[]{:S(2)}) copy-start(bf16[4096,256]{1,0:T(8,128)(2,1)} %key_ref.1) | copy-start | bytes 6291460
  0.6 9.2 %copy-start.1 = (bf16[4096,256]{1,0:T(8,128)(2,1)S(1)}, bf16[4096,256]{1,0:T(8,128)(2,1)}, u32[]{:S(2)}) copy-start(bf16[4096,256]{1,0:T(8,128)(2,1)} %value_ref.1) | copy-start | bytes 6291460
  2.4 20.1 %collective-permute-start.3 = (bf16[128,2176]{1,0:T(8,128)(2,1)S(1)}, bf16[128,2176]{1,0:T(8,128)(2,1)S(1)}, u32[]{:S(2)}, u32[]{:S(2)}) collective-permute-start(bf16[128,2176]{1,0:T(8,128)(2,1)S(1)} %get-tuple-element.40.factors_0), channel_id=1, source_target_pairs={{0,8},{4,12},{8,0},{12,4},{1,9},{5,13},{9,1},{13,5},{2,10},{6,14},... | collective-permute-start | bytes 1671176 | tf_op jit(solution)/shard_map/ppermute | solution.py:197
  5.4 15.9 %collective-permute-start = (bf16[18,48,128]{2,1,0:T(8,128)(2,1)S(1)}, bf16[18,48,128]{2,1,0:T(8,128)(2,1)S(1)}, u32[]{:S(2)}, u32[]{:S(2)}) collective-permute-start(bf16[18,48,128]{2,1,0:T(8,128)(2,1)S(1)} %get-tuple-element.36), channel_id=1, source_target_pairs={{0,1},{1,0},{2,3},{3,2},{4,5},{5,4},{6,7},{7,6},{8,9},{9,8},{10,11... | collective-permute-start | bytes 663560 | tf_op jit(solution)/shard_map/ppermute | solution.py:197
  7.0 15.5 %collective-permute-start.1 = (bf16[18,48,128]{2,1,0:T(8,128)(2,1)S(1)}, bf16[18,48,128]{2,1,0:T(8,128)(2,1)S(1)}, u32[]{:S(2)}, u32[]{:S(2)}) collective-permute-start(bf16[18,48,128]{2,1,0:T(8,128)(2,1)S(1)} %get-tuple-element.37), channel_id=1, source_target_pairs={{0,2},{1,3},{2,0},{3,1},{4,6},{5,7},{6,4},{7,5},{8,10},{9,11},{10,... | collective-permute-start | bytes 663560 | tf_op jit(solution)/shard_map/ppermute | solution.py:197
  9.6 11.7 %collective-permute-start.2 = (bf16[8,48,128]{2,1,0:T(8,128)(2,1)S(1)}, bf16[8,48,128]{2,1,0:T(8,128)(2,1)S(1)}, u32[]{:S(2)}, u32[]{:S(2)}) collective-permute-start(bf16[8,48,128]{2,1,0:T(8,128)(2,1)S(1)} %get-tuple-element.38), channel_id=1, source_target_pairs={{0,3},{1,2},{2,1},{3,0},{4,7},{5,6},{6,5},{7,4},{8,11},{9,10},{10,... | collective-permute-start | bytes 294920 | tf_op jit(solution)/shard_map/ppermute | solution.py:197
  9.8 20.1 %collective-permute-start.6 = (bf16[128,2176]{1,0:T(8,128)(2,1)S(1)}, bf16[128,2176]{1,0:T(8,128)(2,1)S(1)}, u32[]{:S(2)}, u32[]{:S(2)}) collective-permute-start(bf16[128,2176]{1,0:T(8,128)(2,1)S(1)} %get-tuple-element.40.factors_0), channel_id=1, source_target_pairs={{0,4},{4,0},{8,12},{12,8},{1,5},{5,1},{9,13},{13,9},{2,6},{6,2},{1... | collective-permute-start | bytes 1671176 | tf_op jit(solution)/shard_map/ppermute | solution.py:197
  22.6 7.8 %collective-permute-start.7 = (bf16[128,2176]{1,0:T(8,128)(2,1)S(1)}, bf16[128,2176]{1,0:T(8,128)(2,1)S(1)}, u32[]{:S(2)}, u32[]{:S(2)}) collective-permute-start(bf16[128,2176]{1,0:T(8,128)(2,1)S(1)} %collective-permute-done.3.factors_2), channel_id=1, source_target_pairs={{0,4},{4,0},{8,12},{12,8},{1,5},{5,1},{9,13},{13,9},{2,6},{6,2},{1... | collective-permute-start | bytes 1671176 | tf_op jit(solution)/shard_map/ppermute | solution.py:197
  22.6 3.0 %collective-permute-start.4 = (bf16[16,5120]{1,0:T(8,128)(2,1)S(1)}, bf16[16,5120]{1,0:T(8,128)(2,1)S(1)}, u32[]{:S(2)}, u32[]{:S(2)}) collective-permute-start(bf16[16,5120]{1,0:T(8,128)(2,1)S(1)} %get-tuple-element.43), channel_id=1, source_target_pairs={{0,4},{4,0},{8,12},{12,8},{1,5},{5,1},{9,13},{13,9},{2,6},{6,2},{1... | collective-permute-start | bytes 491528 | tf_op jit(solution)/shard_map/ppermute | solution.py:197
  23.1 7.2 %collective-permute-start.8 = (bf16[10,48,128]{2,1,0:T(8,128)(2,1)S(1)}, bf16[10,48,128]{2,1,0:T(8,128)(2,1)S(1)}, u32[]{:S(2)}, u32[]{:S(2)}) collective-permute-start(bf16[10,48,128]{2,1,0:T(8,128)(2,1)S(1)} %get-tuple-element.48), channel_id=1, source_target_pairs={{0,3},{1,2},{2,1},{3,0},{4,7},{5,6},{6,5},{7,4},{8,11},{9,10},{10,... | collective-permute-start | bytes 368648 | tf_op jit(solution)/shard_map/ppermute | solution.py:197
  25.7 4.6 %collective-permute-start.5 = (bf16[8,5120]{1,0:T(8,128)(2,1)S(1)}, bf16[8,5120]{1,0:T(8,128)(2,1)S(1)}, u32[]{:S(2)}, u32[]{:S(2)}) collective-permute-start(bf16[8,5120]{1,0:T(8,128)(2,1)S(1)} %get-tuple-element.45._), channel_id=1, source_target_pairs={{0,8},{4,12},{8,0},{12,4},{1,9},{5,13},{9,1},{13,5},{2,10},{6,14},... | collective-permute-start | bytes 245768 | tf_op jit(solution)/shard_map/ppermute | solution.py:197
  33.2 4.3 %collective-permute-start.10 = (bf16[8,4096]{1,0:T(8,128)(2,1)S(1)}, bf16[8,4096]{1,0:T(8,128)(2,1)S(1)}, u32[]{:S(2)}, u32[]{:S(2)}) collective-permute-start(bf16[8,4096]{1,0:T(8,128)(2,1)S(1)} %get-tuple-element.49._.heads_0), channel_id=1, source_target_pairs={{0,8},{4,12},{8,0},{12,4},{1,9},{5,13},{9,1},{13,5},{2,10},{6,14},... | collective-permute-start | bytes 196616 | tf_op jit(solution)/shard_map/ppermute | solution.py:197
  34.4 3.5 %collective-permute-start.9 = (bf16[8,4096]{1,0:T(8,128)(2,1)S(1)}, bf16[8,4096]{1,0:T(8,128)(2,1)S(1)}, u32[]{:S(2)}, u32[]{:S(2)}) collective-permute-start(bf16[8,4096]{1,0:T(8,128)(2,1)S(1)} %get-tuple-element.49._.heads_0), channel_id=1, source_target_pairs={{0,4},{4,0},{8,12},{12,8},{1,5},{5,1},{9,13},{13,9},{2,6},{6,2},{1... | collective-permute-start | bytes 196616 | tf_op jit(solution)/shard_map/ppermute | solution.py:197
  37.6 1.3 %collective-permute-start.11 = (bf16[8,4096]{1,0:T(8,128)(2,1)S(1)}, bf16[8,4096]{1,0:T(8,128)(2,1)S(1)}, u32[]{:S(2)}, u32[]{:S(2)}) collective-permute-start(bf16[8,4096]{1,0:T(8,128)(2,1)S(1)} %collective-permute-done.10.heads_2), channel_id=1, source_target_pairs={{0,4},{4,0},{8,12},{12,8},{1,5},{5,1},{9,13},{13,9},{2,6},{6,2},{1... | collective-permute-start | bytes 196616 | tf_op jit(solution)/shard_map/ppermute | solution.py:197
  41.1 11.4 %collective-permute-start.12 = (bf16[32,1152]{1,0:T(8,128)(2,1)S(1)}, bf16[32,1152]{1,0:T(8,128)(2,1)S(1)}, u32[]{:S(2)}, u32[]{:S(2)}) collective-permute-start(bf16[32,1152]{1,0:T(8,128)(2,1)S(1)} %get-tuple-element.54), channel_id=1, source_target_pairs={{0,3},{1,2},{2,1},{3,0},{4,7},{5,6},{6,5},{7,4},{8,11},{9,10},{10,... | collective-permute-start | bytes 221192 | tf_op jit(solution)/shard_map/ppermute | solution.py:197
  45.5 7.0 %collective-permute-start.13 = (bf16[32,1152]{1,0:T(8,128)(2,1)S(1)}, bf16[32,1152]{1,0:T(8,128)(2,1)S(1)}, u32[]{:S(2)}, u32[]{:S(2)}) collective-permute-start(bf16[32,1152]{1,0:T(8,128)(2,1)S(1)} %shard_map.195), channel_id=1, source_target_pairs={{0,2},{1,3},{2,0},{3,1},{4,6},{5,7},{6,4},{7,5},{8,10},{9,11},{10,... | collective-permute-start | bytes 221192 | tf_op jit(solution)/shard_map/ppermute | solution.py:197
  48.0 4.8 %copy-start.2 = (bf16[128,1024]{1,0:T(8,128)(2,1)S(1)}, bf16[128,1024]{1,0:T(8,128)(2,1)}, u32[]{:S(2)}) copy-start(bf16[128,1024]{1,0:T(8,128)(2,1)} %b_out_ref.1) | copy-start | bytes 786436
  48.0 4.8 %collective-permute-start.14 = (bf16[32,1152]{1,0:T(8,128)(2,1)S(1)}, bf16[32,1152]{1,0:T(8,128)(2,1)S(1)}, u32[]{:S(2)}, u32[]{:S(2)}) collective-permute-start(bf16[32,1152]{1,0:T(8,128)(2,1)S(1)} %shard_map.197), channel_id=1, source_target_pairs={{0,1},{1,0},{2,3},{3,2},{4,5},{5,4},{6,7},{7,6},{8,9},{9,8},{10,11... | collective-permute-start | bytes 221192 | tf_op jit(solution)/shard_map/ppermute | solution.py:197
  53.0 6.3 %collective-permute-start.17 = (bf16[32,1024]{1,0:T(8,128)(2,1)S(1)}, bf16[32,1024]{1,0:T(8,128)(2,1)S(1)}, u32[]{:S(2)}, u32[]{:S(2)}) collective-permute-start(bf16[32,1024]{1,0:T(8,128)(2,1)S(1)} %shard_map.198.part_0), channel_id=1, source_target_pairs={{0,3},{1,2},{2,1},{3,0},{4,7},{5,6},{6,5},{7,4},{8,11},{9,10},{10,... | collective-permute-start | bytes 196616 | tf_op jit(solution)/shard_map/ppermute | solution.py:197
  56.0 5.5 %collective-permute-start.16 = (bf16[32,1024]{1,0:T(8,128)(2,1)S(1)}, bf16[32,1024]{1,0:T(8,128)(2,1)S(1)}, u32[]{:S(2)}, u32[]{:S(2)}) collective-permute-start(bf16[32,1024]{1,0:T(8,128)(2,1)S(1)} %shard_map.198.part_0), channel_id=1, source_target_pairs={{0,2},{1,3},{2,0},{3,1},{4,6},{5,7},{6,4},{7,5},{8,10},{9,11},{10,... | collective-permute-start | bytes 196616 | tf_op jit(solution)/shard_map/ppermute | solution.py:197
  56.0 5.5 %collective-permute-start.15 = (bf16[32,1024]{1,0:T(8,128)(2,1)S(1)}, bf16[32,1024]{1,0:T(8,128)(2,1)S(1)}, u32[]{:S(2)}, u32[]{:S(2)}) collective-permute-start(bf16[32,1024]{1,0:T(8,128)(2,1)S(1)} %shard_map.198.part_0), channel_id=1, source_target_pairs={{0,1},{1,0},{2,3},{3,2},{4,5},{5,4},{6,7},{7,6},{8,9},{9,8},{10,11... | collective-permute-start | bytes 196616 | tf_op jit(solution)/shard_map/ppermute | solution.py:197

commit v4 on v3

--- a/solution.py
+++ b/solution.py
@@ -743,21 +743,28 @@
     result_ref[:, part:] = low_ref[...].astype(result_ref.dtype)
 
 
-def own_output_body(all_rows, low_ref, weight_ref, result_ref, held, sems):
-    copies = fetch_copies(weight_ref, lax.axis_index("tensor"), 0, held, sems)
+def own_output_body(all_rows, low_ref, first_ref, weight_ref, result_ref, held, sems):
+    tensor_index = lax.axis_index("tensor")
+    done = first_ref.shape[0]
+    copies = fetch_copies(weight_ref, tensor_index, done, held, sems)
     for copy in copies:
         copy.start()
     part = held.shape[1]
     rows = held.shape[0] // len(copies)
-    result_ref[:, part:] = low_ref[...]
+
+    @pl.when(tensor_index >= 0)
+    def multiplied():
+        result_ref[:, part:] = low_ref[...]
+        result_ref[:, :part] = product(all_rows, first_ref)
+
     for piece, copy in enumerate(copies):
         copy.wait()
         here = slice(piece * rows, (piece + 1) * rows)
-        term = jnp.dot(all_rows[:, here], held[here, :], preferred_element_type=F32)
-        if piece == 0:
-            result_ref[:, :part] = term
-        else:
-            result_ref[:, :part] += term
+        result_ref[:, :part] += jnp.dot(
+            all_rows[:, done + piece * rows : done + (piece + 1) * rows],
+            held[here, :],
+            preferred_element_type=F32,
+        )
 
 
 def add_far_body(keep_ref, far, sum_ref):
@@ -938,7 +945,7 @@
         [pltpu.VMEM((rows, extended), F32)],
     )(keep, arrived)
     arrived = swapped(send, "dp", 2)
-    (block_3,) = fetched(send, (3, 0, 8))
+    block_3, own_first = fetched(send, (3, 0, 8), (0, 0, 2))
     group = heads_here // key_heads
     positions = n_tensor * span + 16
     owners = lax.axis_size("dp")
@@ -999,11 +1006,11 @@
     (total,) = kernel_call(
         own_output_body,
         (summed,),
-        [vmem_spec(), vmem_spec(), hbm_spec()],
-        [weight_block(8), pltpu.SemaphoreType.DMA((8,))],
+        [vmem_spec()] * 3 + [hbm_spec()],
+        [weight_block(6), pltpu.SemaphoreType.DMA((6,))],
         mib=12,
         moved=40e6,
-    )(all_rows, low, w_out)
+    )(all_rows, low, own_first, w_out)
     total = added(added(total, far_3, 40e6), far_2, 40e6)
     (done,) = kernel_call(
         functools.partial(finish_body, rows_dev),

time: 62.6 us -> 62.6 us (level)
  starting transfers between devices: 21.4 us -> 22.1 us
    ppermute x18, starting transfers between devices: 21.4 us -> 22.1 us  [swapped(): return lax.ppermute(array, axis, [(k, k ^ mask) for k in range(size)])]
  transfers between devices with their start and end apart: 18 -> 18, of which waited for: 8 -> 7; matrix products, arithmetic and copies ran while one was open for 0% -> 0% of each run, Pallas kernels for 40% -> 40%
where the time goes in v4:
time: 62.6 us; the launch traced here: 62.4 us
  Pallas kernels  32.7 us (52%)
  starting transfers between devices  22.1 us (35%)
  waiting for transfers between devices  6.81 us (11%)
  between operations  0.82 us (1%)
    ppermute x18, starting transfers between devices, swapped(): return lax.ppermute(array, axis, [(k, k ^ mask) for k in range(size)])  22.1 us
    pallas_call x1, Pallas kernels, on_device_joined(): kernel_call(functools.partial(project_body, rows_dev), (shape((both, join...  11.4 us
    pallas_call x2, Pallas kernels, fetched(): kernel_call(functools.partial(fetch_body, [(mask, first * eighth) for mas...  6.96 us
    ppermute x18, waiting for transfers between devices, swapped(): return lax.ppermute(array, axis, [(k, k ^ mask) for k in range(size)])  6.81 us
    pallas_call x1, Pallas kernels, on_device_joined(): kernel_call(own_output_body, (summed,), [vmem_spec()] * 3 + [hbm_spec()],...  3.21 us
    pallas_call x2, Pallas kernels, next_output(): kernel_call(next_output_body, (message,), [vmem_spec()] * (2 + len(weight...  3.08 us
    pallas_call x1, Pallas kernels, on_device_joined(): kernel_call(functools.partial(attend_body, rows_dev), (shape((share, quer...  2.9 us
    pallas_call x1, Pallas kernels, on_device_joined(): kernel_call(functools.partial(far_output_body, 1, 4 * eighth), (message,...  2.22 us
  transfers between devices with their start and end apart: 18, of which 7 were waited for; matrix products, arithmetic and copies ran while one was open for 0% of the time, Pallas kernels for 40%

profile of v4, /device:TPU:0, one launch (start us, length us, event | category | flops | bytes accessed | tf_op | source)
XLA Modules:
  0.0 62.4 jit_solution(14126866164144401373)
XLA Ops:
  0.7 1.7 %shard_map.185 = (bf16[32,4096]{1,0:T(8,128)(2,1)S(1)}, f32[32,128]{1,0:T(8,128)S(1)}, f32[32,384]{1,0:T(8,128)S(1)}, bf16[16,48,128]{2,1,0:T(8,128)(2,1)S(1)}, ...) custom-call(bf16[16,4096]{1,0:T(8,128)(2,1)} %first_ref.1, ...), custom_call_target="tpu_custom_call" | custom-call | bytes 60000000 | tf_op jit(solution)/shard_map/pallas_call | solution.py:846
  2.4 3.0 %collective-permute-start.3 = (bf16[128,2176]{1,0:T(8,128)(2,1)S(1)}, bf16[128,2176]{1,0:T(8,128)(2,1)S(1)}, u32[]{:S(2)}, u32[]{:S(2)}) collective-permute-start(bf16[128,2176]{1,0:T(8,128)(2,1)S(1)} %get-tuple-element.42.factors_0), channel_id=1, source_target_pairs={{0,8},{4,12},{8,0},{12,4},{1,9},{5,13},{9,1},{13,5},{2,10},{6,14},... | collective-permute-start | bytes 1671176 | tf_op jit(solution)/shard_map/ppermute | solution.py:197
  5.4 1.6 %collective-permute-start = (bf16[18,48,128]{2,1,0:T(8,128)(2,1)S(1)}, bf16[18,48,128]{2,1,0:T(8,128)(2,1)S(1)}, u32[]{:S(2)}, u32[]{:S(2)}) collective-permute-start(bf16[18,48,128]{2,1,0:T(8,128)(2,1)S(1)} %get-tuple-element.38), channel_id=1, source_target_pairs={{0,1},{1,0},{2,3},{3,2},{4,5},{5,4},{6,7},{7,6},{8,9},{9,8},{10,11... | collective-permute-start | bytes 663560 | tf_op jit(solution)/shard_map/ppermute | solution.py:197
  7.0 2.6 %collective-permute-start.1 = (bf16[18,48,128]{2,1,0:T(8,128)(2,1)S(1)}, bf16[18,48,128]{2,1,0:T(8,128)(2,1)S(1)}, u32[]{:S(2)}, u32[]{:S(2)}) collective-permute-start(bf16[18,48,128]{2,1,0:T(8,128)(2,1)S(1)} %get-tuple-element.39), channel_id=1, source_target_pairs={{0,2},{1,3},{2,0},{3,1},{4,6},{5,7},{6,4},{7,5},{8,10},{9,11},{10,... | collective-permute-start | bytes 663560 | tf_op jit(solution)/shard_map/ppermute | solution.py:197
  9.6 0.2 collective-permute-start.2
  9.8 0.0 collective-permute-start.6
  9.8 11.4 %shard_map.186 = (f32[32,4608]{1,0:T(8,128)S(1)}, f32[16,128]{1,0:T(8,128)S(1)}, s32[8,128]{1,0:T(8,128)S(1)}) custom-call(s32[4]{0:T(128)} %lengths_ref.1, bf16[32,4096]{1,0:T(8,128)(2,1)S(1)} %get-tuple-element.32.scaled_ref, bf16[4096,4096]{1,0:T(8,128)(2,1)} %query_ref.1, bf16[4096,256]{1,0:T(8,128)(2,1)S(1)} %copy-done, bf16[4096,256]{1,0:T(8,128)(2,1)S(1)} %copy-done.1), custom_call_target="tpu_custom_call" | custom-call | bytes 37748736 | tf_op jit(solution)/shard_map/pallas_call | solution.py:889
  21.2 0.1 collective-permute-done.2.far_3
  21.3 0.0 collective-permute-done.far_1
  21.3 1.2 %collective-permute-done.1.far_2 = bf16[18,48,128]{2,1,0:T(8,128)(2,1)S(1)} collective-permute-done((bf16[18,48,128]{2,1,0:T(8,128)(2,1)S(1)}, bf16[18,48,128]{2,1,0:T(8,128)(2,1)S(1)}, u32[]{:S(2)}, u32[]{:S(2)}) %collective-permute-start.1) | collective-permute-done | bytes 221216 | tf_op jit(solution)/shard_map/ppermute | solution.py:197
  22.4 0.1 shard_map.187
  22.5 0.0 collective-permute-done.3.factors_2
  22.6 0.1 collective-permute-start.7
  22.6 0.5 collective-permute-start.4
  23.1 2.5 %collective-permute-start.8 = (bf16[10,48,128]{2,1,0:T(8,128)(2,1)S(1)}, bf16[10,48,128]{2,1,0:T(8,128)(2,1)S(1)}, u32[]{:S(2)}, u32[]{:S(2)}) collective-permute-start(bf16[10,48,128]{2,1,0:T(8,128)(2,1)S(1)} %get-tuple-element.50), channel_id=1, source_target_pairs={{0,3},{1,2},{2,1},{3,0},{4,7},{5,6},{6,5},{7,4},{8,11},{9,10},{10,... | collective-permute-start | bytes 368648 | tf_op jit(solution)/shard_map/ppermute | solution.py:197
  25.6 0.0 collective-permute-done.4.arrived_ref
  25.6 0.1 shard_map.188
  25.7 0.6 collective-permute-start.5
  26.3 4.1 %shard_map.189 = (bf16[4096,1024]{1,0:T(8,128)(2,1)S(1)}, bf16[1024,1024]{1,0:T(8,128)(2,1)S(1)}) custom-call(bf16[4096,4096]{1,0:T(8,128)(2,1)} %weight_ref.9, bf16[8,5120]{1,0:T(8,128)(2,1)S(1)} %get-tuple-element.47._), custom_call_target="tpu_custom_call" | custom-call | bytes 10485760 | tf_op jit(solution)/shard_map/pallas_call | solution.py:918
  30.4 0.0 collective-permute-done.6.factors_1
  30.4 0.0 collective-permute-done.8.far_late
  30.4 0.0 collective-permute-done.5.arrived_ref
  30.4 0.0 collective-permute-done.7.factors_3
  30.4 2.9 %shard_map.190 = (bf16[8,4096]{1,0:T(8,128)(2,1)S(1)}, bf16[3072,1024]{1,0:T(8,128)(2,1)S(1)}) custom-call(s32[8,128]{1,0:T(8,128)S(1)} %get-tuple-element.33.length_ref, f32[16,128]{1,0:T(8,128)S(1)} %get-tuple-element.34.trig_ref, f32[8,5120]{1,0:T(8,128)S(1)} %get-tuple-element.46.kept_ref, bf16[8,5120]{1,0:T(8,128)(2,1)S(1)} %collective-permute-done.5.arrived_ref, ...), custom_call_target="tpu_custom_call" | custom-call | bytes 10000000 | tf_op jit(solution)/shard_map/pallas_call | solution.py:952
  33.3 1.6 %collective-permute-start.10 = (bf16[8,4096]{1,0:T(8,128)(2,1)S(1)}, bf16[8,4096]{1,0:T(8,128)(2,1)S(1)}, u32[]{:S(2)}, u32[]{:S(2)}) collective-permute-start(bf16[8,4096]{1,0:T(8,128)(2,1)S(1)} %get-tuple-element.52._.heads_0), channel_id=1, source_target_pairs={{0,8},{4,12},{8,0},{12,4},{1,9},{5,13},{9,1},{13,5},{2,10},{6,14},... | collective-permute-start | bytes 196616 | tf_op jit(solution)/shard_map/ppermute | solution.py:197
  34.9 0.0 collective-permute-start.9
  34.9 2.9 %shard_map.191 = (bf16[1024,1024]{1,0:T(8,128)(2,1)S(1)}, bf16[2048,1024]{1,0:T(8,128)(2,1)S(1)}) custom-call(bf16[4096,4096]{1,0:T(8,128)(2,1)} %weight_ref.9, bf16[8,4096]{1,0:T(8,128)(2,1)S(1)} %get-tuple-element.52._.heads_0), custom_call_target="tpu_custom_call" | custom-call | bytes 6291456 | tf_op jit(solution)/shard_map/pallas_call | solution.py:918
  37.8 0.0 collective-permute-done.10.heads_2
  37.8 0.6 collective-permute-start.11
  38.4 0.0 collective-permute-done.9.heads_1
  38.4 0.9 %collective-permute-done.11.heads_3 = bf16[8,4096]{1,0:T(8,128)(2,1)S(1)} collective-permute-done((bf16[8,4096]{1,0:T(8,128)(2,1)S(1)}, bf16[8,4096]{1,0:T(8,128)(2,1)S(1)}, u32[]{:S(2)}, u32[]{:S(2)}) %collective-permute-start.11) | collective-permute-done | bytes 65568 | tf_op jit(solution)/shard_map/ppermute | solution.py:197
  39.3 2.2 %shard_map.192 = (bf16[32,1152]{1,0:T(8,128)(2,1)S(1)}, f32[32,128]{1,0:T(8,128)S(1)}, bf16[32,4096]{1,0:T(8,128)(2,1)S(1)}, bf16[2048,1024]{1,0:T(8,128)(2,1)S(1)}) custom-call(bf16[8,4096]{1,0:T(8,128)(2,1)S(1)} %get-tuple-element.52._.heads_0, bf16[8,4096]{1,0:T(8,128)(2,1)S(1)} %collective-permute-done.9.heads_1, ...), custom_call_target="tpu_custom_call" | custom-call | bytes 10000000 | tf_op jit(solution)/shard_map/pallas_call | solution.py:975
  41.5 2.4 %collective-permute-start.12 = (bf16[32,1152]{1,0:T(8,128)(2,1)S(1)}, bf16[32,1152]{1,0:T(8,128)(2,1)S(1)}, u32[]{:S(2)}, u32[]{:S(2)}) collective-permute-start(bf16[32,1152]{1,0:T(8,128)(2,1)S(1)} %get-tuple-element.58), channel_id=1, source_target_pairs={{0,3},{1,2},{2,1},{3,0},{4,7},{5,6},{6,5},{7,4},{8,11},{9,10},{10,... | collective-permute-start | bytes 221192 | tf_op jit(solution)/shard_map/ppermute | solution.py:197
  43.9 1.5 %shard_map.195 = bf16[32,1152]{1,0:T(8,128)(2,1)S(1)} custom-call(bf16[32,4096]{1,0:T(8,128)(2,1)S(1)} %get-tuple-element.55.all_rows, f32[32,128]{1,0:T(8,128)S(1)} %get-tuple-element.56.low_ref, bf16[3072,1024]{1,0:T(8,128)(2,1)S(1)} %get-tuple-element.59.blocks_and_result_0_, bf16[1024,1024]{1,0:T(8,128)(2,1)S(1)} %get-tuple-element.60.blocks_and_result_1_), custom_call_target="tpu_custom_call" | custom-call | bytes 40000000 | tf_op jit(solution)/shard_map/pallas_call | solution.py:991
  45.5 1.0 %collective-permute-start.13 = (bf16[32,1152]{1,0:T(8,128)(2,1)S(1)}, bf16[32,1152]{1,0:T(8,128)(2,1)S(1)}, u32[]{:S(2)}, u32[]{:S(2)}) collective-permute-start(bf16[32,1152]{1,0:T(8,128)(2,1)S(1)} %shard_map.195), channel_id=1, source_target_pairs={{0,2},{1,3},{2,0},{3,1},{4,6},{5,7},{6,4},{7,5},{8,10},{9,11},{10,... | collective-permute-start | bytes 221192 | tf_op jit(solution)/shard_map/ppermute | solution.py:197
  46.5 1.5 %shard_map.197 = bf16[32,1152]{1,0:T(8,128)(2,1)S(1)} custom-call(bf16[32,4096]{1,0:T(8,128)(2,1)S(1)} %get-tuple-element.55.all_rows, f32[32,128]{1,0:T(8,128)S(1)} %get-tuple-element.56.low_ref, bf16[2048,1024]{1,0:T(8,128)(2,1)S(1)} %get-tuple-element.53._.blocks_and_result_0_, bf16[2048,1024]{1,0:T(8,128)(2,1)S(1)} %get-tuple-element.61.blocks_and_result_1_), custom_call_target="tpu_custom_call" | custom-call | bytes 40000000 | tf_op jit(solution)/shard_map/pallas_call | solution.py:991
  48.0 1.0 %collective-permute-start.14 = (bf16[32,1152]{1,0:T(8,128)(2,1)S(1)}, bf16[32,1152]{1,0:T(8,128)(2,1)S(1)}, u32[]{:S(2)}, u32[]{:S(2)}) collective-permute-start(bf16[32,1152]{1,0:T(8,128)(2,1)S(1)} %shard_map.197), channel_id=1, source_target_pairs={{0,1},{1,0},{2,3},{3,2},{4,5},{5,4},{6,7},{7,6},{8,9},{9,8},{10,11... | collective-permute-start | bytes 221192 | tf_op jit(solution)/shard_map/ppermute | solution.py:197
  49.1 3.2 %shard_map.193.keep_ref = f32[32,1152]{1,0:T(8,128)S(1)} custom-call(bf16[32,4096]{1,0:T(8,128)(2,1)S(1)} %get-tuple-element.55.all_rows, f32[32,128]{1,0:T(8,128)S(1)} %get-tuple-element.56.low_ref, bf16[1024,1024]{1,0:T(8,128)(2,1)S(1)} %get-tuple-element.57.first_ref, bf16[4096,4096]{1,0:T(8,128)(2,1)} %weight_ref.9), custom_call_target="tpu_custom_call" | custom-call | bytes 40000000 | tf_op jit(solution)/shard_map/pallas_call | solution.py:1006
  52.3 0.0 collective-permute-done.12.far
  52.3 0.0 collective-permute-done.13.far
  52.4 0.5 collective-permute-done.14.far_1
  52.8 0.2 shard_map.198.part_0
  53.0 3.0 %collective-permute-start.17 = (bf16[32,1024]{1,0:T(8,128)(2,1)S(1)}, bf16[32,1024]{1,0:T(8,128)(2,1)S(1)}, u32[]{:S(2)}, u32[]{:S(2)}) collective-permute-start(bf16[32,1024]{1,0:T(8,128)(2,1)S(1)} %shard_map.198.part_0), channel_id=1, source_target_pairs={{0,3},{1,2},{2,1},{3,0},{4,7},{5,6},{6,5},{7,4},{8,11},{9,10},{10,... | collective-permute-start | bytes 196616 | tf_op jit(solution)/shard_map/ppermute | solution.py:197
  56.0 1.5 %collective-permute-start.15 = (bf16[32,1024]{1,0:T(8,128)(2,1)S(1)}, bf16[32,1024]{1,0:T(8,128)(2,1)S(1)}, u32[]{:S(2)}, u32[]{:S(2)}) collective-permute-start(bf16[32,1024]{1,0:T(8,128)(2,1)S(1)} %shard_map.198.part_0), channel_id=1, source_target_pairs={{0,1},{1,0},{2,3},{3,2},{4,5},{5,4},{6,7},{7,6},{8,9},{9,8},{10,11... | collective-permute-start | bytes 196616 | tf_op jit(solution)/shard_map/ppermute | solution.py:197
  57.5 1.8 %collective-permute-done.17.part_3 = bf16[32,1024]{1,0:T(8,128)(2,1)S(1)} collective-permute-done((bf16[32,1024]{1,0:T(8,128)(2,1)S(1)}, bf16[32,1024]{1,0:T(8,128)(2,1)S(1)}, u32[]{:S(2)}, u32[]{:S(2)}) %collective-permute-start.17) | collective-permute-done | bytes 65568 | tf_op jit(solution)/shard_map/ppermute | solution.py:197
  59.3 2.3 %collective-permute-done.16.part_2 = bf16[32,1024]{1,0:T(8,128)(2,1)S(1)} collective-permute-done((bf16[32,1024]{1,0:T(8,128)(2,1)S(1)}, bf16[32,1024]{1,0:T(8,128)(2,1)S(1)}, u32[]{:S(2)}, u32[]{:S(2)}) %collective-permute-start.16) | collective-permute-done | bytes 65568 | tf_op jit(solution)/shard_map/ppermute | solution.py:197
  61.6 0.1 collective-permute-done.15.part_1
  61.7 0.8 %shard_map.199 = (bf16[16,4096]{1,0:T(8,128)(2,1)}, bf16[16,4096]{1,0:T(8,128)(2,1)}) custom-call(bf16[32,1024]{1,0:T(8,128)(2,1)S(1)} %shard_map.198.part_0, bf16[32,1024]{1,0:T(8,128)(2,1)S(1)} %collective-permute-done.15.part_1, bf16[32,1024]{1,0:T(8,128)(2,1)S(1)} %collective-permute-done.16.part_2, bf16[32,1024]{1,0:T(8,128)(2,1)S(1)} %collective-permute-done.17.part_3), custom_call_target="tpu_custom_call" | custom-call | tf_op jit(solution)/shard_map/pallas_call | solution.py:1022
  (9 shorter events, 0.1 us)
Async XLA Ops:
  0.6 9.2 %copy-start = (bf16[4096,256]{1,0:T(8,128)(2,1)S(1)}, bf16[4096,256]{1,0:T(8,128)(2,1)}, u32[]{:S(2)}) copy-start(bf16[4096,256]{1,0:T(8,128)(2,1)} %key_ref.1) | copy-start | bytes 6291460
  0.6 9.2 %copy-start.1 = (bf16[4096,256]{1,0:T(8,128)(2,1)S(1)}, bf16[4096,256]{1,0:T(8,128)(2,1)}, u32[]{:S(2)}) copy-start(bf16[4096,256]{1,0:T(8,128)(2,1)} %value_ref.1) | copy-start | bytes 6291460
  2.4 20.1 %collective-permute-start.3 = (bf16[128,2176]{1,0:T(8,128)(2,1)S(1)}, bf16[128,2176]{1,0:T(8,128)(2,1)S(1)}, u32[]{:S(2)}, u32[]{:S(2)}) collective-permute-start(bf16[128,2176]{1,0:T(8,128)(2,1)S(1)} %get-tuple-element.42.factors_0), channel_id=1, source_target_pairs={{0,8},{4,12},{8,0},{12,4},{1,9},{5,13},{9,1},{13,5},{2,10},{6,14},... | collective-permute-start | bytes 1671176 | tf_op jit(solution)/shard_map/ppermute | solution.py:197
  5.4 15.9 %collective-permute-start = (bf16[18,48,128]{2,1,0:T(8,128)(2,1)S(1)}, bf16[18,48,128]{2,1,0:T(8,128)(2,1)S(1)}, u32[]{:S(2)}, u32[]{:S(2)}) collective-permute-start(bf16[18,48,128]{2,1,0:T(8,128)(2,1)S(1)} %get-tuple-element.38), channel_id=1, source_target_pairs={{0,1},{1,0},{2,3},{3,2},{4,5},{5,4},{6,7},{7,6},{8,9},{9,8},{10,11... | collective-permute-start | bytes 663560 | tf_op jit(solution)/shard_map/ppermute | solution.py:197
  7.0 15.5 %collective-permute-start.1 = (bf16[18,48,128]{2,1,0:T(8,128)(2,1)S(1)}, bf16[18,48,128]{2,1,0:T(8,128)(2,1)S(1)}, u32[]{:S(2)}, u32[]{:S(2)}) collective-permute-start(bf16[18,48,128]{2,1,0:T(8,128)(2,1)S(1)} %get-tuple-element.39), channel_id=1, source_target_pairs={{0,2},{1,3},{2,0},{3,1},{4,6},{5,7},{6,4},{7,5},{8,10},{9,11},{10,... | collective-permute-start | bytes 663560 | tf_op jit(solution)/shard_map/ppermute | solution.py:197
  9.6 11.7 %collective-permute-start.2 = (bf16[8,48,128]{2,1,0:T(8,128)(2,1)S(1)}, bf16[8,48,128]{2,1,0:T(8,128)(2,1)S(1)}, u32[]{:S(2)}, u32[]{:S(2)}) collective-permute-start(bf16[8,48,128]{2,1,0:T(8,128)(2,1)S(1)} %get-tuple-element.40), channel_id=1, source_target_pairs={{0,3},{1,2},{2,1},{3,0},{4,7},{5,6},{6,5},{7,4},{8,11},{9,10},{10,... | collective-permute-start | bytes 294920 | tf_op jit(solution)/shard_map/ppermute | solution.py:197
  9.8 20.6 %collective-permute-start.6 = (bf16[128,2176]{1,0:T(8,128)(2,1)S(1)}, bf16[128,2176]{1,0:T(8,128)(2,1)S(1)}, u32[]{:S(2)}, u32[]{:S(2)}) collective-permute-start(bf16[128,2176]{1,0:T(8,128)(2,1)S(1)} %get-tuple-element.42.factors_0), channel_id=1, source_target_pairs={{0,4},{4,0},{8,12},{12,8},{1,5},{5,1},{9,13},{13,9},{2,6},{6,2},{1... | collective-permute-start | bytes 1671176 | tf_op jit(solution)/shard_map/ppermute | solution.py:197
  22.6 7.9 %collective-permute-start.7 = (bf16[128,2176]{1,0:T(8,128)(2,1)S(1)}, bf16[128,2176]{1,0:T(8,128)(2,1)S(1)}, u32[]{:S(2)}, u32[]{:S(2)}) collective-permute-start(bf16[128,2176]{1,0:T(8,128)(2,1)S(1)} %collective-permute-done.3.factors_2), channel_id=1, source_target_pairs={{0,4},{4,0},{8,12},{12,8},{1,5},{5,1},{9,13},{13,9},{2,6},{6,2},{1... | collective-permute-start | bytes 1671176 | tf_op jit(solution)/shard_map/ppermute | solution.py:197
  22.6 3.0 %collective-permute-start.4 = (bf16[16,5120]{1,0:T(8,128)(2,1)S(1)}, bf16[16,5120]{1,0:T(8,128)(2,1)S(1)}, u32[]{:S(2)}, u32[]{:S(2)}) collective-permute-start(bf16[16,5120]{1,0:T(8,128)(2,1)S(1)} %get-tuple-element.45), channel_id=1, source_target_pairs={{0,4},{4,0},{8,12},{12,8},{1,5},{5,1},{9,13},{13,9},{2,6},{6,2},{1... | collective-permute-start | bytes 491528 | tf_op jit(solution)/shard_map/ppermute | solution.py:197
  23.1 7.3 %collective-permute-start.8 = (bf16[10,48,128]{2,1,0:T(8,128)(2,1)S(1)}, bf16[10,48,128]{2,1,0:T(8,128)(2,1)S(1)}, u32[]{:S(2)}, u32[]{:S(2)}) collective-permute-start(bf16[10,48,128]{2,1,0:T(8,128)(2,1)S(1)} %get-tuple-element.50), channel_id=1, source_target_pairs={{0,3},{1,2},{2,1},{3,0},{4,7},{5,6},{6,5},{7,4},{8,11},{9,10},{10,... | collective-permute-start | bytes 368648 | tf_op jit(solution)/shard_map/ppermute | solution.py:197
  25.7 4.7 %collective-permute-start.5 = (bf16[8,5120]{1,0:T(8,128)(2,1)S(1)}, bf16[8,5120]{1,0:T(8,128)(2,1)S(1)}, u32[]{:S(2)}, u32[]{:S(2)}) collective-permute-start(bf16[8,5120]{1,0:T(8,128)(2,1)S(1)} %get-tuple-element.47._), channel_id=1, source_target_pairs={{0,8},{4,12},{8,0},{12,4},{1,9},{5,13},{9,1},{13,5},{2,10},{6,14},... | collective-permute-start | bytes 245768 | tf_op jit(solution)/shard_map/ppermute | solution.py:197
  33.3 4.5 %collective-permute-start.10 = (bf16[8,4096]{1,0:T(8,128)(2,1)S(1)}, bf16[8,4096]{1,0:T(8,128)(2,1)S(1)}, u32[]{:S(2)}, u32[]{:S(2)}) collective-permute-start(bf16[8,4096]{1,0:T(8,128)(2,1)S(1)} %get-tuple-element.52._.heads_0), channel_id=1, source_target_pairs={{0,8},{4,12},{8,0},{12,4},{1,9},{5,13},{9,1},{13,5},{2,10},{6,14},... | collective-permute-start | bytes 196616 | tf_op jit(solution)/shard_map/ppermute | solution.py:197
  34.9 3.5 %collective-permute-start.9 = (bf16[8,4096]{1,0:T(8,128)(2,1)S(1)}, bf16[8,4096]{1,0:T(8,128)(2,1)S(1)}, u32[]{:S(2)}, u32[]{:S(2)}) collective-permute-start(bf16[8,4096]{1,0:T(8,128)(2,1)S(1)} %get-tuple-element.52._.heads_0), channel_id=1, source_target_pairs={{0,4},{4,0},{8,12},{12,8},{1,5},{5,1},{9,13},{13,9},{2,6},{6,2},{1... | collective-permute-start | bytes 196616 | tf_op jit(solution)/shard_map/ppermute | solution.py:197
  37.8 1.5 %collective-permute-start.11 = (bf16[8,4096]{1,0:T(8,128)(2,1)S(1)}, bf16[8,4096]{1,0:T(8,128)(2,1)S(1)}, u32[]{:S(2)}, u32[]{:S(2)}) collective-permute-start(bf16[8,4096]{1,0:T(8,128)(2,1)S(1)} %collective-permute-done.10.heads_2), channel_id=1, source_target_pairs={{0,4},{4,0},{8,12},{12,8},{1,5},{5,1},{9,13},{13,9},{2,6},{6,2},{1... | collective-permute-start | bytes 196616 | tf_op jit(solution)/shard_map/ppermute | solution.py:197
  41.5 10.8 %collective-permute-start.12 = (bf16[32,1152]{1,0:T(8,128)(2,1)S(1)}, bf16[32,1152]{1,0:T(8,128)(2,1)S(1)}, u32[]{:S(2)}, u32[]{:S(2)}) collective-permute-start(bf16[32,1152]{1,0:T(8,128)(2,1)S(1)} %get-tuple-element.58), channel_id=1, source_target_pairs={{0,3},{1,2},{2,1},{3,0},{4,7},{5,6},{6,5},{7,4},{8,11},{9,10},{10,... | collective-permute-start | bytes 221192 | tf_op jit(solution)/shard_map/ppermute | solution.py:197
  45.5 6.8 %collective-permute-start.13 = (bf16[32,1152]{1,0:T(8,128)(2,1)S(1)}, bf16[32,1152]{1,0:T(8,128)(2,1)S(1)}, u32[]{:S(2)}, u32[]{:S(2)}) collective-permute-start(bf16[32,1152]{1,0:T(8,128)(2,1)S(1)} %shard_map.195), channel_id=1, source_target_pairs={{0,2},{1,3},{2,0},{3,1},{4,6},{5,7},{6,4},{7,5},{8,10},{9,11},{10,... | collective-permute-start | bytes 221192 | tf_op jit(solution)/shard_map/ppermute | solution.py:197
  48.0 4.8 %collective-permute-start.14 = (bf16[32,1152]{1,0:T(8,128)(2,1)S(1)}, bf16[32,1152]{1,0:T(8,128)(2,1)S(1)}, u32[]{:S(2)}, u32[]{:S(2)}) collective-permute-start(bf16[32,1152]{1,0:T(8,128)(2,1)S(1)} %shard_map.197), channel_id=1, source_target_pairs={{0,1},{1,0},{2,3},{3,2},{4,5},{5,4},{6,7},{7,6},{8,9},{9,8},{10,11... | collective-permute-start | bytes 221192 | tf_op jit(solution)/shard_map/ppermute | solution.py:197
  49.1 3.7 %copy-start.2 = (bf16[128,1024]{1,0:T(8,128)(2,1)S(1)}, bf16[128,1024]{1,0:T(8,128)(2,1)}, u32[]{:S(2)}) copy-start(bf16[128,1024]{1,0:T(8,128)(2,1)} %b_out_ref.1) | copy-start | bytes 786436
  53.0 6.2 %collective-permute-start.17 = (bf16[32,1024]{1,0:T(8,128)(2,1)S(1)}, bf16[32,1024]{1,0:T(8,128)(2,1)S(1)}, u32[]{:S(2)}, u32[]{:S(2)}) collective-permute-start(bf16[32,1024]{1,0:T(8,128)(2,1)S(1)} %shard_map.198.part_0), channel_id=1, source_target_pairs={{0,3},{1,2},{2,1},{3,0},{4,7},{5,6},{6,5},{7,4},{8,11},{9,10},{10,... | collective-permute-start | bytes 196616 | tf_op jit(solution)/shard_map/ppermute | solution.py:197
  56.0 5.6 %collective-permute-start.16 = (bf16[32,1024]{1,0:T(8,128)(2,1)S(1)}, bf16[32,1024]{1,0:T(8,128)(2,1)S(1)}, u32[]{:S(2)}, u32[]{:S(2)}) collective-permute-start(bf16[32,1024]{1,0:T(8,128)(2,1)S(1)} %shard_map.198.part_0), channel_id=1, source_target_pairs={{0,2},{1,3},{2,0},{3,1},{4,6},{5,7},{6,4},{7,5},{8,10},{9,11},{10,... | collective-permute-start | bytes 196616 | tf_op jit(solution)/shard_map/ppermute | solution.py:197
  56.0 5.7 %collective-permute-start.15 = (bf16[32,1024]{1,0:T(8,128)(2,1)S(1)}, bf16[32,1024]{1,0:T(8,128)(2,1)S(1)}, u32[]{:S(2)}, u32[]{:S(2)}) collective-permute-start(bf16[32,1024]{1,0:T(8,128)(2,1)S(1)} %shard_map.198.part_0), channel_id=1, source_target_pairs={{0,1},{1,0},{2,3},{3,2},{4,5},{5,4},{6,7},{7,6},{8,9},{9,8},{10,11... | collective-permute-start | bytes 196616 | tf_op jit(solution)/shard_map/ppermute | solution.py:197

commit v5 on v4

--- a/solution.py
+++ b/solution.py
@@ -721,12 +721,18 @@
         low = jnp.zeros((all_rows.shape[0], rank), F32)
         for distance, factors in enumerate((factors_0, factors_1, factors_2, factors_3)):
             owner = jnp.bitwise_xor(dp_index, distance)
-            for piece in range(pieces):
-                low = low + jnp.dot(
-                    all_rows[:, aligned(owner * block + piece * rank, rank, 128)],
-                    factors[:, base + piece * rank : base + (piece + 1) * rank],
-                    preferred_element_type=F32,
-                )
+            joined = jnp.concatenate(
+                [
+                    factors[:, base + piece * rank : base + (piece + 1) * rank]
+                    for piece in range(pieces)
+                ],
+                axis=0,
+            )
+            low = low + jnp.dot(
+                all_rows[:, aligned(owner * block, block, 128)],
+                joined,
+                preferred_element_type=F32,
+            )
         low_ref[...] = low
         part = block_ref.shape[1]
         send_ref[:, :part] = product(all_rows, block_ref).astype(BF16)

time: 62.6 us -> 62.6 us (level)
  no operation moved by 1% of the time
where the time goes in v5:
time: 62.6 us; the launch traced here: 62.4 us
  Pallas kernels  32.7 us (52%)
  starting transfers between devices  22.1 us (35%)
  waiting for transfers between devices  6.81 us (11%)
  between operations  0.82 us (1%)
    ppermute x18, starting transfers between devices, swapped(): return lax.ppermute(array, axis, [(k, k ^ mask) for k in range(size)])  22.1 us
    pallas_call x1, Pallas kernels, on_device_joined(): kernel_call(functools.partial(project_body, rows_dev), (shape((both, join...  11.4 us
    pallas_call x2, Pallas kernels, fetched(): kernel_call(functools.partial(fetch_body, [(mask, first * eighth) for mas...  6.96 us
    ppermute x18, waiting for transfers between devices, swapped(): return lax.ppermute(array, axis, [(k, k ^ mask) for k in range(size)])  6.81 us
    pallas_call x1, Pallas kernels, on_device_joined(): kernel_call(own_output_body, (summed,), [vmem_spec()] * 3 + [hbm_spec()],...  3.21 us
    pallas_call x2, Pallas kernels, next_output(): kernel_call(next_output_body, (message,), [vmem_spec()] * (2 + len(weight...  3.08 us
    pallas_call x1, Pallas kernels, on_device_joined(): kernel_call(functools.partial(attend_body, rows_dev), (shape((share, quer...  2.9 us
    pallas_call x1, Pallas kernels, on_device_joined(): kernel_call(functools.partial(far_output_body, 1, 4 * eighth), (message,...  2.22 us
  transfers between devices with their start and end apart: 18, of which 7 were waited for; matrix products, arithmetic and copies ran while one was open for 0% of the time, Pallas kernels for 40%

profile of v5, /device:TPU:0, one launch (start us, length us, event | category | flops | bytes accessed | tf_op | source)
XLA Modules:
  0.0 62.4 jit_solution(417237304419741217)
XLA Ops:
  0.7 1.7 %shard_map.185 = (bf16[32,4096]{1,0:T(8,128)(2,1)S(1)}, f32[32,128]{1,0:T(8,128)S(1)}, f32[32,384]{1,0:T(8,128)S(1)}, bf16[16,48,128]{2,1,0:T(8,128)(2,1)S(1)}, ...) custom-call(bf16[16,4096]{1,0:T(8,128)(2,1)} %first_ref.1, ...), custom_call_target="tpu_custom_call" | custom-call | bytes 60000000 | tf_op jit(solution)/shard_map/pallas_call | solution.py:852
  2.4 3.0 %collective-permute-start.3 = (bf16[128,2176]{1,0:T(8,128)(2,1)S(1)}, bf16[128,2176]{1,0:T(8,128)(2,1)S(1)}, u32[]{:S(2)}, u32[]{:S(2)}) collective-permute-start(bf16[128,2176]{1,0:T(8,128)(2,1)S(1)} %get-tuple-element.42.factors_0), channel_id=1, source_target_pairs={{0,8},{4,12},{8,0},{12,4},{1,9},{5,13},{9,1},{13,5},{2,10},{6,14},... | collective-permute-start | bytes 1671176 | tf_op jit(solution)/shard_map/ppermute | solution.py:197
  5.4 1.6 %collective-permute-start = (bf16[18,48,128]{2,1,0:T(8,128)(2,1)S(1)}, bf16[18,48,128]{2,1,0:T(8,128)(2,1)S(1)}, u32[]{:S(2)}, u32[]{:S(2)}) collective-permute-start(bf16[18,48,128]{2,1,0:T(8,128)(2,1)S(1)} %get-tuple-element.38), channel_id=1, source_target_pairs={{0,1},{1,0},{2,3},{3,2},{4,5},{5,4},{6,7},{7,6},{8,9},{9,8},{10,11... | collective-permute-start | bytes 663560 | tf_op jit(solution)/shard_map/ppermute | solution.py:197
  7.0 2.6 %collective-permute-start.1 = (bf16[18,48,128]{2,1,0:T(8,128)(2,1)S(1)}, bf16[18,48,128]{2,1,0:T(8,128)(2,1)S(1)}, u32[]{:S(2)}, u32[]{:S(2)}) collective-permute-start(bf16[18,48,128]{2,1,0:T(8,128)(2,1)S(1)} %get-tuple-element.39), channel_id=1, source_target_pairs={{0,2},{1,3},{2,0},{3,1},{4,6},{5,7},{6,4},{7,5},{8,10},{9,11},{10,... | collective-permute-start | bytes 663560 | tf_op jit(solution)/shard_map/ppermute | solution.py:197
  9.6 0.2 collective-permute-start.2
  9.8 0.0 collective-permute-start.6
  9.8 11.4 %shard_map.186 = (f32[32,4608]{1,0:T(8,128)S(1)}, f32[16,128]{1,0:T(8,128)S(1)}, s32[8,128]{1,0:T(8,128)S(1)}) custom-call(s32[4]{0:T(128)} %lengths_ref.1, bf16[32,4096]{1,0:T(8,128)(2,1)S(1)} %get-tuple-element.32.scaled_ref, bf16[4096,4096]{1,0:T(8,128)(2,1)} %query_ref.1, bf16[4096,256]{1,0:T(8,128)(2,1)S(1)} %copy-done, bf16[4096,256]{1,0:T(8,128)(2,1)S(1)} %copy-done.1), custom_call_target="tpu_custom_call" | custom-call | bytes 37748736 | tf_op jit(solution)/shard_map/pallas_call | solution.py:895
  21.2 0.1 collective-permute-done.2.far_3
  21.3 0.0 collective-permute-done.far_1
  21.3 1.2 %collective-permute-done.1.far_2 = bf16[18,48,128]{2,1,0:T(8,128)(2,1)S(1)} collective-permute-done((bf16[18,48,128]{2,1,0:T(8,128)(2,1)S(1)}, bf16[18,48,128]{2,1,0:T(8,128)(2,1)S(1)}, u32[]{:S(2)}, u32[]{:S(2)}) %collective-permute-start.1) | collective-permute-done | bytes 221216 | tf_op jit(solution)/shard_map/ppermute | solution.py:197
  22.4 0.1 shard_map.187
  22.5 0.0 collective-permute-done.3.factors_2
  22.6 0.1 collective-permute-start.7
  22.6 0.5 collective-permute-start.4
  23.1 2.5 %collective-permute-start.8 = (bf16[10,48,128]{2,1,0:T(8,128)(2,1)S(1)}, bf16[10,48,128]{2,1,0:T(8,128)(2,1)S(1)}, u32[]{:S(2)}, u32[]{:S(2)}) collective-permute-start(bf16[10,48,128]{2,1,0:T(8,128)(2,1)S(1)} %get-tuple-element.50), channel_id=1, source_target_pairs={{0,3},{1,2},{2,1},{3,0},{4,7},{5,6},{6,5},{7,4},{8,11},{9,10},{10,... | collective-permute-start | bytes 368648 | tf_op jit(solution)/shard_map/ppermute | solution.py:197
  25.6 0.0 collective-permute-done.4.arrived_ref
  25.6 0.1 shard_map.188
  25.7 0.6 collective-permute-start.5
  26.3 4.1 %shard_map.189 = (bf16[4096,1024]{1,0:T(8,128)(2,1)S(1)}, bf16[1024,1024]{1,0:T(8,128)(2,1)S(1)}) custom-call(bf16[4096,4096]{1,0:T(8,128)(2,1)} %weight_ref.9, bf16[8,5120]{1,0:T(8,128)(2,1)S(1)} %get-tuple-element.47._), custom_call_target="tpu_custom_call" | custom-call | bytes 10485760 | tf_op jit(solution)/shard_map/pallas_call | solution.py:924
  30.4 0.0 collective-permute-done.6.factors_1
  30.4 0.0 collective-permute-done.8.far_late
  30.4 0.0 collective-permute-done.5.arrived_ref
  30.4 0.0 collective-permute-done.7.factors_3
  30.4 2.9 %shard_map.190 = (bf16[8,4096]{1,0:T(8,128)(2,1)S(1)}, bf16[3072,1024]{1,0:T(8,128)(2,1)S(1)}) custom-call(s32[8,128]{1,0:T(8,128)S(1)} %get-tuple-element.33.length_ref, f32[16,128]{1,0:T(8,128)S(1)} %get-tuple-element.34.trig_ref, f32[8,5120]{1,0:T(8,128)S(1)} %get-tuple-element.46.kept_ref, bf16[8,5120]{1,0:T(8,128)(2,1)S(1)} %collective-permute-done.5.arrived_ref, ...), custom_call_target="tpu_custom_call" | custom-call | bytes 10000000 | tf_op jit(solution)/shard_map/pallas_call | solution.py:958
  33.3 1.6 %collective-permute-start.10 = (bf16[8,4096]{1,0:T(8,128)(2,1)S(1)}, bf16[8,4096]{1,0:T(8,128)(2,1)S(1)}, u32[]{:S(2)}, u32[]{:S(2)}) collective-permute-start(bf16[8,4096]{1,0:T(8,128)(2,1)S(1)} %get-tuple-element.52._.heads_0), channel_id=1, source_target_pairs={{0,8},{4,12},{8,0},{12,4},{1,9},{5,13},{9,1},{13,5},{2,10},{6,14},... | collective-permute-start | bytes 196616 | tf_op jit(solution)/shard_map/ppermute | solution.py:197
  34.9 0.0 collective-permute-start.9
  34.9 2.9 %shard_map.191 = (bf16[1024,1024]{1,0:T(8,128)(2,1)S(1)}, bf16[2048,1024]{1,0:T(8,128)(2,1)S(1)}) custom-call(bf16[4096,4096]{1,0:T(8,128)(2,1)} %weight_ref.9, bf16[8,4096]{1,0:T(8,128)(2,1)S(1)} %get-tuple-element.52._.heads_0), custom_call_target="tpu_custom_call" | custom-call | bytes 6291456 | tf_op jit(solution)/shard_map/pallas_call | solution.py:924
  37.8 0.0 collective-permute-done.10.heads_2
  37.8 0.6 collective-permute-start.11
  38.4 0.0 collective-permute-done.9.heads_1
  38.4 0.9 %collective-permute-done.11.heads_3 = bf16[8,4096]{1,0:T(8,128)(2,1)S(1)} collective-permute-done((bf16[8,4096]{1,0:T(8,128)(2,1)S(1)}, bf16[8,4096]{1,0:T(8,128)(2,1)S(1)}, u32[]{:S(2)}, u32[]{:S(2)}) %collective-permute-start.11) | collective-permute-done | bytes 65568 | tf_op jit(solution)/shard_map/ppermute | solution.py:197
  39.3 2.2 %shard_map.192 = (bf16[32,1152]{1,0:T(8,128)(2,1)S(1)}, f32[32,128]{1,0:T(8,128)S(1)}, bf16[32,4096]{1,0:T(8,128)(2,1)S(1)}, bf16[2048,1024]{1,0:T(8,128)(2,1)S(1)}) custom-call(bf16[8,4096]{1,0:T(8,128)(2,1)S(1)} %get-tuple-element.52._.heads_0, bf16[8,4096]{1,0:T(8,128)(2,1)S(1)} %collective-permute-done.9.heads_1, ...), custom_call_target="tpu_custom_call" | custom-call | bytes 10000000 | tf_op jit(solution)/shard_map/pallas_call | solution.py:981
  41.5 2.4 %collective-permute-start.12 = (bf16[32,1152]{1,0:T(8,128)(2,1)S(1)}, bf16[32,1152]{1,0:T(8,128)(2,1)S(1)}, u32[]{:S(2)}, u32[]{:S(2)}) collective-permute-start(bf16[32,1152]{1,0:T(8,128)(2,1)S(1)} %get-tuple-element.58), channel_id=1, source_target_pairs={{0,3},{1,2},{2,1},{3,0},{4,7},{5,6},{6,5},{7,4},{8,11},{9,10},{10,... | collective-permute-start | bytes 221192 | tf_op jit(solution)/shard_map/ppermute | solution.py:197
  43.9 1.5 %shard_map.195 = bf16[32,1152]{1,0:T(8,128)(2,1)S(1)} custom-call(bf16[32,4096]{1,0:T(8,128)(2,1)S(1)} %get-tuple-element.55.all_rows, f32[32,128]{1,0:T(8,128)S(1)} %get-tuple-element.56.low_ref, bf16[3072,1024]{1,0:T(8,128)(2,1)S(1)} %get-tuple-element.59.blocks_and_result_0_, bf16[1024,1024]{1,0:T(8,128)(2,1)S(1)} %get-tuple-element.60.blocks_and_result_1_), custom_call_target="tpu_custom_call" | custom-call | bytes 40000000 | tf_op jit(solution)/shard_map/pallas_call | solution.py:997
  45.5 1.0 %collective-permute-start.13 = (bf16[32,1152]{1,0:T(8,128)(2,1)S(1)}, bf16[32,1152]{1,0:T(8,128)(2,1)S(1)}, u32[]{:S(2)}, u32[]{:S(2)}) collective-permute-start(bf16[32,1152]{1,0:T(8,128)(2,1)S(1)} %shard_map.195), channel_id=1, source_target_pairs={{0,2},{1,3},{2,0},{3,1},{4,6},{5,7},{6,4},{7,5},{8,10},{9,11},{10,... | collective-permute-start | bytes 221192 | tf_op jit(solution)/shard_map/ppermute | solution.py:197
  46.5 1.5 %shard_map.197 = bf16[32,1152]{1,0:T(8,128)(2,1)S(1)} custom-call(bf16[32,4096]{1,0:T(8,128)(2,1)S(1)} %get-tuple-element.55.all_rows, f32[32,128]{1,0:T(8,128)S(1)} %get-tuple-element.56.low_ref, bf16[2048,1024]{1,0:T(8,128)(2,1)S(1)} %get-tuple-element.53._.blocks_and_result_0_, bf16[2048,1024]{1,0:T(8,128)(2,1)S(1)} %get-tuple-element.61.blocks_and_result_1_), custom_call_target="tpu_custom_call" | custom-call | bytes 40000000 | tf_op jit(solution)/shard_map/pallas_call | solution.py:997
  48.0 1.0 %collective-permute-start.14 = (bf16[32,1152]{1,0:T(8,128)(2,1)S(1)}, bf16[32,1152]{1,0:T(8,128)(2,1)S(1)}, u32[]{:S(2)}, u32[]{:S(2)}) collective-permute-start(bf16[32,1152]{1,0:T(8,128)(2,1)S(1)} %shard_map.197), channel_id=1, source_target_pairs={{0,1},{1,0},{2,3},{3,2},{4,5},{5,4},{6,7},{7,6},{8,9},{9,8},{10,11... | collective-permute-start | bytes 221192 | tf_op jit(solution)/shard_map/ppermute | solution.py:197
  49.1 3.2 %shard_map.193.keep_ref = f32[32,1152]{1,0:T(8,128)S(1)} custom-call(bf16[32,4096]{1,0:T(8,128)(2,1)S(1)} %get-tuple-element.55.all_rows, f32[32,128]{1,0:T(8,128)S(1)} %get-tuple-element.56.low_ref, bf16[1024,1024]{1,0:T(8,128)(2,1)S(1)} %get-tuple-element.57.first_ref, bf16[4096,4096]{1,0:T(8,128)(2,1)} %weight_ref.9), custom_call_target="tpu_custom_call" | custom-call | bytes 40000000 | tf_op jit(solution)/shard_map/pallas_call | solution.py:1012
  52.3 0.0 collective-permute-done.12.far
  52.3 0.0 collective-permute-done.13.far
  52.4 0.5 collective-permute-done.14.far_1
  52.8 0.2 shard_map.198.part_0
  53.0 3.0 %collective-permute-start.17 = (bf16[32,1024]{1,0:T(8,128)(2,1)S(1)}, bf16[32,1024]{1,0:T(8,128)(2,1)S(1)}, u32[]{:S(2)}, u32[]{:S(2)}) collective-permute-start(bf16[32,1024]{1,0:T(8,128)(2,1)S(1)} %shard_map.198.part_0), channel_id=1, source_target_pairs={{0,3},{1,2},{2,1},{3,0},{4,7},{5,6},{6,5},{7,4},{8,11},{9,10},{10,... | collective-permute-start | bytes 196616 | tf_op jit(solution)/shard_map/ppermute | solution.py:197
  56.0 1.5 %collective-permute-start.15 = (bf16[32,1024]{1,0:T(8,128)(2,1)S(1)}, bf16[32,1024]{1,0:T(8,128)(2,1)S(1)}, u32[]{:S(2)}, u32[]{:S(2)}) collective-permute-start(bf16[32,1024]{1,0:T(8,128)(2,1)S(1)} %shard_map.198.part_0), channel_id=1, source_target_pairs={{0,1},{1,0},{2,3},{3,2},{4,5},{5,4},{6,7},{7,6},{8,9},{9,8},{10,11... | collective-permute-start | bytes 196616 | tf_op jit(solution)/shard_map/ppermute | solution.py:197
  57.5 1.8 %collective-permute-done.17.part_3 = bf16[32,1024]{1,0:T(8,128)(2,1)S(1)} collective-permute-done((bf16[32,1024]{1,0:T(8,128)(2,1)S(1)}, bf16[32,1024]{1,0:T(8,128)(2,1)S(1)}, u32[]{:S(2)}, u32[]{:S(2)}) %collective-permute-start.17) | collective-permute-done | bytes 65568 | tf_op jit(solution)/shard_map/ppermute | solution.py:197
  59.3 2.3 %collective-permute-done.16.part_2 = bf16[32,1024]{1,0:T(8,128)(2,1)S(1)} collective-permute-done((bf16[32,1024]{1,0:T(8,128)(2,1)S(1)}, bf16[32,1024]{1,0:T(8,128)(2,1)S(1)}, u32[]{:S(2)}, u32[]{:S(2)}) %collective-permute-start.16) | collective-permute-done | bytes 65568 | tf_op jit(solution)/shard_map/ppermute | solution.py:197
  61.6 0.1 collective-permute-done.15.part_1
  61.7 0.8 %shard_map.199 = (bf16[16,4096]{1,0:T(8,128)(2,1)}, bf16[16,4096]{1,0:T(8,128)(2,1)}) custom-call(bf16[32,1024]{1,0:T(8,128)(2,1)S(1)} %shard_map.198.part_0, bf16[32,1024]{1,0:T(8,128)(2,1)S(1)} %collective-permute-done.15.part_1, bf16[32,1024]{1,0:T(8,128)(2,1)S(1)} %collective-permute-done.16.part_2, bf16[32,1024]{1,0:T(8,128)(2,1)S(1)} %collective-permute-done.17.part_3), custom_call_target="tpu_custom_call" | custom-call | tf_op jit(solution)/shard_map/pallas_call | solution.py:1028
  (9 shorter events, 0.1 us)
Async XLA Ops:
  0.6 9.2 %copy-start = (bf16[4096,256]{1,0:T(8,128)(2,1)S(1)}, bf16[4096,256]{1,0:T(8,128)(2,1)}, u32[]{:S(2)}) copy-start(bf16[4096,256]{1,0:T(8,128)(2,1)} %key_ref.1) | copy-start | bytes 6291460
  0.6 9.2 %copy-start.1 = (bf16[4096,256]{1,0:T(8,128)(2,1)S(1)}, bf16[4096,256]{1,0:T(8,128)(2,1)}, u32[]{:S(2)}) copy-start(bf16[4096,256]{1,0:T(8,128)(2,1)} %value_ref.1) | copy-start | bytes 6291460
  2.4 20.1 %collective-permute-start.3 = (bf16[128,2176]{1,0:T(8,128)(2,1)S(1)}, bf16[128,2176]{1,0:T(8,128)(2,1)S(1)}, u32[]{:S(2)}, u32[]{:S(2)}) collective-permute-start(bf16[128,2176]{1,0:T(8,128)(2,1)S(1)} %get-tuple-element.42.factors_0), channel_id=1, source_target_pairs={{0,8},{4,12},{8,0},{12,4},{1,9},{5,13},{9,1},{13,5},{2,10},{6,14},... | collective-permute-start | bytes 1671176 | tf_op jit(solution)/shard_map/ppermute | solution.py:197
  5.4 15.9 %collective-permute-start = (bf16[18,48,128]{2,1,0:T(8,128)(2,1)S(1)}, bf16[18,48,128]{2,1,0:T(8,128)(2,1)S(1)}, u32[]{:S(2)}, u32[]{:S(2)}) collective-permute-start(bf16[18,48,128]{2,1,0:T(8,128)(2,1)S(1)} %get-tuple-element.38), channel_id=1, source_target_pairs={{0,1},{1,0},{2,3},{3,2},{4,5},{5,4},{6,7},{7,6},{8,9},{9,8},{10,11... | collective-permute-start | bytes 663560 | tf_op jit(solution)/shard_map/ppermute | solution.py:197
  7.0 15.5 %collective-permute-start.1 = (bf16[18,48,128]{2,1,0:T(8,128)(2,1)S(1)}, bf16[18,48,128]{2,1,0:T(8,128)(2,1)S(1)}, u32[]{:S(2)}, u32[]{:S(2)}) collective-permute-start(bf16[18,48,128]{2,1,0:T(8,128)(2,1)S(1)} %get-tuple-element.39), channel_id=1, source_target_pairs={{0,2},{1,3},{2,0},{3,1},{4,6},{5,7},{6,4},{7,5},{8,10},{9,11},{10,... | collective-permute-start | bytes 663560 | tf_op jit(solution)/shard_map/ppermute | solution.py:197
  9.6 11.7 %collective-permute-start.2 = (bf16[8,48,128]{2,1,0:T(8,128)(2,1)S(1)}, bf16[8,48,128]{2,1,0:T(8,128)(2,1)S(1)}, u32[]{:S(2)}, u32[]{:S(2)}) collective-permute-start(bf16[8,48,128]{2,1,0:T(8,128)(2,1)S(1)} %get-tuple-element.40), channel_id=1, source_target_pairs={{0,3},{1,2},{2,1},{3,0},{4,7},{5,6},{6,5},{7,4},{8,11},{9,10},{10,... | collective-permute-start | bytes 294920 | tf_op jit(solution)/shard_map/ppermute | solution.py:197
  9.8 20.6 %collective-permute-start.6 = (bf16[128,2176]{1,0:T(8,128)(2,1)S(1)}, bf16[128,2176]{1,0:T(8,128)(2,1)S(1)}, u32[]{:S(2)}, u32[]{:S(2)}) collective-permute-start(bf16[128,2176]{1,0:T(8,128)(2,1)S(1)} %get-tuple-element.42.factors_0), channel_id=1, source_target_pairs={{0,4},{4,0},{8,12},{12,8},{1,5},{5,1},{9,13},{13,9},{2,6},{6,2},{1... | collective-permute-start | bytes 1671176 | tf_op jit(solution)/shard_map/ppermute | solution.py:197
  22.6 7.9 %collective-permute-start.7 = (bf16[128,2176]{1,0:T(8,128)(2,1)S(1)}, bf16[128,2176]{1,0:T(8,128)(2,1)S(1)}, u32[]{:S(2)}, u32[]{:S(2)}) collective-permute-start(bf16[128,2176]{1,0:T(8,128)(2,1)S(1)} %collective-permute-done.3.factors_2), channel_id=1, source_target_pairs={{0,4},{4,0},{8,12},{12,8},{1,5},{5,1},{9,13},{13,9},{2,6},{6,2},{1... | collective-permute-start | bytes 1671176 | tf_op jit(solution)/shard_map/ppermute | solution.py:197
  22.6 3.0 %collective-permute-start.4 = (bf16[16,5120]{1,0:T(8,128)(2,1)S(1)}, bf16[16,5120]{1,0:T(8,128)(2,1)S(1)}, u32[]{:S(2)}, u32[]{:S(2)}) collective-permute-start(bf16[16,5120]{1,0:T(8,128)(2,1)S(1)} %get-tuple-element.45), channel_id=1, source_target_pairs={{0,4},{4,0},{8,12},{12,8},{1,5},{5,1},{9,13},{13,9},{2,6},{6,2},{1... | collective-permute-start | bytes 491528 | tf_op jit(solution)/shard_map/ppermute | solution.py:197
  23.1 7.3 %collective-permute-start.8 = (bf16[10,48,128]{2,1,0:T(8,128)(2,1)S(1)}, bf16[10,48,128]{2,1,0:T(8,128)(2,1)S(1)}, u32[]{:S(2)}, u32[]{:S(2)}) collective-permute-start(bf16[10,48,128]{2,1,0:T(8,128)(2,1)S(1)} %get-tuple-element.50), channel_id=1, source_target_pairs={{0,3},{1,2},{2,1},{3,0},{4,7},{5,6},{6,5},{7,4},{8,11},{9,10},{10,... | collective-permute-start | bytes 368648 | tf_op jit(solution)/shard_map/ppermute | solution.py:197
  25.7 4.7 %collective-permute-start.5 = (bf16[8,5120]{1,0:T(8,128)(2,1)S(1)}, bf16[8,5120]{1,0:T(8,128)(2,1)S(1)}, u32[]{:S(2)}, u32[]{:S(2)}) collective-permute-start(bf16[8,5120]{1,0:T(8,128)(2,1)S(1)} %get-tuple-element.47._), channel_id=1, source_target_pairs={{0,8},{4,12},{8,0},{12,4},{1,9},{5,13},{9,1},{13,5},{2,10},{6,14},... | collective-permute-start | bytes 245768 | tf_op jit(solution)/shard_map/ppermute | solution.py:197
  33.3 4.5 %collective-permute-start.10 = (bf16[8,4096]{1,0:T(8,128)(2,1)S(1)}, bf16[8,4096]{1,0:T(8,128)(2,1)S(1)}, u32[]{:S(2)}, u32[]{:S(2)}) collective-permute-start(bf16[8,4096]{1,0:T(8,128)(2,1)S(1)} %get-tuple-element.52._.heads_0), channel_id=1, source_target_pairs={{0,8},{4,12},{8,0},{12,4},{1,9},{5,13},{9,1},{13,5},{2,10},{6,14},... | collective-permute-start | bytes 196616 | tf_op jit(solution)/shard_map/ppermute | solution.py:197
  34.9 3.5 %collective-permute-start.9 = (bf16[8,4096]{1,0:T(8,128)(2,1)S(1)}, bf16[8,4096]{1,0:T(8,128)(2,1)S(1)}, u32[]{:S(2)}, u32[]{:S(2)}) collective-permute-start(bf16[8,4096]{1,0:T(8,128)(2,1)S(1)} %get-tuple-element.52._.heads_0), channel_id=1, source_target_pairs={{0,4},{4,0},{8,12},{12,8},{1,5},{5,1},{9,13},{13,9},{2,6},{6,2},{1... | collective-permute-start | bytes 196616 | tf_op jit(solution)/shard_map/ppermute | solution.py:197
  37.8 1.5 %collective-permute-start.11 = (bf16[8,4096]{1,0:T(8,128)(2,1)S(1)}, bf16[8,4096]{1,0:T(8,128)(2,1)S(1)}, u32[]{:S(2)}, u32[]{:S(2)}) collective-permute-start(bf16[8,4096]{1,0:T(8,128)(2,1)S(1)} %collective-permute-done.10.heads_2), channel_id=1, source_target_pairs={{0,4},{4,0},{8,12},{12,8},{1,5},{5,1},{9,13},{13,9},{2,6},{6,2},{1... | collective-permute-start | bytes 196616 | tf_op jit(solution)/shard_map/ppermute | solution.py:197
  41.5 10.8 %collective-permute-start.12 = (bf16[32,1152]{1,0:T(8,128)(2,1)S(1)}, bf16[32,1152]{1,0:T(8,128)(2,1)S(1)}, u32[]{:S(2)}, u32[]{:S(2)}) collective-permute-start(bf16[32,1152]{1,0:T(8,128)(2,1)S(1)} %get-tuple-element.58), channel_id=1, source_target_pairs={{0,3},{1,2},{2,1},{3,0},{4,7},{5,6},{6,5},{7,4},{8,11},{9,10},{10,... | collective-permute-start | bytes 221192 | tf_op jit(solution)/shard_map/ppermute | solution.py:197
  45.5 6.8 %collective-permute-start.13 = (bf16[32,1152]{1,0:T(8,128)(2,1)S(1)}, bf16[32,1152]{1,0:T(8,128)(2,1)S(1)}, u32[]{:S(2)}, u32[]{:S(2)}) collective-permute-start(bf16[32,1152]{1,0:T(8,128)(2,1)S(1)} %shard_map.195), channel_id=1, source_target_pairs={{0,2},{1,3},{2,0},{3,1},{4,6},{5,7},{6,4},{7,5},{8,10},{9,11},{10,... | collective-permute-start | bytes 221192 | tf_op jit(solution)/shard_map/ppermute | solution.py:197
  48.0 4.8 %collective-permute-start.14 = (bf16[32,1152]{1,0:T(8,128)(2,1)S(1)}, bf16[32,1152]{1,0:T(8,128)(2,1)S(1)}, u32[]{:S(2)}, u32[]{:S(2)}) collective-permute-start(bf16[32,1152]{1,0:T(8,128)(2,1)S(1)} %shard_map.197), channel_id=1, source_target_pairs={{0,1},{1,0},{2,3},{3,2},{4,5},{5,4},{6,7},{7,6},{8,9},{9,8},{10,11... | collective-permute-start | bytes 221192 | tf_op jit(solution)/shard_map/ppermute | solution.py:197
  49.1 3.7 %copy-start.2 = (bf16[128,1024]{1,0:T(8,128)(2,1)S(1)}, bf16[128,1024]{1,0:T(8,128)(2,1)}, u32[]{:S(2)}) copy-start(bf16[128,1024]{1,0:T(8,128)(2,1)} %b_out_ref.1) | copy-start | bytes 786436
  53.0 6.2 %collective-permute-start.17 = (bf16[32,1024]{1,0:T(8,128)(2,1)S(1)}, bf16[32,1024]{1,0:T(8,128)(2,1)S(1)}, u32[]{:S(2)}, u32[]{:S(2)}) collective-permute-start(bf16[32,1024]{1,0:T(8,128)(2,1)S(1)} %shard_map.198.part_0), channel_id=1, source_target_pairs={{0,3},{1,2},{2,1},{3,0},{4,7},{5,6},{6,5},{7,4},{8,11},{9,10},{10,... | collective-permute-start | bytes 196616 | tf_op jit(solution)/shard_map/ppermute | solution.py:197
  56.0 5.6 %collective-permute-start.16 = (bf16[32,1024]{1,0:T(8,128)(2,1)S(1)}, bf16[32,1024]{1,0:T(8,128)(2,1)S(1)}, u32[]{:S(2)}, u32[]{:S(2)}) collective-permute-start(bf16[32,1024]{1,0:T(8,128)(2,1)S(1)} %shard_map.198.part_0), channel_id=1, source_target_pairs={{0,2},{1,3},{2,0},{3,1},{4,6},{5,7},{6,4},{7,5},{8,10},{9,11},{10,... | collective-permute-start | bytes 196616 | tf_op jit(solution)/shard_map/ppermute | solution.py:197
  56.0 5.7 %collective-permute-start.15 = (bf16[32,1024]{1,0:T(8,128)(2,1)S(1)}, bf16[32,1024]{1,0:T(8,128)(2,1)S(1)}, u32[]{:S(2)}, u32[]{:S(2)}) collective-permute-start(bf16[32,1024]{1,0:T(8,128)(2,1)S(1)} %shard_map.198.part_0), channel_id=1, source_target_pairs={{0,1},{1,0},{2,3},{3,2},{4,5},{5,4},{6,7},{7,6},{8,9},{9,8},{10,11... | collective-permute-start | bytes 196616 | tf_op jit(solution)/shard_map/ppermute | solution.py:197
